TPU v7x, 128 devices: a whole 4x4x4 slice. The times are simulated.
128 devices in a mesh: ctx: 16 (over x, y), head: 8 (over z, core).
Axes of the slice: x: 4, y: 4, z: 4, core: 2. Of those that a mesh axis runs over, the one named last changes fastest.
Arguments:
- head_inputs: bfloat16 [16384, 8192], P(('ctx', 'head')), may hold values from -6 to 6
- gate_inputs: bfloat16 [16384, 8192], P(('ctx', 'head')), may hold values from -6 to 6
- write_keys: bfloat16 [16384, 1024], P(('ctx', 'head')), may hold values from -6 to 6
- read_queries: bfloat16 [16384, 1024], P(('ctx', 'head')), may hold values from -0.5 to 0.5
- step_logits: bfloat16 [16384, 128], P(('ctx', 'head')), may hold values from -3 to 3
- step_bias: float32 [128], P('head'), may hold values from -6 to 0
- decay_log: float32 [128], P('head'), may hold values from -7 to -2
- skip_scale: float32 [128], P('head'), may hold values from 0.5 to 1.5
- norm_gain: float32 [8192], replicated, may hold values from 0.1 to 1.9
- document_starts: int32 [64], P('ctx'), may hold values from 0 to 256, as said below
Outputs:
- layer_output: bfloat16 [16384, 8192], P(('ctx', 'head'))
Inputs may be any that keep to these rules, and one draw needn't show every extreme that they name: `document_starts`: each entry is the position within its block of 256 tokens at which a document starts, or 256 where none starts; the first block starts one at 0.
All inputs are finite; a program needn't handle non-finite values.
Results may differ from a plain program's by a relative error of at most 0.0058.
Values may be sent and summed in bfloat16 or wider, within the bound.
No kernel may reach another device: no remote copies, remote signals or barrier semaphores. Data moves between devices by JAX's collectives and lax.ppermute only.
A program may use at most 128 MiB of HBM per device.

v0:
```python
import jax
import jax.numpy as jnp
from jax import lax
from jax.sharding import PartitionSpec as P

HEAD_DIM = 64
STATE = 128
BLOCK = 256


def entering(part, axis, combine, identity):
    place = lax.axis_index(axis)
    gathered = jax.tree.map(lambda a: lax.all_gather(a, axis), part)
    state = jax.tree.map(lambda a, e: jnp.zeros_like(a) + jnp.asarray(e, a.dtype), part, identity)

    def one(hop, state):
        return combine(
            state, jax.tree.map(lambda a: lax.dynamic_index_in_dim(a, hop, 0, False), gathered)
        )

    return lax.fori_loop(0, place, one, state)


def block_terms(block_x, block_b, block_c, block_logit, start_at, step_bias, decay_log):
    length = block_x.shape[0]
    per_group = block_x.shape[1] // block_b.shape[1]
    step_size = jax.nn.softplus(block_logit.astype(jnp.float32) + step_bias)
    log_decay = -jnp.exp(decay_log) * step_size
    cumulative = jnp.cumsum(log_decay, axis=0)
    position = jnp.arange(length, dtype=jnp.int32)
    segment = position >= start_at
    allowed = (segment[:, None] == segment[None, :]) & (position[:, None] >= position[None, :])
    scores = jnp.einsum("tgn,sgn->gts", block_c, block_b, preferred_element_type=jnp.float32)
    scores = jnp.repeat(scores, per_group, axis=0)
    across = cumulative.T
    spread = across[:, :, None] - across[:, None, :]
    damping = jnp.where(allowed[None], jnp.exp(jnp.where(allowed[None], spread, 0.0)), 0.0)
    mixing = (damping * scores * step_size.T[:, None, :]).astype(jnp.bfloat16)
    inside = jnp.einsum("hts,shp->thp", mixing, block_x, preferred_element_type=jnp.float32)
    keep = segment == segment[length - 1]
    tail = (
        jnp.where(keep[:, None], jnp.exp(cumulative[length - 1][None, :] - cumulative), 0.0)
        * step_size
    )
    scaled = (block_x.astype(jnp.float32) * tail[:, :, None]).astype(jnp.bfloat16)
    keys_heads = jnp.repeat(block_b, per_group, axis=1)
    written = jnp.einsum("thp,thn->hpn", scaled, keys_heads, preferred_element_type=jnp.float32)
    carried = jnp.where(start_at >= length, jnp.exp(cumulative[length - 1]), 0.0)
    return (inside, written, carried, cumulative, segment)


def local(
    head_inputs,
    gate_inputs,
    write_keys,
    read_queries,
    step_logits,
    step_bias,
    decay_log,
    skip_scale,
    norm_gain,
    document_starts,
):
    local_heads = step_bias.shape[0]
    head_x, head_b, head_c, head_logit = (
        lax.all_to_all(head_inputs, "head", split_axis=1, concat_axis=0, tiled=True),
        lax.all_to_all(write_keys, "head", split_axis=1, concat_axis=0, tiled=True),
        lax.all_to_all(read_queries, "head", split_axis=1, concat_axis=0, tiled=True),
        lax.all_to_all(step_logits, "head", split_axis=1, concat_axis=0, tiled=True),
    )
    length = head_x.shape[0]
    blocks = length // BLOCK
    group_count = head_b.shape[1] // STATE
    per_group = local_heads // group_count
    x_blocks = head_x.reshape(blocks, BLOCK, local_heads, HEAD_DIM)
    b_blocks = head_b.reshape(blocks, BLOCK, group_count, STATE)
    c_blocks = head_c.reshape(blocks, BLOCK, group_count, STATE)
    logit_blocks = head_logit.reshape(blocks, BLOCK, local_heads)

    def local_block(items):
        block_x, block_b, block_c, block_logit, start_at = items
        return block_terms(block_x, block_b, block_c, block_logit, start_at, step_bias, decay_log)

    inside, written, carried, cumulative, segment = lax.map(
        local_block, (x_blocks, b_blocks, c_blocks, logit_blocks, document_starts)
    )

    def summarize(carry_pair, items):
        total, running = carry_pair
        factor, term = items
        return ((total * factor, factor[:, None, None] * running + term), None)

    zero_state = jnp.zeros((local_heads, HEAD_DIM, STATE), jnp.float32)
    (own_decay, own_state), _ = lax.scan(
        summarize, (jnp.ones((local_heads,), jnp.float32), zero_state), (carried, written)
    )

    def combine(earlier, later):
        return (earlier[0] * later[0], later[0][:, None, None] * earlier[1] + later[1])

    _, incoming = entering(
        (own_decay, own_state), "ctx", combine, (jnp.ones_like(own_decay), zero_state)
    )

    def advance(running, items):
        block_x, block_c, inside_part, carried_part, written_part, cumulative_part, segment_part = (
            items
        )
        frozen = running.astype(jnp.bfloat16)
        query_heads = jnp.repeat(block_c, per_group, axis=1)
        outside = jnp.einsum(
            "thn,hpn->thp", query_heads, frozen, preferred_element_type=jnp.float32
        )
        factor = jnp.where(segment_part[:, None], 0.0, jnp.exp(cumulative_part))
        mixed = (
            inside_part
            + outside * factor[:, :, None]
            + skip_scale[None, :, None] * block_x.astype(jnp.float32)
        ).astype(jnp.bfloat16)
        return (carried_part[:, None, None] * running + written_part, mixed)

    _, mixed = lax.scan(
        advance, incoming, (x_blocks, c_blocks, inside, carried, written, cumulative, segment)
    )
    scanned = mixed.reshape(length, local_heads * HEAD_DIM)
    returned = lax.all_to_all(scanned, "head", split_axis=0, concat_axis=1, tiled=True)
    gated = returned.astype(jnp.float32) * jax.nn.silu(gate_inputs.astype(jnp.float32))
    power = jnp.mean(gated * gated, axis=-1, keepdims=True)
    return (gated * lax.rsqrt(power + 1e-05) * norm_gain).astype(jnp.bfloat16)


def solution(mesh):
    return jax.shard_map(
        local,
        mesh=mesh,
        in_specs=(
            P(("ctx", "head"), None),
            P(("ctx", "head"), None),
            P(("ctx", "head"), None),
            P(("ctx", "head"), None),
            P(("ctx", "head"), None),
            P("head"),
            P("head"),
            P("head"),
            P(),
            P("ctx"),
        ),
        out_specs=P(("ctx", "head"), None),
        check_vma=False,
    )
```

profile of v0, /device:TPU:30, one launch (start us, length us, event | category | flops | bytes accessed | tf_op | source)
XLA Modules:
  0.0 285.5 jit_solution(590334770697413025)
XLA Ops:
  8.1 5.3 %all-to-all-start.1 = ((bf16[128,8,16]{0,2,1:T(8,128)(2,1)}), bf16[128,8,16]{0,2,1:T(8,128)(2,1)S(1)}, u32[]{:S(2)}, u32[]{:S(2)}) async-start(bf16[128,8,16]{0,2,1:T(8,128)(2,1)} %bitcast.27), calls=%async_computation.1 | async-start | bytes 65536 | tf_op jit(solution)/shard_map/all_to_all | solution.py:69
  14.1 4.7 %all-to-all-done.1 = bf16[128,8,16]{0,2,1:T(8,128)(2,1)S(1)} async-done(((bf16[128,8,16]{0,2,1:T(8,128)(2,1)}), bf16[128,8,16]{0,2,1:T(8,128)(2,1)S(1)}, u32[]{:S(2)}, u32[]{:S(2)}) %all-to-all-start.1) | async-done | bytes 32800 | tf_op jit(solution)/shard_map/all_to_all | solution.py:69
  18.8 3.4 %all-to-all-start.2 = ((bf16[128,8,128]{2,0,1:T(8,128)(2,1)}), bf16[128,8,128]{2,0,1:T(8,128)(2,1)S(1)}, u32[]{:S(2)}, u32[]{:S(2)}) async-start(bf16[128,8,128]{2,0,1:T(8,128)(2,1)} %copy_bitcast_fusion.3), calls=%async_computation.2 | async-start | bytes 524288 | tf_op jit(solution)/shard_map/all_to_all | solution.py:68
  22.3 4.1 %copy.50 = bf16[128,8192]{0,1:T(8,128)(2,1)} copy(bf16[128,8192]{1,0:T(8,128)(2,1)} %param.18) | data formatting | bytes 4194304 | tf_op args[0]
  26.4 3.3 %all-to-all-done.2 = bf16[128,8,128]{2,0,1:T(8,128)(2,1)S(1)} async-done(((bf16[128,8,128]{2,0,1:T(8,128)(2,1)}), bf16[128,8,128]{2,0,1:T(8,128)(2,1)S(1)}, u32[]{:S(2)}, u32[]{:S(2)}) %all-to-all-start.2) | async-done | bytes 262176 | tf_op jit(solution)/shard_map/all_to_all | solution.py:68
  29.7 3.6 %all-to-all-start = ((bf16[128,8,1024]{0,2,1:T(8,128)(2,1)}), bf16[128,8,1024]{0,2,1:T(8,128)(2,1)S(1)}, u32[]{:S(2)}, u32[]{:S(2)}) async-start(bf16[128,8,1024]{0,2,1:T(8,128)(2,1)} %bitcast.210), calls=%async_computation | async-start | bytes 4194304 | tf_op jit(solution)/shard_map/all_to_all | solution.py:66
  34.1 26.4 %all-to-all-done = bf16[128,8,1024]{0,2,1:T(8,128)(2,1)S(1)} async-done(((bf16[128,8,1024]{0,2,1:T(8,128)(2,1)}), bf16[128,8,1024]{0,2,1:T(8,128)(2,1)S(1)}, u32[]{:S(2)}, u32[]{:S(2)}) %all-to-all-start) | async-done | bytes 2097184 | tf_op jit(solution)/shard_map/all_to_all | solution.py:66
  60.4 3.4 %all-to-all-start.3 = ((bf16[128,8,128]{2,0,1:T(8,128)(2,1)}), bf16[128,8,128]{2,0,1:T(8,128)(2,1)S(1)}, u32[]{:S(2)}, u32[]{:S(2)}) async-start(bf16[128,8,128]{2,0,1:T(8,128)(2,1)} %copy_bitcast_fusion.2), calls=%async_computation.3 | async-start | bytes 524288 | tf_op jit(solution)/shard_map/all_to_all | solution.py:67
  64.1 4.3 %copy.51 = bf16[8,128,1024]{1,0,2:T(8,128)(2,1)} copy(bf16[8,128,1024]{1,2,0:T(8,128)(2,1)} %bitcast.209) | data formatting | bytes 4194304 | tf_op jit(solution)/shard_map/all_to_all | solution.py:66
  68.3 4.4 %reshape.220 = bf16[4,256,16,64]{1,0,3,2:T(4,128)(2,1)} reshape(bf16[8,128,1024]{1,0,2:T(8,128)(2,1)} %copy.51) | data formatting | bytes 4194304 | tf_op jit(solution)/shard_map/reshape | solution.py:75
  76.0 47.2 %while.57 = (s32[]{:T(128)}, f32[4,256,16,64]{1,3,2,0:T(8,128)}, f32[4,16,64,128]{3,2,1,0:T(8,128)S(1)}, f32[4,16]{1,0:T(4,128)S(1)}, f32[4,256,16]{1,2,0:T(8,12...) while((s32[]{:T(128)}, f32[4,256,16,64]{1,3,2,0:T(8,128)}, ...), condition=%wide.region_3.4_spmd, body=%wide.region_0.3_spmd.sunk | while | flops 225993792 | bytes 3875038 | solution.py:84
  81.4 3.6 %fusion.67 = f32[4,256,16,64]{1,3,2,0:T(8,128)} fusion(f32[4,256,16,64]{1,3,2,0:T(8,128)} %get-tuple-element.745, s32[]{:T(128)} %get-tuple-element.744, f32[16,256]{1,0:T(8,128)S(1)} %get-tuple-element.700, f32[256,256]{1,0:T(8,128)S(1)} %fusion.65, f32[16,256]{1,0:T(8,128)S(1)} %get-tuple-element.701, pred[256,256]{1,0:T(8,128)(4,1)S(1)} %fusion.66, ...), kind=kOutput, calls=%fused_computation.16.clone.1 | convolution fusion | flops 140509184 | bytes 1950720 | tf_op jit(solution)/shard_map/while/body/eval_jaxpr/hts,shp->thp/dot_general | solution.py:39
  93.2 3.6 %fusion.67 = f32[4,256,16,64]{1,3,2,0:T(8,128)} fusion(f32[4,256,16,64]{1,3,2,0:T(8,128)} %get-tuple-element.745, s32[]{:T(128)} %get-tuple-element.744, f32[16,256]{1,0:T(8,128)S(1)} %get-tuple-element.700, f32[256,256]{1,0:T(8,128)S(1)} %fusion.65, f32[16,256]{1,0:T(8,128)S(1)} %get-tuple-element.701, pred[256,256]{1,0:T(8,128)(4,1)S(1)} %fusion.66, ...), kind=kOutput, calls=%fused_computation.16.clone.1 | convolution fusion | flops 140509184 | bytes 1950720 | tf_op jit(solution)/shard_map/while/body/eval_jaxpr/hts,shp->thp/dot_general | solution.py:39
  105.0 3.6 %fusion.67 = f32[4,256,16,64]{1,3,2,0:T(8,128)} fusion(f32[4,256,16,64]{1,3,2,0:T(8,128)} %get-tuple-element.745, s32[]{:T(128)} %get-tuple-element.744, f32[16,256]{1,0:T(8,128)S(1)} %get-tuple-element.700, f32[256,256]{1,0:T(8,128)S(1)} %fusion.65, f32[16,256]{1,0:T(8,128)S(1)} %get-tuple-element.701, pred[256,256]{1,0:T(8,128)(4,1)S(1)} %fusion.66, ...), kind=kOutput, calls=%fused_computation.16.clone.1 | convolution fusion | flops 140509184 | bytes 1950720 | tf_op jit(solution)/shard_map/while/body/eval_jaxpr/hts,shp->thp/dot_general | solution.py:39
  116.8 3.6 %fusion.67 = f32[4,256,16,64]{1,3,2,0:T(8,128)} fusion(f32[4,256,16,64]{1,3,2,0:T(8,128)} %get-tuple-element.745, s32[]{:T(128)} %get-tuple-element.744, f32[16,256]{1,0:T(8,128)S(1)} %get-tuple-element.700, f32[256,256]{1,0:T(8,128)S(1)} %fusion.65, f32[16,256]{1,0:T(8,128)S(1)} %get-tuple-element.701, pred[256,256]{1,0:T(8,128)(4,1)S(1)} %fusion.66, ...), kind=kOutput, calls=%fused_computation.16.clone.1 | convolution fusion | flops 140509184 | bytes 1950720 | tf_op jit(solution)/shard_map/while/body/eval_jaxpr/hts,shp->thp/dot_general | solution.py:39
  126.3 35.4 %all-reduce = f32[256]{0:T(256)S(1)} all-reduce(f32[256]{0:T(256)S(1)} %dynamic-update-slice), channel_id=2, replica_groups=mesh['ctx'=16,'head'=8] {'ctx'}, use_global_device_ids=true, to_apply=%add | all-reduce | flops 256 | bytes 2048
  161.8 33.3 %all-gather.4.cloned.1.call-done = f32[256,64,128]{2,1,0:T(8,128)} async-done(((f32[16,64,128]{2,1,0:T(8,128)}), f32[256,64,128]{2,1,0:T(8,128)}) %all-gather.4.cloned.1.call-update) | async-done | bytes 8388624 | tf_op jit(solution)/shard_map/all_gather | solution.py:13
  195.1 18.6 %while.58 = (s32[]{:T(128)}, f32[16,64,128]{2,1,0:T(8,128)S(1)}, s32[]{:T(128)}, f32[16,16]{1,0:T(8,128)S(1)}, f32[16,16,64,128]{3,2,1,0:T(8,128)}, /*index=5*/s32[]{:T(128)}, s32[]{:T(128)}, s32[]{:T(128)}) while((s32[]{:T(128)}, f32[16,64,128]{2,1,0:T(8,128)S(1)}, s32[]{:T(128)}, f32[16,16]{1,0:T(8,128)S(1)}, f32[16,16,64,128]{3,2,1,0:T(8,128)}, ...), condition=%wide.region_7.8_spmd, body=%wide.region_6.7_spmd.sunk | while | flops 262149 | bytes 1573183 | solution.py:21
  213.7 14.4 %while.59 = (s32[]{:T(128)}, f32[16,64,128]{2,1,0:T(8,128)S(1)}, bf16[4,256,16,64]{1,3,2,0:T(8,128)(2,1)}, f32[4,16]{1,0:T(4,128)S(1)}, f32[4,16,64,128]{3,2,1,0...) while((s32[]{:T(128)}, f32[16,64,128]{2,1,0:T(8,128)S(1)}, ...), condition=%wide.region_9.10_spmd, body=%wide.region_8.9_spmd.sunk | while | flops 69079040 | bytes 4441737 | solution.py:122
  228.1 3.4 %copy.61 = bf16[4,256,16,64]{1,0,3,2:T(4,128)(2,1)S(1)} copy(bf16[4,256,16,64]{1,3,2,0:T(8,128)(2,1)} %get-tuple-element.296) | data formatting | bytes 4194304 | tf_op jit(solution)/shard_map/while | solution.py:122
  236.9 4.4 %all-to-all-start.4 = ((bf16[8,128,1024]{1,2,0:T(8,128)(2,1)}), bf16[8,128,1024]{1,2,0:T(8,128)(2,1)S(1)}, u32[]{:S(2)}, u32[]{:S(2)}) async-start(bf16[8,128,1024]{1,2,0:T(8,128)(2,1)} %copy.62), calls=%async_computation.4 | async-start | bytes 4194304 | tf_op jit(solution)/shard_map/all_to_all | solution.py:126
  241.3 4.1 %copy.63 = bf16[128,8192]{0,1:T(8,128)(2,1)} copy(bf16[128,8192]{1,0:T(8,128)(2,1)} %param.19) | data formatting | bytes 4194304 | tf_op args[1]
  245.4 23.1 %all-to-all-done.4 = bf16[8,128,1024]{1,2,0:T(8,128)(2,1)S(1)} async-done(((bf16[8,128,1024]{1,2,0:T(8,128)(2,1)}), bf16[8,128,1024]{1,2,0:T(8,128)(2,1)S(1)}, u32[]{:S(2)}, u32[]{:S(2)}) %all-to-all-start.4) | async-done | bytes 2097184 | tf_op jit(solution)/shard_map/all_to_all | solution.py:126
  274.5 4.1 %copy.64 = bf16[128,8192]{1,0:T(8,128)(2,1)} copy(bf16[128,8192]{0,1:T(8,128)(2,1)} %multiply_convert_fusion.8) | data formatting | bytes 4194304 | tf_op jit(solution)/shard_map/convert_element_type | solution.py:129
  (198 shorter events, 83.1 us)
Async XLA Ops:
  6.5 6.8 %copy-start = (bf16[128,1024]{1,0:T(8,128)(2,1)S(1)}, bf16[128,1024]{1,0:T(8,128)(2,1)}, u32[]{:S(2)}) copy-start(bf16[128,1024]{1,0:T(8,128)(2,1)} %param.21) | copy-start | bytes 786436
  8.1 10.8 %all-to-all-start.1 = ((bf16[128,8,16]{0,2,1:T(8,128)(2,1)}), bf16[128,8,16]{0,2,1:T(8,128)(2,1)S(1)}, u32[]{:S(2)}, u32[]{:S(2)}) async-start(bf16[128,8,16]{0,2,1:T(8,128)(2,1)} %bitcast.27), calls=%async_computation.1 | async-start | bytes 65536 | tf_op jit(solution)/shard_map/all_to_all | solution.py:69
  18.8 10.9 %all-to-all-start.2 = ((bf16[128,8,128]{2,0,1:T(8,128)(2,1)}), bf16[128,8,128]{2,0,1:T(8,128)(2,1)S(1)}, u32[]{:S(2)}, u32[]{:S(2)}) async-start(bf16[128,8,128]{2,0,1:T(8,128)(2,1)} %copy_bitcast_fusion.3), calls=%async_computation.2 | async-start | bytes 524288 | tf_op jit(solution)/shard_map/all_to_all | solution.py:68
  22.2 11.1 %copy-start.4 = (bf16[128,1024]{1,0:T(8,128)(2,1)S(1)}, bf16[128,1024]{1,0:T(8,128)(2,1)}, u32[]{:S(2)}) copy-start(bf16[128,1024]{1,0:T(8,128)(2,1)} %param.20) | copy-start | bytes 786436
  22.2 41.7 %copy-start.8 = (f32[16]{0:T(128)S(1)}, f32[16]{0:T(128)}, u32[]{:S(2)}) copy-start(f32[16]{0:T(128)} %param.24) | copy-start | bytes 196
  29.7 30.7 %all-to-all-start = ((bf16[128,8,1024]{0,2,1:T(8,128)(2,1)}), bf16[128,8,1024]{0,2,1:T(8,128)(2,1)S(1)}, u32[]{:S(2)}, u32[]{:S(2)}) async-start(bf16[128,8,1024]{0,2,1:T(8,128)(2,1)} %bitcast.210), calls=%async_computation | async-start | bytes 4194304 | tf_op jit(solution)/shard_map/all_to_all | solution.py:66
  60.4 3.5 %copy-start.3 = (bf16[128,8,1024]{0,2,1:T(8,128)(2,1)}, bf16[128,8,1024]{0,2,1:T(8,128)(2,1)S(1)}, u32[]{:S(2)}) copy-start(bf16[128,8,1024]{0,2,1:T(8,128)(2,1)S(1)} %all-to-all-done) | copy-start | bytes 6291460
  60.4 15.6 %all-to-all-start.3 = ((bf16[128,8,128]{2,0,1:T(8,128)(2,1)}), bf16[128,8,128]{2,0,1:T(8,128)(2,1)S(1)}, u32[]{:S(2)}, u32[]{:S(2)}) async-start(bf16[128,8,128]{2,0,1:T(8,128)(2,1)} %copy_bitcast_fusion.2), calls=%async_computation.3 | async-start | bytes 524288 | tf_op jit(solution)/shard_map/all_to_all | solution.py:67
  63.8 131.2 %all-gather.4.cloned.1.call-start = ((), (), s32[]{:S(2)}) async-start(), calls=%async_computation.5 | async-start | bytes 8912896 | tf_op jit(solution)/shard_map/all_gather | solution.py:13
  68.3 7.7 %copy-start.5 = (f32[16]{0:T(128)S(1)}, f32[16]{0:T(128)}, u32[]{:S(2)}) copy-start(f32[16]{0:T(128)} %param.23) | copy-start | bytes 196
  68.3 7.7 %copy-start.9 = (s32[4]{0:T(128)S(1)}, s32[4]{0:T(128)}, u32[]{:S(2)}) copy-start(s32[4]{0:T(128)} %param.27) | copy-start | bytes 52
  123.3 1.5 copy-start.10
  123.9 0.8 copy-start.1
  195.1 18.6 %copy-start.7 = (f32[16]{0:T(128)S(1)}, f32[16]{0:T(128)}, u32[]{:S(2)}) copy-start(f32[16]{0:T(128)} %param.25) | copy-start | bytes 196
  236.9 31.6 %all-to-all-start.4 = ((bf16[8,128,1024]{1,2,0:T(8,128)(2,1)}), bf16[8,128,1024]{1,2,0:T(8,128)(2,1)S(1)}, u32[]{:S(2)}, u32[]{:S(2)}) async-start(bf16[8,128,1024]{1,2,0:T(8,128)(2,1)} %copy.62), calls=%async_computation.4 | async-start | bytes 4194304 | tf_op jit(solution)/shard_map/all_to_all | solution.py:126
  241.3 30.4 %copy-start.6 = (f32[8192]{0:T(1024)S(1)}, f32[8192]{0:T(1024)}, u32[]{:S(2)}) copy-start(f32[8192]{0:T(1024)} %param.26) | copy-start | bytes 98308
  268.5 3.2 %copy-start.2 = (bf16[128,8192]{0,1:T(8,128)(2,1)S(1)}, bf16[128,8192]{0,1:T(8,128)(2,1)}, u32[]{:S(2)}) copy-start(bf16[128,8192]{0,1:T(8,128)(2,1)} %copy.63) | copy-start | bytes 6291460
Sparse Core Ops, SparseCore 0:
  124.8 70.2 all-gather.3
where the time goes:
time: 288 us; the launch traced here: 285 us
  waiting for transfers between devices  90.8 us (32%)
  other arithmetic  45.6 us (16%)
  local copies, waits for them, and re-layouts  44.4 us (15%)
  blocking collectives  35.4 us (12%)
  matrix products  31 us (11%)
  starting transfers between devices  20.2 us (7%)
  between operations  14.3 us (5%)
  loops' own time  3.67 us (1%)
    unnamed x1, blocking collectives  35.4 us
    all_gather x1, waiting for transfers between devices, entering(): gathered = jax.tree.map(lambda a: lax.all_gather(a, axis), part)  33.3 us
    all_to_all x1, waiting for transfers between devices, local(): lax.all_to_all(head_inputs, 'head', split_axis=1, concat_axis=0, tiled=True)  26.4 us
    all_to_all x1, waiting for transfers between devices, local(): lax.all_to_all(scanned, 'head', split_axis=0, concat_axis=1, tiled=True)  23.1 us
    add x15, other arithmetic, combine(): later[0][:, None, None] * earlier[1] + later[1]  17.8 us
    dot_general x4, matrix products, block_terms(): jnp.einsum('hts,shp->thp', mixing, block_x, preferred_element_type=jnp.fl...  14.3 us
    unnamed x28, local copies, waits for them, and re-layouts  11.4 us
    dot_general x4, matrix products, advance(): jnp.einsum('thn,hpn->thp', query_heads, frozen, preferred_element_type=jn...  10.6 us
  transfers between devices with their start and end apart: 6, of which 5 were waited for; matrix products, arithmetic and copies ran while one was open for 8% of the time, Pallas kernels for 0%

commit v1 on v0

v1 whole, which is shorter than its diff:
```python
import functools

import jax
import jax.numpy as jnp
from jax import lax
from jax.experimental import pallas as pl
from jax.experimental.pallas import tpu as pltpu
from jax.sharding import PartitionSpec as P

HEADS = 128
HEAD_DIM = 64
STATE = 128
GROUPS = 8
BLOCK = 256
INNER = HEADS * HEAD_DIM
CHUNK = 128
PER_GROUP = HEADS // GROUPS
WIDE = PER_GROUP * HEAD_DIM
SLAB = 8
SLABS = STATE // SLAB
EPS = 1e-5

bf16 = jnp.bfloat16
f32 = jnp.float32


def iota(shape, axis):
    return lax.broadcasted_iota(jnp.int32, shape, axis)


def spreader(rows, parts):
    lane = iota((rows, WIDE), 0)
    head = iota((rows, WIDE), 1) // HEAD_DIM
    low = lane % 128
    hit = (low % PER_GROUP == head) & (low < parts * PER_GROUP)
    return jnp.where(hit, 1.0, 0.0).astype(bf16)


def to_front(v, group):
    return pltpu.roll(v, (HEADS - PER_GROUP * group) % HEADS, 1)


def spread(v, group, spread_ref):
    front = to_front(v, group)
    high = front.astype(bf16)
    low = (front - high.astype(f32)).astype(bf16)
    return jnp.dot(
        jnp.concatenate([high, low], axis=1), spread_ref[...], preferred_element_type=f32
    )


def softplus(v):
    return jnp.maximum(v, 0.0) + jnp.log1p(jnp.exp(-jnp.abs(v)))


def write_kernel(start_ref, logit_ref, bias_ref, decay_ref, x_ref, b_ref, pay_ref, p_ref, q_ref, spread_ref):
    group = pl.program_id(0)
    start = start_ref[0]

    @pl.when(group == 0)
    def _():
        step = softplus(logit_ref[...].astype(f32) + bias_ref[...])
        rate = -jnp.exp(decay_ref[...]) * step
        lower = jnp.where(iota((CHUNK, CHUNK), 0) >= iota((CHUNK, CHUNK), 1), 1.0, 0.0).astype(bf16)
        cum = jnp.zeros((CHUNK, HEADS), f32)
        rest = rate
        for _ in range(3):
            part = rest.astype(bf16)
            cum = cum + jnp.dot(lower, part, preferred_element_type=f32)
            rest = rest - part.astype(f32)
        p_ref[...] = jnp.exp(cum)
        q_ref[...] = jnp.exp(-cum) * step
        spread_ref[...] = spreader(2 * HEADS, 1)

    xq = (x_ref[...].astype(f32) * spread(q_ref[...], group, spread_ref)).astype(bf16)
    position = iota((CHUNK, STATE), 0)
    kept = (position >= start) | (start >= CHUNK)
    keys = jnp.where(kept, b_ref[...].astype(f32), 0.0).astype(bf16)
    written = lax.dot_general(keys, xq, (((0,), (0,)), ((), ())), preferred_element_type=f32)
    last = jnp.broadcast_to(p_ref[CHUNK - 1 : CHUNK, :], (SLAB, HEADS))
    written = written.reshape(SLABS, SLAB, WIDE) * spread(last, group, spread_ref)[None]
    pay_ref[:, 0, :, :WIDE] = written.astype(bf16)
    carried = to_front(jnp.where(start >= CHUNK, last, 0.0), group)
    high = carried.astype(bf16).astype(f32)
    middle = (carried - high).astype(bf16).astype(f32)
    low = carried - high - middle
    lane = iota((SLAB, HEADS), 1)
    packed = jnp.where(
        lane < PER_GROUP,
        high,
        jnp.where(
            lane < 2 * PER_GROUP,
            pltpu.roll(middle, PER_GROUP, 1),
            jnp.where(lane < 3 * PER_GROUP, pltpu.roll(low, 2 * PER_GROUP, 1), 0.0),
        ),
    ).astype(bf16)
    pay_ref[:, 0, :, WIDE:] = jnp.broadcast_to(packed[None], (SLABS, SLAB, HEADS))


def scan_kernel(chunks, pay_ref, out_ref, carried_ref):
    packed = pay_ref[:, :, WIDE:].astype(f32).reshape(chunks * SLAB, HEADS).astype(bf16)
    carried = jnp.dot(packed, spreader(HEADS, 3), preferred_element_type=f32)
    carried_ref[...] = carried.reshape(chunks, SLAB, WIDE)

    def one(k, state):
        out_ref[k] = state.astype(bf16)
        return carried_ref[k] * state + pay_ref[k, :, :WIDE].astype(f32)

    lax.fori_loop(0, chunks, one, jnp.zeros((SLAB, WIDE), f32), unroll=8)


def inside_kernel(start_ref, p_ref, q_ref, skip_ref, x_ref, b_ref, c_ref, y_ref, spread_ref):
    group = pl.program_id(0)
    start = start_ref[0]

    @pl.when(group == 0)
    def _():
        spread_ref[...] = spreader(2 * HEADS, 1)

    x = x_ref[...].astype(f32)
    xq = (x * spread(q_ref[...], group, spread_ref)).astype(bf16)
    score = lax.dot_general(c_ref[...], b_ref[...], (((1,), (1,)), ((), ())), preferred_element_type=f32)
    t = iota((CHUNK, CHUNK), 0)
    s = iota((CHUNK, CHUNK), 1)
    allowed = (s <= t) & ((t >= start) == (s >= start))
    mixing = jnp.where(allowed, score, 0.0).astype(bf16)
    inside = jnp.dot(mixing, xq, preferred_element_type=f32)
    skip = spread(jnp.broadcast_to(skip_ref[...], (SLAB, HEADS)), group, spread_ref)[:1]
    y_ref[...] = inside * spread(p_ref[...], group, spread_ref) + skip * x


def outside_kernel(start_ref, p_ref, y_ref, c_ref, state_ref, gate_ref, gain_ref, out_ref, gated_ref, power_ref, spread_ref):
    group = pl.program_id(0)
    start = start_ref[0]

    @pl.when(group == 0)
    def _():
        spread_ref[...] = spreader(2 * HEADS, 1)
        power_ref[...] = jnp.zeros_like(power_ref)

    seen = iota((CHUNK, STATE), 0) < start
    queries = jnp.where(seen, c_ref[...].astype(f32), 0.0).astype(bf16)
    state = state_ref[:, 0].astype(f32).reshape(STATE, WIDE).astype(bf16)
    outside = jnp.dot(queries, state, preferred_element_type=f32)
    mixed = y_ref[...] + outside * spread(p_ref[...], group, spread_ref)
    gate = gate_ref[...].astype(f32)
    gated = mixed * (gate / (1.0 + jnp.exp(-gate)))
    gated_ref[group] = gated
    power_ref[...] += jnp.sum(gated * gated, axis=1, keepdims=True)

    @pl.when(group == GROUPS - 1)
    def _():
        scale = lax.rsqrt(power_ref[...] * (1.0 / INNER) + EPS)
        for g in range(GROUPS):
            columns = slice(g * WIDE, (g + 1) * WIDE)
            out_ref[:, columns] = (gated_ref[g] * scale * gain_ref[:, columns]).astype(bf16)


def params(mib):
    return pltpu.CompilerParams(
        dimension_semantics=("arbitrary",), vmem_limit_bytes=mib * 2**20
    )


def local(
    head_inputs,
    gate_inputs,
    write_keys,
    read_queries,
    step_logits,
    step_bias,
    decay_log,
    skip_scale,
    norm_gain,
    document_starts,
):
    half = lax.axis_index("head") % 2
    block_start = document_starts[lax.axis_index("head") // 2]
    begun = block_start - half * CHUNK
    start = jnp.where((begun >= 0) & (begun < CHUNK), begun, CHUNK).reshape(1)
    own = jnp.stack([step_bias, decay_log, skip_scale])
    heads = lax.all_gather(own, "head", axis=1, tiled=True)
    bias, decay, skip = heads[0:1], heads[1:2], heads[2:3]

    smem = pl.BlockSpec(memory_space=pltpu.SMEM)
    small = pl.BlockSpec((CHUNK, HEADS), lambda g: (0, 0))
    row = pl.BlockSpec((1, HEADS), lambda g: (0, 0))
    channels = pl.BlockSpec((CHUNK, WIDE), lambda g: (0, g))
    states = pl.BlockSpec((CHUNK, STATE), lambda g: (0, g))
    table = jax.ShapeDtypeStruct((CHUNK, HEADS), f32)
    spread_scratch = pltpu.VMEM((2 * HEADS, WIDE), bf16)
    chunks = SLABS * GROUPS

    pay, p, q = pl.pallas_call(
        write_kernel,
        grid=(GROUPS,),
        in_specs=[smem, small, row, row, channels, states],
        out_specs=[
            pl.BlockSpec((SLABS, 1, SLAB, WIDE + HEADS), lambda g: (0, g, 0, 0)),
            small,
            small,
        ],
        out_shape=[
            jax.ShapeDtypeStruct((SLABS, GROUPS, SLAB, WIDE + HEADS), bf16),
            table,
            table,
        ],
        scratch_shapes=[spread_scratch],
        compiler_params=params(32),
        cost_estimate=pl.CostEstimate(flops=2 * 2 * CHUNK * STATE * INNER, bytes_accessed=5 * 2**20, transcendentals=0),
        name="write",
    )(start, step_logits, bias, decay, head_inputs, write_keys)

    arrived = lax.all_to_all(
        pay.reshape(chunks, SLAB, WIDE + HEADS), ("ctx", "head"), 0, 0, tiled=True
    )

    y = pl.pallas_call(
        inside_kernel,
        grid=(GROUPS,),
        in_specs=[smem, small, small, row, channels, states, states],
        out_specs=channels,
        out_shape=jax.ShapeDtypeStruct((CHUNK, INNER), f32),
        scratch_shapes=[spread_scratch],
        compiler_params=params(32),
        cost_estimate=pl.CostEstimate(flops=2 * 4 * CHUNK * STATE * INNER, bytes_accessed=7 * 2**20, transcendentals=0),
        name="inside",
    )(start, p, q, skip, head_inputs, write_keys, read_queries)

    frozen = pl.pallas_call(
        functools.partial(scan_kernel, chunks),
        out_shape=jax.ShapeDtypeStruct((chunks, SLAB, WIDE), bf16),
        scratch_shapes=[pltpu.VMEM((chunks, SLAB, WIDE), f32)],
        compiler_params=pltpu.CompilerParams(vmem_limit_bytes=32 * 2**20),
        name="scan",
    )(arrived)

    returned = lax.all_to_all(frozen, ("ctx", "head"), 0, 0, tiled=True)

    return pl.pallas_call(
        outside_kernel,
        grid=(GROUPS,),
        in_specs=[
            smem,
            small,
            channels,
            states,
            pl.BlockSpec((SLABS, 1, SLAB, WIDE), lambda g: (0, g, 0, 0)),
            channels,
            pl.BlockSpec((1, INNER), lambda g: (0, 0)),
        ],
        out_specs=pl.BlockSpec((CHUNK, INNER), lambda g: (0, 0)),
        out_shape=jax.ShapeDtypeStruct((CHUNK, INNER), bf16),
        scratch_shapes=[
            pltpu.VMEM((GROUPS, CHUNK, WIDE), f32),
            pltpu.VMEM((CHUNK, 1), f32),
            spread_scratch,
        ],
        compiler_params=params(32),
        name="outside",
    )(
        start,
        p,
        y,
        read_queries,
        returned.reshape(SLABS, GROUPS, SLAB, WIDE),
        gate_inputs,
        norm_gain.reshape(1, INNER),
    )


def solution(mesh):
    tokens = P(("ctx", "head"), None)
    return jax.shard_map(
        local,
        mesh=mesh,
        in_specs=(tokens,) * 5 + (P("head"),) * 3 + (P(), P("ctx")),
        out_specs=tokens,
        check_vma=False,
    )
```

time: 288 us -> 118 us (0.41)
  the two profiles are of different devices: /device:TPU:30 before, /device:TPU:1 now
where the time goes in v1:
time: 118 us; the launch traced here: 117 us
  blocking collectives  55.6 us (47%)
  waiting for transfers between devices  22.3 us (19%)
  Pallas kernels  20.6 us (17%)
  local copies, waits for them, and re-layouts  11.7 us (10%)
  starting transfers between devices  5.83 us (5%)
    all_to_all x1, blocking collectives, local(): lax.all_to_all(pay.reshape(chunks, SLAB, WIDE + HEADS), ('ctx', 'head'),...  41.5 us
    all_to_all x1, waiting for transfers between devices, local(): returned = lax.all_to_all(frozen, ('ctx', 'head'), 0, 0, tiled=True)  22.3 us
    all_gather x1, blocking collectives, local(): heads = lax.all_gather(own, 'head', axis=1, tiled=True)  14.1 us
    unnamed x23, local copies, waits for them, and re-layouts  10.4 us
    pallas_call x1, Pallas kernels, local(): pl.pallas_call(outside_kernel, grid=(GROUPS,), in_specs=[smem, small, cha...  8.47 us
    pallas_call x1, Pallas kernels, local(): pl.pallas_call(inside_kernel, grid=(GROUPS,), in_specs=[smem, small, smal...  6.04 us
    all_to_all x1, starting transfers between devices, local(): returned = lax.all_to_all(frozen, ('ctx', 'head'), 0, 0, tiled=True)  5.83 us
    pallas_call x1, Pallas kernels, local(): pl.pallas_call(write_kernel, grid=(GROUPS,), in_specs=[smem, small, row,...  4.88 us
  transfers between devices with their start and end apart: 1, of which 1 were waited for; matrix products, arithmetic and copies ran while one was open for 0% of the time, Pallas kernels for 5%

profile of v1, /device:TPU:1, one launch (start us, length us, event | category | flops | bytes accessed | tf_op | source)
XLA Modules:
  0.0 117.4 jit_solution(4363990437583909596)
XLA Ops:
  0.0 1.2 %dynamic_slice.3 = s32[1]{0:T(128)} dynamic-slice(s32[4]{0:T(128)} %param.19, s32[]{:T(128)S(6)} %select_n.19), dynamic_slice_sizes={1} | dynamic-slice | bytes 12 | tf_op jit(solution)/shard_map/dynamic_slice | solution.py:178
  1.9 0.7 maximum_bitcast_fusion
  2.6 14.1 %all-gather = f32[8,16,3]{1,2,0:T(4,128)S(1)} all-gather(f32[1,16,3]{1,2,0:T(4,128)S(1)} %maximum_bitcast_fusion), channel_id=1, replica_groups=mesh['ctx'=16,'head'=8] {'head'}, dimensions={0}, use_global_device_ids=true | all-gather | bytes 1728 | tf_op jit(solution)/shard_map/all_gather | solution.py:182
  16.7 0.1 reshape.17
  16.8 1.6 %copy-done.2 = bf16[128,8192]{1,0:T(8,128)(2,1)S(1)} copy-done((bf16[128,8192]{1,0:T(8,128)(2,1)S(1)}, bf16[128,8192]{1,0:T(8,128)(2,1)}, u32[]{:S(2)}) %copy-start.2) | copy-done | bytes 2097176
  18.4 0.9 copy-done.6
  19.3 0.8 copy-done.9
  20.1 4.9 %write.1 = (bf16[16,8,8,1152]{3,2,1,0:T(8,128)(2,1)S(1)}, f32[128,128]{1,0:T(8,128)S(1)}, f32[128,128]{1,0:T(8,128)S(1)}) custom-call(s32[1]{0:T(128)} %bitcast.1.start_ref, bf16[128,128]{1,0:T(8,128)(2,1)S(1)} %copy-done.9, f32[1,128]{1,0:T(1,128)S(1)} %get-tuple-element.13.bias_ref, f32[1,128]{1,0:T(1,128)S(1)} %get-tuple-element.12.decay_ref, ...), custom_call_target="tpu_custom_call" | custom-call | flops 536870912 | bytes 5242880 | tf_op jit(solution)/shard_map/write/pallas_call | solution.py:194
  24.9 41.5 %all_to_all.10.pay_ref = bf16[128,8,1152]{2,1,0:T(8,128)(2,1)S(1)} all-to-all(bf16[128,8,1152]{2,1,0:T(8,128)(2,1)S(1)} %bitcast.15), channel_id=1, replica_groups=mesh['ctx'=16,'head'=8] {'ctx','head'}, dimensions={0} | all-to-all | bytes 4718592 | tf_op jit(solution)/shard_map/all_to_all | solution.py:214
  66.5 1.2 %scan.1 = bf16[128,8,1024]{2,1,0:T(8,128)(2,1)S(1)} custom-call(bf16[128,8,1152]{2,1,0:T(8,128)(2,1)S(1)} %all_to_all.10.pay_ref), custom_call_target="tpu_custom_call" | custom-call | tf_op jit(solution)/shard_map/scan/pallas_call | solution.py:230
  67.7 0.0 copy-start.4
  67.7 1.3 %copy-done.4 = bf16[128,8,1024]{2,1,0:T(8,128)(2,1)} copy-done((bf16[128,8,1024]{2,1,0:T(8,128)(2,1)}, bf16[128,8,1024]{2,1,0:T(8,128)(2,1)S(1)}, u32[]{:S(2)}) %copy-start.4) | copy-done | bytes 2097176
  69.0 5.8 %all-to-all-start.1 = ((bf16[128,8,1024]{2,1,0:T(8,128)(2,1)}), bf16[128,8,1024]{2,1,0:T(8,128)(2,1)}, u32[]{:S(2)}, u32[]{:S(2)}) async-start(bf16[128,8,1024]{2,1,0:T(8,128)(2,1)} %copy-done.4), calls=%async_computation.1 | async-start | bytes 4194304 | tf_op jit(solution)/shard_map/all_to_all | solution.py:238
  74.9 0.0 copy-done.3
  74.9 0.0 copy-done.7
  74.9 0.0 copy-done.8
  74.9 0.0 copy-start.10
  74.9 6.0 %inside.1.y_ref = f32[128,8192]{1,0:T(8,128)S(1)} custom-call(s32[1]{0:T(128)} %bitcast.1.start_ref, f32[128,128]{1,0:T(8,128)S(1)} %get-tuple-element.8.p_ref, f32[128,128]{1,0:T(8,128)S(1)} %get-tuple-element.9.q_ref, f32[1,128]{1,0:T(1,128)S(1)} %get-tuple-element.11.skip_ref, bf16[128,8192]{1,0:T(8,128)(2,1)S(1)} %copy-done.3, ...), custom_call_target="tpu_custom_call" | custom-call | flops 1073741824 | bytes 7340032 | tf_op jit(solution)/shard_map/inside/pallas_call | solution.py:218
  81.0 0.0 copy-start
  81.0 1.9 %copy-done = f32[128,8192]{1,0:T(8,128)} copy-done((f32[128,8192]{1,0:T(8,128)}, f32[128,8192]{1,0:T(8,128)S(1)}, u32[]{:S(2)}) %copy-start) | copy-done | bytes 4194328
  82.9 22.3 %all-to-all-done.1 = bf16[128,8,1024]{2,1,0:T(8,128)(2,1)} async-done(((bf16[128,8,1024]{2,1,0:T(8,128)(2,1)}), bf16[128,8,1024]{2,1,0:T(8,128)(2,1)}, u32[]{:S(2)}, u32[]{:S(2)}) %all-to-all-start.1) | async-done | bytes 2097184 | tf_op jit(solution)/shard_map/all_to_all | solution.py:238
  105.2 2.2 %copy-done.1 = f32[128,8192]{1,0:T(8,128)S(1)} copy-done((f32[128,8192]{1,0:T(8,128)S(1)}, f32[128,8192]{1,0:T(8,128)}, u32[]{:S(2)}) %copy-start.1) | copy-done | bytes 4194328
  107.4 1.6 %copy-done.5 = bf16[128,8192]{1,0:T(8,128)(2,1)S(1)} copy-done((bf16[128,8192]{1,0:T(8,128)(2,1)S(1)}, bf16[128,8192]{1,0:T(8,128)(2,1)}, u32[]{:S(2)}) %copy-start.5) | copy-done | bytes 2097176
  108.9 8.5 %outside.1 = bf16[128,8192]{1,0:T(8,128)(2,1)} custom-call(s32[1]{0:T(128)} %bitcast.1.start_ref, f32[128,128]{1,0:T(8,128)S(1)} %get-tuple-element.8.p_ref, f32[128,8192]{1,0:T(8,128)S(1)} %copy-done.1, bf16[128,1024]{1,0:T(8,128)(2,1)S(1)} %copy-done.8, bf16[16,8,8,1024]{3,2,1,0:T(8,128)(2,1)} %bitcast.9.state_ref, bf16[128,8192]{1,0:T(8,128)(2,1)S(1)} %copy-done.5, ...), custom_call_target="tpu_custom_call" | custom-call | tf_op jit(solution)/shard_map/outside/pallas_call | solution.py:240
  (11 shorter events, 0.0 us)
Async XLA Ops:
  16.8 1.6 %copy-start.2 = (bf16[128,8192]{1,0:T(8,128)(2,1)S(1)}, bf16[128,8192]{1,0:T(8,128)(2,1)}, u32[]{:S(2)}) copy-start(bf16[128,8192]{1,0:T(8,128)(2,1)} %x_ref.3) | copy-start | bytes 6291460
  18.4 0.9 copy-start.6
  19.3 0.8 copy-start.9
  67.7 1.3 %copy-start.4 = (bf16[128,8,1024]{2,1,0:T(8,128)(2,1)}, bf16[128,8,1024]{2,1,0:T(8,128)(2,1)S(1)}, u32[]{:S(2)}) copy-start(bf16[128,8,1024]{2,1,0:T(8,128)(2,1)S(1)} %scan.1) | copy-start | bytes 6291460
  69.0 5.8 %copy-start.3 = (bf16[128,8192]{1,0:T(8,128)(2,1)S(1)}, bf16[128,8192]{1,0:T(8,128)(2,1)}, u32[]{:S(2)}) copy-start(bf16[128,8192]{1,0:T(8,128)(2,1)} %x_ref.3) | copy-start | bytes 6291460
  69.0 5.9 %copy-start.7 = (bf16[128,1024]{1,0:T(8,128)(2,1)S(1)}, bf16[128,1024]{1,0:T(8,128)(2,1)}, u32[]{:S(2)}) copy-start(bf16[128,1024]{1,0:T(8,128)(2,1)} %b_ref.3) | copy-start | bytes 786436
  69.0 5.9 %copy-start.8 = (bf16[128,1024]{1,0:T(8,128)(2,1)S(1)}, bf16[128,1024]{1,0:T(8,128)(2,1)}, u32[]{:S(2)}) copy-start(bf16[128,1024]{1,0:T(8,128)(2,1)} %c_ref.3) | copy-start | bytes 786436
  69.0 36.1 %all-to-all-start.1 = ((bf16[128,8,1024]{2,1,0:T(8,128)(2,1)}), bf16[128,8,1024]{2,1,0:T(8,128)(2,1)}, u32[]{:S(2)}, u32[]{:S(2)}) async-start(bf16[128,8,1024]{2,1,0:T(8,128)(2,1)} %copy-done.4), calls=%async_computation.1 | async-start | bytes 4194304 | tf_op jit(solution)/shard_map/all_to_all | solution.py:238
  74.9 30.3 %copy-start.10 = (f32[8192]{0:T(1024)S(1)}, f32[8192]{0:T(1024)}, u32[]{:S(2)}) copy-start(f32[8192]{0:T(1024)} %param.18) | copy-start | bytes 98308
  81.0 1.9 %copy-start = (f32[128,8192]{1,0:T(8,128)}, f32[128,8192]{1,0:T(8,128)S(1)}, u32[]{:S(2)}) copy-start(f32[128,8192]{1,0:T(8,128)S(1)} %inside.1.y_ref) | copy-start | bytes 12582916
  105.2 2.2 %copy-start.1 = (f32[128,8192]{1,0:T(8,128)S(1)}, f32[128,8192]{1,0:T(8,128)}, u32[]{:S(2)}) copy-start(f32[128,8192]{1,0:T(8,128)} %copy-done) | copy-start | bytes 12582916
  107.4 1.6 %copy-start.5 = (bf16[128,8192]{1,0:T(8,128)(2,1)S(1)}, bf16[128,8192]{1,0:T(8,128)(2,1)}, u32[]{:S(2)}) copy-start(bf16[128,8192]{1,0:T(8,128)(2,1)} %gate_ref.1) | copy-start | bytes 6291460

commit v2 on v1

v2 whole, which is shorter than its diff:
```python
import functools

import jax
import jax.numpy as jnp
from jax import lax
from jax.experimental import pallas as pl
from jax.experimental.pallas import tpu as pltpu
from jax.sharding import Mesh
from jax.sharding import PartitionSpec as P

HEADS = 128
HEAD_DIM = 64
STATE = 128
GROUPS = 8
INNER = HEADS * HEAD_DIM
CHUNK = 128
CORES = 2
HALF = GROUPS // CORES
HALF_HEADS = HEADS // CORES
PER_GROUP = HEADS // GROUPS
WIDE = PER_GROUP * HEAD_DIM
HALF_WIDE = HALF * WIDE
SLAB = 8
SLABS = STATE // SLAB
LANES = 128
EPS = 1e-5

bf16 = jnp.bfloat16
f32 = jnp.float32


def iota(shape, axis):
    return lax.broadcasted_iota(jnp.int32, shape, axis)


def spreader(rows, parts):
    lane = iota((rows, WIDE), 0) % LANES
    head = iota((rows, WIDE), 1) // HEAD_DIM
    hit = (lane % PER_GROUP == head) & (lane < parts * PER_GROUP)
    return jnp.where(hit, 1.0, 0.0).astype(bf16)


def to_front(v, group):
    return pltpu.roll(v, (LANES - PER_GROUP * group) % LANES, 1)


def spread(v, group, spread_ref):
    front = to_front(v, group)
    high = front.astype(bf16)
    low = (front - high.astype(f32)).astype(bf16)
    return jnp.dot(
        jnp.concatenate([high, low], axis=1), spread_ref[...], preferred_element_type=f32
    )


def softplus(v):
    return jnp.maximum(v, 0.0) + jnp.log1p(jnp.exp(-jnp.abs(v)))


def cumulated(step, decay):
    rate = -jnp.exp(decay) * step
    lower = jnp.where(iota((CHUNK, CHUNK), 0) >= iota((CHUNK, CHUNK), 1), 1.0, 0.0).astype(bf16)
    cum = jnp.zeros(rate.shape, f32)
    for _ in range(3):
        part = rate.astype(bf16)
        cum = cum + jnp.dot(lower, part, preferred_element_type=f32)
        rate = rate - part.astype(f32)
    return jnp.exp(cum), jnp.exp(-cum) * step


def chunk_start(place, starts_ref, core):
    begun = starts_ref[place // CORES] - core * CHUNK
    return jnp.where((begun >= 0) & (begun < CHUNK), begun, CHUNK)


def write_kernel(
    place_ref, starts_ref, *refs
):
    own_refs, (logit_ref, logit_got_ref, x_ref, x_got_ref, b_ref, b_got_ref) = refs[:HALF], refs[HALF : HALF + 6]
    pay_ref, middle_ref, params_ref, decay_ref, p_ref, q_ref, spread_ref = refs[HALF + 6 :]
    group = pl.program_id(0)
    place = place_ref[0]
    core = place % CORES

    @pl.when(group == 0)
    def _():
        spread_ref[...] = spreader(2 * LANES, 1)
        lane = iota((SLAB, LANES), 1)
        params = jnp.zeros((SLAB, LANES), f32)
        for turn in range(HALF):
            some = jnp.where(lane < PER_GROUP, own_refs[turn][...], 0.0)
            params = params + pltpu.roll(some, PER_GROUP * ((place // CORES + turn) % HALF), 1)
        params_ref[...] = params
        half = iota((CHUNK, LANES), 1) < HALF_HEADS
        for chunk, ref in enumerate((logit_ref, logit_got_ref)):
            logit = pltpu.roll(ref[...].astype(f32), (LANES - HALF_HEADS * core) % LANES, 1)
            step = jnp.where(half, softplus(logit + params[0:1]), 0.0)
            p_ref[chunk], q_ref[chunk] = cumulated(step, params[1:2])

    def states(chunk, of_core, x, b):
        start = chunk_start(place, starts_ref, of_core)
        xq = (x[...].astype(f32) * spread(q_ref[chunk], group, spread_ref)).astype(bf16)
        kept = (iota((CHUNK, STATE), 0) >= start) | (start >= CHUNK)
        keys = jnp.where(kept, b[...].astype(f32), 0.0).astype(bf16)
        written = lax.dot_general(keys, xq, (((0,), (0,)), ((), ())), preferred_element_type=f32)
        last = jnp.broadcast_to(p_ref[chunk, CHUNK - 1 : CHUNK, :], (SLAB, LANES))
        wide = spread(last, group, spread_ref)
        written = written.reshape(SLABS, SLAB, WIDE) * wide[None]
        return written, jnp.where(start >= CHUNK, last, 0.0), jnp.where(start >= CHUNK, wide, 0.0)

    def body(first, second):
        before, decay_before, _ = states(*first)
        after, decay_after, wide_after = states(*second)
        middle_ref[...] = before.reshape(STATE, WIDE)
        decay_ref[...] = decay_before
        pay_ref[:, 0, :, :WIDE] = (before * wide_after[None] + after).astype(bf16)
        carried = to_front(decay_before * decay_after, group)
        high = carried.astype(bf16).astype(f32)
        middle = (carried - high).astype(bf16).astype(f32)
        low = carried - high - middle
        lane = iota((SLAB, LANES), 1)
        packed = jnp.where(
            lane < PER_GROUP,
            high,
            jnp.where(
                lane < 2 * PER_GROUP,
                pltpu.roll(middle, PER_GROUP, 1),
                jnp.where(lane < 3 * PER_GROUP, pltpu.roll(low, 2 * PER_GROUP, 1), 0.0),
            ),
        ).astype(bf16)
        pay_ref[:, 0, :, WIDE:] = jnp.broadcast_to(packed[None], (SLABS, SLAB, LANES))

    mine = (0, core, x_ref, b_ref)
    other = (1, 1 - core, x_got_ref, b_got_ref)

    @pl.when(core == 0)
    def _():
        body(mine, other)

    @pl.when(core == 1)
    def _():
        body(other, mine)


def scan_kernel(blocks, pay_ref, out_ref, carried_ref):
    packed = pay_ref[:, :, WIDE:].astype(f32).reshape(blocks * SLAB, LANES).astype(bf16)
    carried = jnp.dot(packed, spreader(LANES, 3), preferred_element_type=f32)
    carried_ref[...] = carried.reshape(blocks, SLAB, WIDE)

    def one(k, state):
        out_ref[k] = state.astype(bf16)
        return carried_ref[k] * state + pay_ref[k, :, :WIDE].astype(f32)

    lax.fori_loop(0, blocks, one, jnp.zeros((SLAB, WIDE), f32), unroll=8)


def inside_kernel(
    place_ref, starts_ref, params_ref, got_ref, logit_ref, x_ref, b_ref, c_ref, gate_ref,
    base_ref, factor_ref, p_ref, q_ref, skip_ref, spread_ref,
):
    group = pl.program_id(0)
    place = place_ref[0]
    core = place % CORES
    start = chunk_start(place, starts_ref, core)

    @pl.when(group == 0)
    def _():
        spread_ref[...] = spreader(2 * LANES, 1)
        params = pltpu.roll(params_ref[...], HALF_HEADS * core, 1) + pltpu.roll(
            got_ref[...], HALF_HEADS * (1 - core), 1
        )
        skip_ref[...] = jnp.broadcast_to(params[2:3], (SLAB, LANES))
        step = softplus(logit_ref[...].astype(f32) + params[0:1])
        p_ref[...], q_ref[...] = cumulated(step, params[1:2])

    x = x_ref[...].astype(f32)
    xq = (x * spread(q_ref[...], group, spread_ref)).astype(bf16)
    score = lax.dot_general(c_ref[...], b_ref[...], (((1,), (1,)), ((), ())), preferred_element_type=f32)
    t = iota((CHUNK, CHUNK), 0)
    s = iota((CHUNK, CHUNK), 1)
    allowed = (s <= t) & ((t >= start) == (s >= start))
    mixing = jnp.where(allowed, score, 0.0).astype(bf16)
    inside = jnp.dot(mixing, xq, preferred_element_type=f32)
    skip = spread(skip_ref[...], group, spread_ref)[:1]
    gate = gate_ref[...].astype(f32)
    silu = gate / (1.0 + jnp.exp(-gate))
    grown = spread(p_ref[...], group, spread_ref)
    base_ref[...] = ((inside * grown + skip * x) * silu).astype(bf16)
    factor_ref[...] = (grown * silu).astype(bf16)


def states_kernel(place_ref, starts_ref, state_ref, middle_ref, decay_ref, own_ref, sent_ref, spread_ref):
    group = pl.program_id(0)
    core = place_ref[0] % CORES

    @pl.when(group == 0)
    def _():
        spread_ref[...] = spreader(2 * LANES, 1)

    block = state_ref[:, 0].astype(f32)
    decay = spread(decay_ref[...], group, spread_ref)
    first = block.reshape(STATE, WIDE).astype(bf16)
    second = ((block * decay[None]).reshape(STATE, WIDE) + middle_ref[...]).astype(bf16)

    @pl.when(core == 0)
    def _():
        own_ref[...] = first
        sent_ref[...] = second

    @pl.when(core == 1)
    def _():
        own_ref[...] = second
        sent_ref[...] = first


def gated_part(place_ref, starts_ref, base_ref, factor_ref, c_ref, state_ref):
    place = place_ref[0]
    start = chunk_start(place, starts_ref, place % CORES)
    seen = iota((CHUNK, STATE), 0) < start
    queries = jnp.where(seen, c_ref[...].astype(f32), 0.0).astype(bf16)
    outside = jnp.dot(queries, state_ref[...], preferred_element_type=f32)
    gated = base_ref[...].astype(f32) + outside * factor_ref[...].astype(f32)
    squares = gated * gated
    power = squares[:, :LANES]
    for i in range(1, WIDE // LANES):
        power = power + squares[:, i * LANES : (i + 1) * LANES]
    return gated, power


def own_kernel(place_ref, starts_ref, base_ref, factor_ref, c_ref, state_ref, gated_ref, power_ref):
    gated, power = gated_part(place_ref, starts_ref, base_ref, factor_ref, c_ref, state_ref)
    gated_ref[...] = gated

    @pl.when(pl.program_id(0) == 0)
    def _():
        power_ref[...] = jnp.zeros_like(power_ref)

    power_ref[...] += power


def last_kernel(
    place_ref, starts_ref, base_ref, factor_ref, c_ref, state_ref, gated_own_ref, power_own_ref, gain_ref, out_ref, gated_ref, power_ref
):
    group = pl.program_id(0)
    gated, power = gated_part(place_ref, starts_ref, base_ref, factor_ref, c_ref, state_ref)
    gated_ref[group] = gated

    @pl.when(group == 0)
    def _():
        power_ref[...] = power_own_ref[...]

    power_ref[...] += power

    @pl.when(group == HALF - 1)
    def _():
        total = jnp.sum(power_ref[...], axis=1, keepdims=True)
        scale = lax.rsqrt(total * (1.0 / INNER) + EPS)
        core = place_ref[0] % CORES
        for g in range(HALF):
            own = pl.ds(pl.multiple_of(core * HALF_WIDE + g * WIDE, WIDE), WIDE)
            out_ref[:, own] = (gated_own_ref[:, g * WIDE : (g + 1) * WIDE] * scale * gain_ref[:, own]).astype(bf16)
            other = pl.ds(pl.multiple_of((1 - core) * HALF_WIDE + g * WIDE, WIDE), WIDE)
            out_ref[:, other] = (gated_ref[g] * scale * gain_ref[:, other]).astype(bf16)


def local(
    head_inputs,
    gate_inputs,
    write_keys,
    read_queries,
    step_logits,
    step_bias,
    decay_log,
    skip_scale,
    norm_gain,
    document_starts,
):
    depth = lax.axis_size("z")
    blocks = lax.axis_size("ctx") * depth
    core = lax.axis_index("core")
    place = (lax.axis_index("z") * CORES + core).astype(jnp.int32).reshape(1)
    swap = [(0, 1), (1, 0)]
    devices = depth * CORES

    own = jnp.pad(jnp.stack([step_bias, decay_log, skip_scale]), ((0, SLAB - 3), (0, LANES - PER_GROUP)))
    turns = [
        lax.ppermute(
            own,
            ("z", "core"),
            [(HALF * (i % CORES) + (i // CORES + turn) % HALF, i) for i in range(devices)],
        )
        for turn in range(HALF)
    ]
    x_got = lax.ppermute(
        lax.dynamic_slice(head_inputs, (0, (1 - core) * HALF_WIDE), (CHUNK, HALF_WIDE)), "core", swap
    )
    b_got = lax.ppermute(
        lax.dynamic_slice(write_keys, (0, (1 - core) * HALF * STATE), (CHUNK, HALF * STATE)), "core", swap
    )
    logit_got = lax.ppermute(step_logits, "core", swap)

    def call(kernel, steps, ins, outs, out_shape, scratch, name, cost=None):
        return pl.pallas_call(
            kernel,
            grid_spec=pltpu.PrefetchScalarGridSpec(
                num_scalar_prefetch=2,
                grid=(steps,),
                in_specs=ins,
                out_specs=outs,
                scratch_shapes=scratch,
            ),
            out_shape=out_shape,
            compiler_params=pltpu.CompilerParams(
                dimension_semantics=("arbitrary",), vmem_limit_bytes=56 * 2**20
            ),
            cost_estimate=cost,
            name=name,
        )

    def shape(dims, kind):
        return jax.ShapeDtypeStruct(dims, kind)

    def fixed(*dims):
        return pl.BlockSpec(dims, lambda g, place, starts: (0,) * len(dims))

    def plain(width):
        return pl.BlockSpec((CHUNK, width), lambda g, place, starts: (0, g))

    def mine(width):
        return pl.BlockSpec((CHUNK, width), lambda g, place, starts: (0, HALF * (place[0] % CORES) + g))

    def others(width):
        return pl.BlockSpec((CHUNK, width), lambda g, place, starts: (0, HALF * (1 - place[0] % CORES) + g))

    def slabs(width):
        return pl.BlockSpec((SLABS, 1, SLAB, width), lambda g, place, starts: (0, g, 0, 0))

    small = fixed(CHUNK, LANES)
    row = fixed(SLAB, LANES)
    spread_scratch = pltpu.VMEM((2 * LANES, WIDE), bf16)
    table = pltpu.VMEM((CHUNK, LANES), f32)
    tables = pltpu.VMEM((2, CHUNK, LANES), f32)

    pay, middle, params, decay = call(
        write_kernel,
        HALF,
        [row] * HALF + [small, small, mine(WIDE), plain(WIDE), mine(STATE), plain(STATE)],
        [slabs(WIDE + LANES), plain(WIDE), row, row],
        [
            shape((SLABS, HALF, SLAB, WIDE + LANES), bf16),
            shape((STATE, HALF_WIDE), f32),
            shape((SLAB, LANES), f32),
            shape((SLAB, LANES), f32),
        ],
        [tables, tables, spread_scratch],
        "write",
    )(place, document_starts, *turns, step_logits, logit_got, head_inputs, x_got, write_keys, b_got)

    arrived = lax.all_to_all(
        pay.reshape(blocks, SLAB, WIDE + LANES), ("ctx", "z"), 0, 0, tiled=True
    )
    params_got = lax.ppermute(params, "core", swap)

    base, factor = call(
        inside_kernel,
        GROUPS,
        [row, row, small, plain(WIDE), plain(STATE), plain(STATE), plain(WIDE)],
        [plain(WIDE), plain(WIDE)],
        [shape((CHUNK, INNER), bf16), shape((CHUNK, INNER), bf16)],
        [table, table, pltpu.VMEM((SLAB, LANES), f32), spread_scratch],
        "inside",
        pl.CostEstimate(flops=2 * 4 * CHUNK * STATE * INNER, bytes_accessed=9 * 2**20, transcendentals=2**20),
    )(place, document_starts, params, params_got, step_logits, head_inputs, write_keys, read_queries, gate_inputs)

    frozen = pl.pallas_call(
        functools.partial(scan_kernel, blocks),
        out_shape=shape((blocks, SLAB, WIDE), bf16),
        scratch_shapes=[pltpu.VMEM((blocks, SLAB, WIDE), f32)],
        compiler_params=pltpu.CompilerParams(vmem_limit_bytes=32 * 2**20),
        name="scan",
    )(arrived)

    returned = lax.all_to_all(frozen, ("ctx", "z"), 0, 0, tiled=True)

    half_state = shape((STATE, HALF_WIDE), bf16)
    state_own, state_sent = call(
        states_kernel,
        HALF,
        [slabs(WIDE), plain(WIDE), row],
        [plain(WIDE), plain(WIDE)],
        [half_state, half_state],
        [spread_scratch],
        "states",
    )(place, document_starts, returned.reshape(SLABS, HALF, SLAB, WIDE), middle, decay)

    state_got = lax.ppermute(state_sent, "core", swap)

    gated, power = call(
        own_kernel,
        HALF,
        [mine(WIDE), mine(WIDE), mine(STATE), plain(WIDE)],
        [plain(WIDE), small],
        [shape((CHUNK, HALF_WIDE), f32), shape((CHUNK, LANES), f32)],
        [],
        "own",
        pl.CostEstimate(flops=2 * CHUNK * STATE * INNER, bytes_accessed=5 * 2**20, transcendentals=0),
    )(place, document_starts, base, factor, read_queries, state_own)

    return call(
        last_kernel,
        HALF,
        [
            others(WIDE),
            others(WIDE),
            others(STATE),
            plain(WIDE),
            fixed(CHUNK, HALF_WIDE),
            small,
            fixed(1, INNER),
        ],
        fixed(CHUNK, INNER),
        shape((CHUNK, INNER), bf16),
        [pltpu.VMEM((HALF, CHUNK, WIDE), f32), table],
        "last",
    )(place, document_starts, base, factor, read_queries, state_got, gated, power, norm_gain.reshape(1, INNER))


def solution(mesh):
    ctx, head = mesh.devices.shape
    split = Mesh(mesh.devices.reshape(ctx, head // CORES, CORES), ("ctx", "z", "core"))
    tokens = P(("ctx", "z", "core"), None)
    return jax.shard_map(
        local,
        mesh=split,
        in_specs=(tokens,) * 5 + (P(("z", "core")),) * 3 + (P(), P("ctx")),
        out_specs=tokens,
        check_vma=False,
    )
```

time: 118 us -> 111 us (0.941)
  waiting for transfers between devices: 22.3 us -> 5.92 us
  Pallas kernels: 20.6 us -> 35.9 us
  starting transfers between devices: 5.83 us -> 16.8 us
  blocking collectives: 55.6 us -> 47.5 us
  local copies, waits for them, and re-layouts: 11.7 us -> 3.9 us
    all_to_all x1 -> x0, waiting for transfers between devices: 22.3 us -> none  [local(): returned = lax.all_to_all(frozen, ('ctx', 'head'), 0, 0, tiled=True)]
    ppermute x0 -> x9, starting transfers between devices: none -> 16.8 us  [the longest x4 11.4 us: local(): lax.ppermute(own, ('z', 'core'), [(HALF * (i % CORES) + (i // CORES + tur...]
    pallas_call x4 -> x6, Pallas kernels: 20.6 us -> 35.9 us  [the longest x1 10.7 us: local(): call(inside_kernel, GROUPS, [row, row, small, plain(WIDE), plain(STATE),...]
    all_gather x1 -> x0, blocking collectives: 14.1 us -> none  [local(): heads = lax.all_gather(own, 'head', axis=1, tiled=True)]
    unnamed x23 -> x30, local copies, waits for them, and re-layouts: 10.4 us -> 2.56 us
    all_to_all x1 -> x2, blocking collectives: 41.5 us -> 47.5 us  [the longest x1 23.9 us: local(): lax.all_to_all(pay.reshape(blocks, SLAB, WIDE + LANES), ('ctx', 'z'), 0,...]
    ppermute x0 -> x9, waiting for transfers between devices: none -> 5.92 us  [the longest x4 3.84 us: local(): lax.ppermute(own, ('z', 'core'), [(HALF * (i % CORES) + (i // CORES + tur...]
    all_to_all x1 -> x0, starting transfers between devices: 5.83 us -> none  [local(): returned = lax.all_to_all(frozen, ('ctx', 'head'), 0, 0, tiled=True)]
  transfers between devices with their start and end apart: 1 -> 9, of which waited for: 1 -> 3; matrix products, arithmetic and copies ran while one was open for 0% -> 0% of each run, Pallas kernels for 5% -> 14%
where the time goes in v2:
time: 111 us; the launch traced here: 110 us
  blocking collectives  47.5 us (43%)
  Pallas kernels  35.9 us (32%)
  starting transfers between devices  16.8 us (15%)
  waiting for transfers between devices  5.92 us (5%)
  local copies, waits for them, and re-layouts  3.9 us (4%)
    all_to_all x1, blocking collectives, local(): lax.all_to_all(pay.reshape(blocks, SLAB, WIDE + LANES), ('ctx', 'z'), 0,...  23.9 us
    all_to_all x1, blocking collectives, local(): returned = lax.all_to_all(frozen, ('ctx', 'z'), 0, 0, tiled=True)  23.7 us
    ppermute x4, starting transfers between devices, local(): lax.ppermute(own, ('z', 'core'), [(HALF * (i % CORES) + (i // CORES + tur...  11.4 us
    pallas_call x1, Pallas kernels, local(): call(inside_kernel, GROUPS, [row, row, small, plain(WIDE), plain(STATE),...  10.7 us
    pallas_call x1, Pallas kernels, local(): call(write_kernel, HALF, [row] * HALF + [small, small, mine(WIDE), plain(...  7.17 us
    pallas_call x1, Pallas kernels, local(): call(last_kernel, HALF, [others(WIDE), others(WIDE), others(STATE), plain...  6.71 us
    pallas_call x1, Pallas kernels, local(): call(states_kernel, HALF, [slabs(WIDE), plain(WIDE), row], [plain(WIDE),...  5.5 us
    pallas_call x1, Pallas kernels, local(): call(own_kernel, HALF, [mine(WIDE), mine(WIDE), mine(STATE), plain(WIDE)]...  5.12 us
  transfers between devices with their start and end apart: 9, of which 3 were waited for; matrix products, arithmetic and copies ran while one was open for 0% of the time, Pallas kernels for 14%

profile of v2, /device:TPU:1, one launch (start us, length us, event | category | flops | bytes accessed | tf_op | source)
XLA Modules:
  0.0 110.3 jit_solution(10210186986978651806)
XLA Ops:
  0.0 1.3 %constant_dynamic-slice_fusion.1 = bf16[128,4096]{1,0:T(8,128)(2,1)S(1)} fusion(bf16[128,8192]{1,0:T(8,128)(2,1)} %x_ref.1, s32[]{:T(128)S(6)} %select_n.6), kind=kLoop, calls=%fused_computation.5 | loop fusion | bytes 2097156 | tf_op jit(solution)/shard_map/dynamic_slice | solution.py:295
  1.4 1.5 %collective-permute-start.5 = (bf16[128,4096]{1,0:T(8,128)(2,1)S(1)}, bf16[128,4096]{1,0:T(8,128)(2,1)S(1)}, u32[]{:S(2)}, u32[]{:S(2)}) collective-permute-start(bf16[128,4096]{1,0:T(8,128)(2,1)S(1)} %constant_dynamic-slice_fusion.1), channel_id=1, source_target_pairs={{0,1},{1,0},{2,3},{3,2},{4,5},{5,4},{6,7},{7,6},{8,9},{9,8},{10,11... | collective-permute-start | bytes 3145736 | tf_op jit(solution)/shard_map/ppermute | solution.py:294
  2.9 0.1 collective-permute-start.6
  3.0 0.5 collective-permute-start.4
  3.5 3.9 %collective-permute-start.2 = (f32[8,128]{1,0:T(8,128)S(1)}, f32[8,128]{1,0:T(8,128)S(1)}, u32[]{:S(2)}, u32[]{:S(2)}) collective-permute-start(f32[8,128]{1,0:T(8,128)S(1)} %select_maximum_fusion), channel_id=1, source_target_pairs={{2,0},{6,1},{3,2},{7,3},{0,4},{4,5},{1,6},{5,7},{10,8},{14,9},{11,... | collective-permute-start | bytes 12296 | tf_op jit(solution)/shard_map/ppermute | solution.py:287
  7.4 2.1 %collective-permute-start.1 = (f32[8,128]{1,0:T(8,128)S(1)}, f32[8,128]{1,0:T(8,128)S(1)}, u32[]{:S(2)}, u32[]{:S(2)}) collective-permute-start(f32[8,128]{1,0:T(8,128)S(1)} %select_maximum_fusion), channel_id=1, source_target_pairs={{1,0},{5,1},{2,2},{6,3},{3,4},{7,5},{0,6},{4,7},{9,8},{13,9},{10,1... | collective-permute-start | bytes 12296 | tf_op jit(solution)/shard_map/ppermute | solution.py:287
  9.6 1.9 %collective-permute-start = (f32[8,128]{1,0:T(8,128)S(1)}, f32[8,128]{1,0:T(8,128)S(1)}, u32[]{:S(2)}, u32[]{:S(2)}) collective-permute-start(f32[8,128]{1,0:T(8,128)S(1)} %select_maximum_fusion), channel_id=1, source_target_pairs={{0,0},{4,1},{1,2},{5,3},{2,4},{6,5},{3,6},{7,7},{8,8},{12,9},{9,10... | collective-permute-start | bytes 12296 | tf_op jit(solution)/shard_map/ppermute | solution.py:287
  11.5 1.7 %collective-permute-done.1.refs_1_ = f32[8,128]{1,0:T(8,128)S(1)} collective-permute-done((f32[8,128]{1,0:T(8,128)S(1)}, f32[8,128]{1,0:T(8,128)S(1)}, u32[]{:S(2)}, u32[]{:S(2)}) %collective-permute-start.1) | collective-permute-done | bytes 4128 | tf_op jit(solution)/shard_map/ppermute | solution.py:287
  13.2 3.4 %collective-permute-start.3 = (f32[8,128]{1,0:T(8,128)S(1)}, f32[8,128]{1,0:T(8,128)S(1)}, u32[]{:S(2)}, u32[]{:S(2)}) collective-permute-start(f32[8,128]{1,0:T(8,128)S(1)} %select_maximum_fusion), channel_id=1, source_target_pairs={{3,0},{7,1},{0,2},{4,3},{1,4},{5,5},{2,6},{6,7},{11,8},{15,9},{8,1... | collective-permute-start | bytes 12296 | tf_op jit(solution)/shard_map/ppermute | solution.py:287
  16.7 2.1 %collective-permute-done.3.refs_3_ = f32[8,128]{1,0:T(8,128)S(1)} collective-permute-done((f32[8,128]{1,0:T(8,128)S(1)}, f32[8,128]{1,0:T(8,128)S(1)}, u32[]{:S(2)}, u32[]{:S(2)}) %collective-permute-start.3) | collective-permute-done | bytes 4128 | tf_op jit(solution)/shard_map/ppermute | solution.py:287
  18.9 0.5 copy-done.9
  19.5 0.4 copy-done.2
  19.8 7.2 %write.1 = (bf16[16,4,8,1152]{3,2,1,0:T(8,128)(2,1)}, f32[128,4096]{1,0:T(8,128)}, f32[8,128]{1,0:T(8,128)}, f32[8,128]{1,0:T(8,128)}) custom-call(s32[1]{0:T(128)} %bitcast.place_ref, s32[4]{0:T(128)} %starts_ref.9, f32[8,128]{1,0:T(8,128)} %copy-done.8, f32[8,128]{1,0:T(8,128)} %copy-done.7, f32[8,128]{1,0:T(8,128)} %copy-done.6, f32[8,128]{1,0:T(8,128)} %copy-done.9, ...), custom_call_target="tpu_custom_call" | custom-call | tf_op jit(solution)/shard_map/write/pallas_call | solution.py:344
  27.0 23.9 %all_to_all.10.pay_ref = bf16[64,8,1152]{2,1,0:T(8,128)(2,1)S(1)} all-to-all(bf16[64,8,1152]{2,1,0:T(8,128)(2,1)} %bitcast.8), channel_id=1, replica_groups=mesh['ctx'=16,'z'=4,'core'=2] {'ctx','z'}, dimensions={0} | all-to-all | bytes 2359296 | tf_op jit(solution)/shard_map/all_to_all | solution.py:359
  50.9 0.7 scan.1
  51.6 23.7 %all_to_all.11 = bf16[64,8,1024]{2,1,0:T(8,128)(2,1)} all-to-all(bf16[64,8,1024]{2,1,0:T(8,128)(2,1)S(1)} %scan.1), channel_id=1, replica_groups=mesh['ctx'=16,'z'=4,'core'=2] {'ctx','z'}, dimensions={0} | all-to-all | bytes 2097152 | tf_op jit(solution)/shard_map/all_to_all | solution.py:383
  75.2 5.5 %states.1 = (bf16[128,4096]{1,0:T(8,128)(2,1)}, bf16[128,4096]{1,0:T(8,128)(2,1)}) custom-call(s32[1]{0:T(128)} %bitcast.place_ref, s32[4]{0:T(128)} %starts_ref.9, bf16[16,4,8,1024]{3,2,1,0:T(8,128)(2,1)} %bitcast.7, f32[128,4096]{1,0:T(8,128)} %get-tuple-element.19.middle_ref, f32[8,128]{1,0:T(8,128)} %get-tuple-element.20.decay_ref), custom_call_target="tpu_custom_call" | custom-call | tf_op jit(solution)/shard_map/states/pallas_call | solution.py:386
  80.8 3.3 %collective-permute-start.8 = (bf16[128,4096]{1,0:T(8,128)(2,1)}, bf16[128,4096]{1,0:T(8,128)(2,1)S(1)}, u32[]{:S(2)}, u32[]{:S(2)}) collective-permute-start(bf16[128,4096]{1,0:T(8,128)(2,1)} %get-tuple-element.21), channel_id=1, source_target_pairs={{0,1},{1,0},{2,3},{3,2},{4,5},{5,4},{6,7},{7,6},{8,9},{9,8},{10,11... | collective-permute-start | bytes 3145736 | tf_op jit(solution)/shard_map/ppermute | solution.py:396
  84.1 2.1 %collective-permute-done.7.got_ref = f32[8,128]{1,0:T(8,128)S(1)} collective-permute-done((f32[8,128]{1,0:T(8,128)S(1)}, f32[8,128]{1,0:T(8,128)S(1)}, u32[]{:S(2)}, u32[]{:S(2)}) %collective-permute-start.7) | collective-permute-done | bytes 4128 | tf_op jit(solution)/shard_map/ppermute | solution.py:362
  86.2 0.6 copy-done.11
  86.8 10.7 %inside.1 = (bf16[128,8192]{1,0:T(8,128)(2,1)}, bf16[128,8192]{1,0:T(8,128)(2,1)}) custom-call(s32[1]{0:T(128)} %bitcast.place_ref, s32[4]{0:T(128)} %starts_ref.9, f32[8,128]{1,0:T(8,128)} %get-tuple-element.15.params_ref, f32[8,128]{1,0:T(8,128)} %copy-done.11, bf16[128,128]{1,0:T(8,128)(2,1)} %logit_ref.1, bf16[128,8192]{1,0:T(8,128)(2,1)} %x_ref.1, ...), custom_call_target="tpu_custom_call" | custom-call | flops 1073741824 | bytes 9437184 | tf_op jit(solution)/shard_map/inside/pallas_call | solution.py:364
  97.5 5.1 %own.1 = (f32[128,4096]{1,0:T(8,128)}, f32[128,128]{1,0:T(8,128)}) custom-call(s32[1]{0:T(128)} %bitcast.place_ref, s32[4]{0:T(128)} %starts_ref.9, bf16[128,8192]{1,0:T(8,128)(2,1)} %get-tuple-element.16.base_ref, bf16[128,8192]{1,0:T(8,128)(2,1)} %get-tuple-element.17.factor_ref, bf16[128,1024]{1,0:T(8,128)(2,1)} %c_ref.5, ...), custom_call_target="tpu_custom_call" | custom-call | flops 268435456 | bytes 5242880 | tf_op jit(solution)/shard_map/own/pallas_call | solution.py:398
  102.6 1.0 copy-done.1
  103.6 6.7 %last.1 = bf16[128,8192]{1,0:T(8,128)(2,1)} custom-call(s32[1]{0:T(128)} %bitcast.place_ref, s32[4]{0:T(128)} %starts_ref.9, bf16[128,8192]{1,0:T(8,128)(2,1)} %get-tuple-element.16.base_ref, bf16[128,8192]{1,0:T(8,128)(2,1)} %get-tuple-element.17.factor_ref, bf16[128,1024]{1,0:T(8,128)(2,1)} %c_ref.5, bf16[128,4096]{1,0:T(8,128)(2,1)} %copy-done.1, ...), custom_call_target="tpu_custom_call" | custom-call | tf_op jit(solution)/shard_map/last/pallas_call | solution.py:409
  (35 shorter events, 0.2 us)
Async XLA Ops:
  0.0 2.9 %copy-start = (bf16[128,1024]{1,0:T(8,128)(2,1)S(1)}, bf16[128,1024]{1,0:T(8,128)(2,1)}, u32[]{:S(2)}) copy-start(bf16[128,1024]{1,0:T(8,128)(2,1)} %b_ref.1) | copy-start | bytes 786436
  0.0 3.0 %copy-start.3 = (bf16[128,128]{1,0:T(8,128)(2,1)S(1)}, bf16[128,128]{1,0:T(8,128)(2,1)}, u32[]{:S(2)}) copy-start(bf16[128,128]{1,0:T(8,128)(2,1)} %logit_ref.1) | copy-start | bytes 98308
  0.0 3.5 %copy-start.12 = (f32[16]{0:T(128)S(1)}, f32[16]{0:T(128)}, u32[]{:S(2)}) copy-start(f32[16]{0:T(128)} %param.17) | copy-start | bytes 196
  0.0 3.5 %copy-start.13 = (f32[16]{0:T(128)S(1)}, f32[16]{0:T(128)}, u32[]{:S(2)}) copy-start(f32[16]{0:T(128)} %param.16) | copy-start | bytes 196
  0.0 3.5 %copy-start.14 = (f32[16]{0:T(128)S(1)}, f32[16]{0:T(128)}, u32[]{:S(2)}) copy-start(f32[16]{0:T(128)} %param.15) | copy-start | bytes 196
  1.4 17.4 %collective-permute-start.5 = (bf16[128,4096]{1,0:T(8,128)(2,1)S(1)}, bf16[128,4096]{1,0:T(8,128)(2,1)S(1)}, u32[]{:S(2)}, u32[]{:S(2)}) collective-permute-start(bf16[128,4096]{1,0:T(8,128)(2,1)S(1)} %constant_dynamic-slice_fusion.1), channel_id=1, source_target_pairs={{0,1},{1,0},{2,3},{3,2},{4,5},{5,4},{6,7},{7,6},{8,9},{9,8},{10,11... | collective-permute-start | bytes 3145736 | tf_op jit(solution)/shard_map/ppermute | solution.py:294
  2.9 15.9 %collective-permute-start.6 = (bf16[128,512]{1,0:T(8,128)(2,1)S(1)}, bf16[128,512]{1,0:T(8,128)(2,1)S(1)}, u32[]{:S(2)}, u32[]{:S(2)}) collective-permute-start(bf16[128,512]{1,0:T(8,128)(2,1)S(1)} %constant_dynamic-slice_fusion), channel_id=1, source_target_pairs={{0,1},{1,0},{2,3},{3,2},{4,5},{5,4},{6,7},{7,6},{8,9},{9,8},{10,11... | collective-permute-start | bytes 393224 | tf_op jit(solution)/shard_map/ppermute | solution.py:297
  3.0 15.8 %collective-permute-start.4 = (bf16[128,128]{1,0:T(8,128)(2,1)S(1)}, bf16[128,128]{1,0:T(8,128)(2,1)S(1)}, u32[]{:S(2)}, u32[]{:S(2)}) collective-permute-start(bf16[128,128]{1,0:T(8,128)(2,1)S(1)} %copy-done.3), channel_id=1, source_target_pairs={{0,1},{1,0},{2,3},{3,2},{4,5},{5,4},{6,7},{7,6},{8,9},{9,8},{10,11... | collective-permute-start | bytes 98312 | tf_op jit(solution)/shard_map/ppermute | solution.py:300
  3.5 6.1 %collective-permute-start.2 = (f32[8,128]{1,0:T(8,128)S(1)}, f32[8,128]{1,0:T(8,128)S(1)}, u32[]{:S(2)}, u32[]{:S(2)}) collective-permute-start(f32[8,128]{1,0:T(8,128)S(1)} %select_maximum_fusion), channel_id=1, source_target_pairs={{2,0},{6,1},{3,2},{7,3},{0,4},{4,5},{1,6},{5,7},{10,8},{14,9},{11,... | collective-permute-start | bytes 12296 | tf_op jit(solution)/shard_map/ppermute | solution.py:287
  7.4 5.8 %collective-permute-start.1 = (f32[8,128]{1,0:T(8,128)S(1)}, f32[8,128]{1,0:T(8,128)S(1)}, u32[]{:S(2)}, u32[]{:S(2)}) collective-permute-start(f32[8,128]{1,0:T(8,128)S(1)} %select_maximum_fusion), channel_id=1, source_target_pairs={{1,0},{5,1},{2,2},{6,3},{3,4},{7,5},{0,6},{4,7},{9,8},{13,9},{10,1... | collective-permute-start | bytes 12296 | tf_op jit(solution)/shard_map/ppermute | solution.py:287
  9.6 9.3 %copy-start.6 = (f32[8,128]{1,0:T(8,128)}, f32[8,128]{1,0:T(8,128)S(1)}, u32[]{:S(2)}) copy-start(f32[8,128]{1,0:T(8,128)S(1)} %collective-permute-done.2.refs_2_) | copy-start | bytes 12292
  9.6 7.1 %collective-permute-start = (f32[8,128]{1,0:T(8,128)S(1)}, f32[8,128]{1,0:T(8,128)S(1)}, u32[]{:S(2)}, u32[]{:S(2)}) collective-permute-start(f32[8,128]{1,0:T(8,128)S(1)} %select_maximum_fusion), channel_id=1, source_target_pairs={{0,0},{4,1},{1,2},{5,3},{2,4},{6,5},{3,6},{7,7},{8,8},{12,9},{9,10... | collective-permute-start | bytes 12296 | tf_op jit(solution)/shard_map/ppermute | solution.py:287
  13.2 5.6 %copy-start.7 = (f32[8,128]{1,0:T(8,128)}, f32[8,128]{1,0:T(8,128)S(1)}, u32[]{:S(2)}) copy-start(f32[8,128]{1,0:T(8,128)S(1)} %collective-permute-done.1.refs_1_) | copy-start | bytes 12292
  13.2 5.6 %collective-permute-start.3 = (f32[8,128]{1,0:T(8,128)S(1)}, f32[8,128]{1,0:T(8,128)S(1)}, u32[]{:S(2)}, u32[]{:S(2)}) collective-permute-start(f32[8,128]{1,0:T(8,128)S(1)} %select_maximum_fusion), channel_id=1, source_target_pairs={{3,0},{7,1},{0,2},{4,3},{1,4},{5,5},{2,6},{6,7},{11,8},{15,9},{8,1... | collective-permute-start | bytes 12296 | tf_op jit(solution)/shard_map/ppermute | solution.py:287
  16.7 2.2 %copy-start.8 = (f32[8,128]{1,0:T(8,128)}, f32[8,128]{1,0:T(8,128)S(1)}, u32[]{:S(2)}) copy-start(f32[8,128]{1,0:T(8,128)S(1)} %collective-permute-done.refs_0_) | copy-start | bytes 12292
  18.8 0.6 copy-start.9
  18.8 0.6 copy-start.5
  18.8 0.6 copy-start.4
  18.8 1.0 copy-start.2
  75.2 8.8 %copy-start.10 = (f32[8,128]{1,0:T(8,128)S(1)}, f32[8,128]{1,0:T(8,128)}, u32[]{:S(2)}) copy-start(f32[8,128]{1,0:T(8,128)} %get-tuple-element.15.params_ref) | copy-start | bytes 12292
  80.8 21.9 %collective-permute-start.8 = (bf16[128,4096]{1,0:T(8,128)(2,1)}, bf16[128,4096]{1,0:T(8,128)(2,1)S(1)}, u32[]{:S(2)}, u32[]{:S(2)}) collective-permute-start(bf16[128,4096]{1,0:T(8,128)(2,1)} %get-tuple-element.21), channel_id=1, source_target_pairs={{0,1},{1,0},{2,3},{3,2},{4,5},{5,4},{6,7},{7,6},{8,9},{9,8},{10,11... | collective-permute-start | bytes 3145736 | tf_op jit(solution)/shard_map/ppermute | solution.py:396
  84.0 2.2 %collective-permute-start.7 = (f32[8,128]{1,0:T(8,128)S(1)}, f32[8,128]{1,0:T(8,128)S(1)}, u32[]{:S(2)}, u32[]{:S(2)}) collective-permute-start(f32[8,128]{1,0:T(8,128)S(1)} %copy-done.10), channel_id=1, source_target_pairs={{0,1},{1,0},{2,3},{3,2},{4,5},{5,4},{6,7},{7,6},{8,9},{9,8},{10,11... | collective-permute-start | bytes 12296 | tf_op jit(solution)/shard_map/ppermute | solution.py:362
  86.2 0.6 copy-start.11
  102.6 1.0 copy-start.1

commit v3 on v2

v3 whole, which is shorter than its diff:
```python
import functools

import jax
import jax.numpy as jnp
from jax import lax
from jax.experimental import pallas as pl
from jax.experimental.pallas import tpu as pltpu
from jax.sharding import Mesh
from jax.sharding import PartitionSpec as P

HEADS = 128
HEAD_DIM = 64
STATE = 128
GROUPS = 8
INNER = HEADS * HEAD_DIM
CHUNK = 128
CORES = 2
HALF = GROUPS // CORES
HALF_HEADS = HEADS // CORES
PER_GROUP = HEADS // GROUPS
WIDE = PER_GROUP * HEAD_DIM
HALF_WIDE = HALF * WIDE
SLAB = 8
SLABS = STATE // SLAB
LANES = 128
PARTS = 4
EPS = 1e-5

bf16 = jnp.bfloat16
f32 = jnp.float32


def iota(shape, axis):
    return lax.broadcasted_iota(jnp.int32, shape, axis)


def spreader(rows, parts):
    lane = iota((rows, WIDE), 0) % LANES
    head = iota((rows, WIDE), 1) // HEAD_DIM
    hit = (lane % PER_GROUP == head) & (lane < parts * PER_GROUP)
    return jnp.where(hit, 1.0, 0.0).astype(bf16)


def to_front(v, group):
    return pltpu.roll(v, (LANES - PER_GROUP * group) % LANES, 1)


def spread(v, group, spread_ref):
    front = to_front(v, group)
    high = front.astype(bf16)
    low = (front - high.astype(f32)).astype(bf16)
    return jnp.dot(
        jnp.concatenate([high, low], axis=1), spread_ref[...], preferred_element_type=f32
    )


def softplus(v):
    return jnp.maximum(v, 0.0) + jnp.log1p(jnp.exp(-jnp.abs(v)))


def cumulated(step, decay):
    rate = -jnp.exp(decay) * step
    lower = jnp.where(iota((CHUNK, CHUNK), 0) >= iota((CHUNK, CHUNK), 1), 1.0, 0.0).astype(bf16)
    cum = jnp.zeros(rate.shape, f32)
    for _ in range(3):
        part = rate.astype(bf16)
        cum = cum + jnp.dot(lower, part, preferred_element_type=f32)
        rate = rate - part.astype(f32)
    return jnp.exp(cum), jnp.exp(-cum) * step


def chunk_start(place, starts_ref, core):
    begun = starts_ref[place // CORES] - core * CHUNK
    return jnp.where((begun >= 0) & (begun < CHUNK), begun, CHUNK)


def write_kernel(
    place_ref, starts_ref, own0, own1, own2, own3, logit_ref, logit_got_ref, x_ref, x_got_ref, b_ref, b_got_ref,
    pay_ref, middle_ref, params_ref, decay_ref, spread_ref,
):
    place = place_ref[0]
    core = place % CORES
    spread_ref[...] = spreader(2 * LANES, 1)
    lane = iota((SLAB, LANES), 1)
    params = jnp.zeros((SLAB, LANES), f32)
    for turn, ref in enumerate((own0, own1, own2, own3)):
        some = jnp.where(lane < PER_GROUP, ref[...], 0.0)
        params = params + pltpu.roll(some, PER_GROUP * ((place // CORES + turn) % HALF), 1)
    params_ref[...] = params
    half = iota((CHUNK, LANES), 1) < HALF_HEADS
    chunks = []
    for ref, of_core in ((logit_ref, core), (logit_got_ref, 1 - core)):
        logit = pltpu.roll(ref[...].astype(f32), (LANES - HALF_HEADS * core) % LANES, 1)
        step = jnp.where(half, softplus(logit + params[0:1]), 0.0)
        p, q = cumulated(step, params[1:2])
        start = chunk_start(place, starts_ref, of_core)
        last = jnp.broadcast_to(p[CHUNK - 1 : CHUNK, :], (SLAB, LANES))
        kept = (iota((CHUNK, STATE), 0) >= start) | (start >= CHUNK)
        chunks.append((q, last, jnp.where(start >= CHUNK, last, 0.0), kept))
    whole = chunks[0][2] * chunks[1][2]
    high = whole.astype(bf16).astype(f32)
    middle = (whole - high).astype(bf16).astype(f32)
    low = whole - high - middle
    first_decay = jnp.where(core == 0, chunks[0][2], chunks[1][2])
    second_decay = jnp.where(core == 0, chunks[1][2], chunks[0][2])
    decay_ref[...] = first_decay

    for group in range(HALF):
        at = group * WIDE
        own_at = pl.multiple_of(core * HALF_WIDE + at, WIDE)
        own_key = pl.multiple_of((core * HALF + group) * STATE, STATE)
        xs = (x_ref[:, pl.ds(own_at, WIDE)], x_got_ref[:, at : at + WIDE])
        keys = (b_ref[:, pl.ds(own_key, STATE)], b_got_ref[:, group * STATE : (group + 1) * STATE])
        written = []
        for (q, last, _, kept), x, b in zip(chunks, xs, keys):
            xq = (x.astype(f32) * spread(q, group, spread_ref)).astype(bf16)
            b = jnp.where(kept, b.astype(f32), 0.0).astype(bf16)
            w = lax.dot_general(b, xq, (((0,), (0,)), ((), ())), preferred_element_type=f32)
            written.append(w.reshape(SLABS, SLAB, WIDE) * spread(last, group, spread_ref)[None])
        before = jnp.where(core == 0, written[0], written[1])
        after = jnp.where(core == 0, written[1], written[0])
        middle_ref[:, at : at + WIDE] = before.reshape(STATE, WIDE)
        pay_ref[:, group, :, :WIDE] = (before * spread(second_decay, group, spread_ref)[None] + after).astype(bf16)
        packed = jnp.where(
            lane < PER_GROUP,
            to_front(high, group),
            jnp.where(
                lane < 2 * PER_GROUP,
                to_front(middle, group - 1),
                jnp.where(lane < 3 * PER_GROUP, to_front(low, group - 2), 0.0),
            ),
        ).astype(bf16)
        pay_ref[:, group, :, WIDE:] = jnp.broadcast_to(packed[None], (SLABS, SLAB, LANES))


def scan_kernel(blocks, pay_ref, out_ref, carried_ref):
    packed = pay_ref[:, :, WIDE:].astype(f32).reshape(blocks * SLAB, LANES).astype(bf16)
    carried = jnp.dot(packed, spreader(LANES, 3), preferred_element_type=f32)
    carried_ref[...] = carried.reshape(blocks, SLAB, WIDE)

    def one(k, state):
        out_ref[k] = state.astype(bf16)
        return carried_ref[k] * state + pay_ref[k, :, :WIDE].astype(f32)

    lax.fori_loop(0, blocks, one, jnp.zeros((SLAB, WIDE), f32), unroll=8)


def inside_kernel(
    place_ref, starts_ref, params_ref, got_ref, logit_ref, x_ref, b_ref, c_ref, gate_ref,
    base_ref, factor_ref, spread_ref,
):
    place = place_ref[0]
    core = place % CORES
    start = chunk_start(place, starts_ref, core)
    spread_ref[...] = spreader(2 * LANES, 1)
    params = pltpu.roll(params_ref[...], HALF_HEADS * core, 1) + pltpu.roll(
        got_ref[...], HALF_HEADS * (1 - core), 1
    )
    skips = jnp.broadcast_to(params[2:3], (SLAB, LANES))
    step = softplus(logit_ref[...].astype(f32) + params[0:1])
    p, q = cumulated(step, params[1:2])
    t = iota((CHUNK, CHUNK), 0)
    s = iota((CHUNK, CHUNK), 1)
    allowed = (s <= t) & ((t >= start) == (s >= start))
    for group in range(GROUPS):
        columns = slice(group * WIDE, (group + 1) * WIDE)
        states = slice(group * STATE, (group + 1) * STATE)
        x = x_ref[:, columns].astype(f32)
        xq = (x * spread(q, group, spread_ref)).astype(bf16)
        score = lax.dot_general(
            c_ref[:, states], b_ref[:, states], (((1,), (1,)), ((), ())), preferred_element_type=f32
        )
        mixing = jnp.where(allowed, score, 0.0).astype(bf16)
        inside = jnp.dot(mixing, xq, preferred_element_type=f32)
        skip = spread(skips, group, spread_ref)[:1]
        gate = gate_ref[:, columns].astype(f32)
        silu = gate / (1.0 + jnp.exp(-gate))
        grown = spread(p, group, spread_ref)
        base_ref[:, columns] = ((inside * grown + skip * x) * silu).astype(bf16)
        factor_ref[:, columns] = (grown * silu).astype(bf16)


def states_kernel(place_ref, state_ref, middle_ref, decay_ref, own_ref, sent_ref, spread_ref):
    core = place_ref[0] % CORES
    spread_ref[...] = spreader(2 * LANES, 1)
    for group in range(HALF):
        columns = slice(group * WIDE, (group + 1) * WIDE)
        block = state_ref[:, group].astype(f32)
        decay = spread(decay_ref[...], group, spread_ref)
        first = block.reshape(STATE, WIDE)
        second = (block * decay[None]).reshape(STATE, WIDE) + middle_ref[:, columns]
        own_ref[:, columns] = jnp.where(core == 0, first, second).astype(bf16)
        sent_ref[:, columns] = jnp.where(core == 0, second, first).astype(bf16)


def gated_part(place, starts_ref, half, base_ref, factor_ref, c_ref, state_ref, gated_ref, power):
    start = chunk_start(place, starts_ref, place % CORES)
    seen = iota((CHUNK, STATE), 0) < start
    for group in range(HALF):
        columns = pl.ds(pl.multiple_of(half * HALF_WIDE + group * WIDE, WIDE), WIDE)
        states = pl.ds(pl.multiple_of((half * HALF + group) * STATE, STATE), STATE)
        queries = jnp.where(seen, c_ref[:, states].astype(f32), 0.0).astype(bf16)
        here = slice(group * WIDE, (group + 1) * WIDE)
        outside = jnp.dot(queries, state_ref[:, here], preferred_element_type=f32)
        gated = base_ref[:, columns].astype(f32) + outside * factor_ref[:, columns].astype(f32)
        gated_ref[:, here] = gated
        squares = gated * gated
        for i in range(WIDE // LANES):
            power = power + squares[:, i * LANES : (i + 1) * LANES]
    return power


def own_kernel(place_ref, starts_ref, base_ref, factor_ref, c_ref, state_ref, gated_ref, power_ref):
    place = place_ref[0]
    power_ref[...] = gated_part(
        place, starts_ref, place % CORES, base_ref, factor_ref, c_ref, state_ref, gated_ref,
        jnp.zeros((CHUNK, LANES), f32),
    )


def last_kernel(
    place_ref, starts_ref, base_ref, factor_ref, c_ref, state_ref, gated_own_ref, power_own_ref, gain_ref,
    out_ref, gated_ref, done_ref, sems,
):
    place = place_ref[0]
    core = place % CORES
    power = gated_part(
        place, starts_ref, 1 - core, base_ref, factor_ref, c_ref, state_ref, gated_ref, power_own_ref[...]
    )
    total = jnp.sum(power, axis=1, keepdims=True)
    scale = lax.rsqrt(total * (1.0 / INNER) + EPS)
    rows = CHUNK // PARTS
    copies = []
    for part in range(PARTS):
        some = slice(part * rows, (part + 1) * rows)
        for half, ref in ((core, gated_own_ref), (1 - core, gated_ref)):
            columns = pl.ds(pl.multiple_of(half * HALF_WIDE, HALF_WIDE), HALF_WIDE)
            done_ref[some, columns] = (ref[some, :] * scale[some] * gain_ref[:, columns]).astype(bf16)
        copies.append(pltpu.make_async_copy(done_ref.at[some], out_ref.at[some], sems.at[part]))
        copies[-1].start()
    for copy in copies:
        copy.wait()


def local(
    head_inputs,
    gate_inputs,
    write_keys,
    read_queries,
    step_logits,
    step_bias,
    decay_log,
    skip_scale,
    norm_gain,
    document_starts,
):
    depth = lax.axis_size("z")
    blocks = lax.axis_size("ctx") * depth
    core = lax.axis_index("core")
    place = (lax.axis_index("z") * CORES + core).astype(jnp.int32).reshape(1)
    swap = [(0, 1), (1, 0)]
    devices = depth * CORES

    own = jnp.pad(jnp.stack([step_bias, decay_log, skip_scale]), ((0, SLAB - 3), (0, LANES - PER_GROUP)))
    turns = [
        lax.ppermute(
            own,
            ("z", "core"),
            [(HALF * (i % CORES) + (i // CORES + turn) % HALF, i) for i in range(devices)],
        )
        for turn in range(HALF)
    ]
    x_got = lax.ppermute(
        lax.dynamic_slice(head_inputs, (0, (1 - core) * HALF_WIDE), (CHUNK, HALF_WIDE)), "core", swap
    )
    b_got = lax.ppermute(
        lax.dynamic_slice(write_keys, (0, (1 - core) * HALF * STATE), (CHUNK, HALF * STATE)), "core", swap
    )
    logit_got = lax.ppermute(step_logits, "core", swap)

    smem = pl.BlockSpec(memory_space=pltpu.SMEM)
    vmem = pl.BlockSpec(memory_space=pltpu.VMEM)

    def call(kernel, scalars, operands, out_shape, scratch, name, cost=None, out_specs=None):
        return pl.pallas_call(
            kernel,
            in_specs=[smem] * len(scalars) + [vmem] * len(operands),
            out_specs=out_specs or [vmem] * len(out_shape),
            out_shape=out_shape,
            scratch_shapes=scratch,
            compiler_params=pltpu.CompilerParams(vmem_limit_bytes=24 * 2**20),
            cost_estimate=cost,
            name=name,
        )(*scalars, *operands)

    def shape(dims, kind):
        return jax.ShapeDtypeStruct(dims, kind)

    where = (place, document_starts)
    spread_scratch = pltpu.VMEM((2 * LANES, WIDE), bf16)

    pay, middle, params, decay = call(
        write_kernel,
        where,
        (*turns, step_logits, logit_got, head_inputs, x_got, write_keys, b_got),
        [
            shape((SLABS, HALF, SLAB, WIDE + LANES), bf16),
            shape((STATE, HALF_WIDE), f32),
            shape((SLAB, LANES), f32),
            shape((SLAB, LANES), f32),
        ],
        [spread_scratch],
        "write",
    )

    arrived = lax.all_to_all(
        pay.reshape(blocks, SLAB, WIDE + LANES), ("ctx", "z"), 0, 0, tiled=True
    )
    params_got = lax.ppermute(params, "core", swap)

    base, factor = call(
        inside_kernel,
        where,
        (params, params_got, step_logits, head_inputs, write_keys, read_queries, gate_inputs),
        [shape((CHUNK, INNER), bf16), shape((CHUNK, INNER), bf16)],
        [spread_scratch],
        "inside",
        pl.CostEstimate(flops=2 * 4 * CHUNK * STATE * INNER, bytes_accessed=9 * 2**20, transcendentals=2**20),
    )
    arrived, base, factor = lax.optimization_barrier((arrived, base, factor))

    [frozen] = call(
        functools.partial(scan_kernel, blocks),
        (),
        (arrived,),
        [shape((blocks, SLAB, WIDE), bf16)],
        [pltpu.VMEM((blocks, SLAB, WIDE), f32)],
        "scan",
    )

    returned = lax.all_to_all(frozen, ("ctx", "z"), 0, 0, tiled=True)

    half_state = shape((STATE, HALF_WIDE), bf16)
    state_own, state_sent = call(
        states_kernel,
        (place,),
        (returned.reshape(SLABS, HALF, SLAB, WIDE), middle, decay),
        [half_state, half_state],
        [spread_scratch],
        "states",
    )

    state_got = lax.ppermute(state_sent, "core", swap)

    gated, power = call(
        own_kernel,
        where,
        (base, factor, read_queries, state_own),
        [shape((CHUNK, HALF_WIDE), f32), shape((CHUNK, LANES), f32)],
        [],
        "own",
        pl.CostEstimate(flops=2 * CHUNK * STATE * INNER, bytes_accessed=5 * 2**20, transcendentals=0),
    )

    [out] = call(
        last_kernel,
        where,
        (base, factor, read_queries, state_got, gated, power, norm_gain.reshape(1, INNER)),
        [shape((CHUNK, INNER), bf16)],
        [
            pltpu.VMEM((CHUNK, HALF_WIDE), f32),
            pltpu.VMEM((CHUNK, INNER), bf16),
            pltpu.SemaphoreType.DMA((PARTS,)),
        ],
        "last",
        out_specs=[pl.BlockSpec(memory_space=pl.ANY)],
    )
    return out


def solution(mesh):
    ctx, head = mesh.devices.shape
    split = Mesh(mesh.devices.reshape(ctx, head // CORES, CORES), ("ctx", "z", "core"))
    tokens = P(("ctx", "z", "core"), None)
    return jax.shard_map(
        local,
        mesh=split,
        in_specs=(tokens,) * 5 + (P(("z", "core")),) * 3 + (P(), P("ctx")),
        out_specs=tokens,
        check_vma=False,
    )
```

time: 111 us -> 94.3 us (0.85)
  blocking collectives: 47.5 us -> 25.6 us
  Pallas kernels: 35.9 us -> 14.9 us
  local copies, waits for them, and re-layouts: 3.9 us -> 18.8 us
  starting transfers between devices: 16.8 us -> 26.3 us
  waiting for transfers between devices: 5.92 us -> 7.21 us
    all_to_all x1 -> x0, blocking collectives: 23.9 us -> none  [local(): lax.all_to_all(pay.reshape(blocks, SLAB, WIDE + LANES), ('ctx', 'z'), 0,...]
    pallas_call x6, Pallas kernels: 35.9 us -> 14.9 us  [call(): pl.pallas_call(kernel, in_specs=[smem] * len(scalars) + [vmem] * len(oper...]
    unnamed x30 -> x54, local copies, waits for them, and re-layouts: 2.56 us -> 14.8 us
    all_to_all x0 -> x1, starting transfers between devices: none -> 7.79 us  [local(): lax.all_to_all(pay.reshape(blocks, SLAB, WIDE + LANES), ('ctx', 'z'), 0,...]
    ppermute x1, starting transfers between devices: 0.08 us -> 2.96 us  [local(): params_got = lax.ppermute(params, 'core', swap)]
    all_to_all x1, blocking collectives: 23.7 us -> 25.6 us  [local(): returned = lax.all_to_all(frozen, ('ctx', 'z'), 0, 0, tiled=True)]
    dynamic_slice x1, local copies, waits for them, and re-layouts: 0.01 us -> 1.56 us  [local(): lax.dynamic_slice(write_keys, (0, (1 - core) * HALF * STATE), (CHUNK, HAL...]
    ppermute x1, waiting for transfers between devices: 2.07 us -> 0.82 us  [local(): params_got = lax.ppermute(params, 'core', swap)]
  transfers between devices with their start and end apart: 9 -> 10, of which waited for: 3 -> 5; matrix products, arithmetic and copies ran while one was open for 0% -> 2% of each run, Pallas kernels for 14% -> 7%
where the time goes in v3:
time: 94.3 us; the launch traced here: 93.6 us
  starting transfers between devices  26.3 us (28%)
  blocking collectives  25.6 us (27%)
  local copies, waits for them, and re-layouts  18.8 us (20%)
  Pallas kernels  14.9 us (16%)
  waiting for transfers between devices  7.21 us (8%)
    all_to_all x1, blocking collectives, local(): returned = lax.all_to_all(frozen, ('ctx', 'z'), 0, 0, tiled=True)  25.6 us
    pallas_call x6, Pallas kernels, call(): pl.pallas_call(kernel, in_specs=[smem] * len(scalars) + [vmem] * len(oper...  14.9 us
    unnamed x54, local copies, waits for them, and re-layouts  14.8 us
    ppermute x4, starting transfers between devices, local(): lax.ppermute(own, ('z', 'core'), [(HALF * (i % CORES) + (i // CORES + tur...  11 us
    all_to_all x1, starting transfers between devices, local(): lax.all_to_all(pay.reshape(blocks, SLAB, WIDE + LANES), ('ctx', 'z'), 0,...  7.79 us
    ppermute x4, waiting for transfers between devices, local(): lax.ppermute(own, ('z', 'core'), [(HALF * (i % CORES) + (i // CORES + tur...  4.05 us
    ppermute x1, starting transfers between devices, local(): params_got = lax.ppermute(params, 'core', swap)  2.96 us
    ppermute x1, starting transfers between devices, local(): state_got = lax.ppermute(state_sent, 'core', swap)  2.69 us
  transfers between devices with their start and end apart: 10, of which 5 were waited for; matrix products, arithmetic and copies ran while one was open for 2% of the time, Pallas kernels for 7%

profile of v3, /device:TPU:1, one launch (start us, length us, event | category | flops | bytes accessed | tf_op | source)
XLA Modules:
  0.0 93.6 jit_solution(4829723118789337402)
XLA Ops:
  0.0 2.4 %constant_dynamic-slice_fusion.1 = bf16[128,4096]{1,0:T(8,128)(2,1)} fusion(bf16[128,8192]{1,0:T(8,128)(2,1)} %x_ref.3, s32[]{:T(128)S(6)} %select_n.6), kind=kLoop, calls=%fused_computation.5 | loop fusion | bytes 2097156 | tf_op jit(solution)/shard_map/dynamic_slice | solution.py:274
  2.5 1.4 %collective-permute-start.5 = (bf16[128,4096]{1,0:T(8,128)(2,1)}, bf16[128,4096]{1,0:T(8,128)(2,1)S(1)}, u32[]{:S(2)}, u32[]{:S(2)}) collective-permute-start(bf16[128,4096]{1,0:T(8,128)(2,1)} %constant_dynamic-slice_fusion.1), channel_id=1, source_target_pairs={{0,1},{1,0},{2,3},{3,2},{4,5},{5,4},{6,7},{7,6},{8,9},{9,8},{10,11... | collective-permute-start | bytes 3145736 | tf_op jit(solution)/shard_map/ppermute | solution.py:273
  3.9 1.6 %constant_dynamic-slice_fusion = bf16[128,512]{1,0:T(8,128)(2,1)} fusion(bf16[128,1024]{1,0:T(8,128)(2,1)} %b_ref.3, s32[]{:T(128)S(6)} %select_n.7), kind=kLoop, calls=%fused_computation.4 | loop fusion | bytes 262148 | tf_op jit(solution)/shard_map/dynamic_slice | solution.py:277
  6.6 3.8 %collective-permute-start.2 = (f32[8,128]{1,0:T(8,128)}, f32[8,128]{1,0:T(8,128)S(1)}, u32[]{:S(2)}, u32[]{:S(2)}) collective-permute-start(f32[8,128]{1,0:T(8,128)} %select_maximum_fusion), channel_id=1, source_target_pairs={{2,0},{6,1},{3,2},{7,3},{0,4},{4,5},{1,6},{5,7},{10,8},{14,9},{11,... | collective-permute-start | bytes 12296 | tf_op jit(solution)/shard_map/ppermute | solution.py:266
  10.3 2.1 %collective-permute-start.1 = (f32[8,128]{1,0:T(8,128)}, f32[8,128]{1,0:T(8,128)S(1)}, u32[]{:S(2)}, u32[]{:S(2)}) collective-permute-start(f32[8,128]{1,0:T(8,128)} %select_maximum_fusion), channel_id=1, source_target_pairs={{1,0},{5,1},{2,2},{6,3},{3,4},{7,5},{0,6},{4,7},{9,8},{13,9},{10,1... | collective-permute-start | bytes 12296 | tf_op jit(solution)/shard_map/ppermute | solution.py:266
  12.5 1.9 %collective-permute-start = (f32[8,128]{1,0:T(8,128)}, f32[8,128]{1,0:T(8,128)S(1)}, u32[]{:S(2)}, u32[]{:S(2)}) collective-permute-start(f32[8,128]{1,0:T(8,128)} %select_maximum_fusion), channel_id=1, source_target_pairs={{0,0},{4,1},{1,2},{5,3},{2,4},{6,5},{3,6},{7,7},{8,8},{12,9},{9,10... | collective-permute-start | bytes 12296 | tf_op jit(solution)/shard_map/ppermute | solution.py:266
  14.4 2.0 %collective-permute-done.1.own1 = f32[8,128]{1,0:T(8,128)S(1)} collective-permute-done((f32[8,128]{1,0:T(8,128)}, f32[8,128]{1,0:T(8,128)S(1)}, u32[]{:S(2)}, u32[]{:S(2)}) %collective-permute-start.1) | collective-permute-done | bytes 4128 | tf_op jit(solution)/shard_map/ppermute | solution.py:266
  16.4 3.2 %collective-permute-start.3 = (f32[8,128]{1,0:T(8,128)}, f32[8,128]{1,0:T(8,128)}, u32[]{:S(2)}, u32[]{:S(2)}) collective-permute-start(f32[8,128]{1,0:T(8,128)} %select_maximum_fusion), channel_id=1, source_target_pairs={{3,0},{7,1},{0,2},{4,3},{1,4},{5,5},{2,6},{6,7},{11,8},{15,9},{8,1... | collective-permute-start | bytes 12296 | tf_op jit(solution)/shard_map/ppermute | solution.py:266
  20.2 2.1 %collective-permute-done.3.own3 = f32[8,128]{1,0:T(8,128)} collective-permute-done((f32[8,128]{1,0:T(8,128)}, f32[8,128]{1,0:T(8,128)}, u32[]{:S(2)}, u32[]{:S(2)}) %collective-permute-start.3) | collective-permute-done | bytes 4128 | tf_op jit(solution)/shard_map/ppermute | solution.py:266
  23.9 1.2 %copy-done.13 = bf16[128,4096]{1,0:T(8,128)(2,1)S(1)} copy-done((bf16[128,4096]{1,0:T(8,128)(2,1)S(1)}, bf16[128,4096]{1,0:T(8,128)(2,1)}, u32[]{:S(2)}) %copy-start.13) | copy-done | bytes 1048600
  27.5 4.2 %write.1 = (bf16[16,4,8,1152]{3,2,1,0:T(8,128)(2,1)S(1)}, f32[128,4096]{1,0:T(8,128)S(1)}, f32[8,128]{1,0:T(8,128)S(1)}, f32[8,128]{1,0:T(8,128)S(1)}) custom-call(s32[1]{0:T(128)} %bitcast.place_ref, s32[4]{0:T(128)S(1)} %copy-done.19, f32[8,128]{1,0:T(8,128)S(1)} %copy-done.21, f32[8,128]{1,0:T(8,128)S(1)} %collective-permute-done.1.own1, ...), custom_call_target="tpu_custom_call" | custom-call | tf_op jit(solution)/shard_map/write/pallas_call | solution.py:285
  31.7 1.3 %copy-done.6 = f32[128,4096]{1,0:T(8,128)} copy-done((f32[128,4096]{1,0:T(8,128)}, f32[128,4096]{1,0:T(8,128)S(1)}, u32[]{:S(2)}) %copy-start.6) | copy-done | bytes 2097176
  34.7 7.8 %all-to-all-start = ((bf16[64,8,1152]{2,1,0:T(8,128)(2,1)}), bf16[64,8,1152]{2,1,0:T(8,128)(2,1)S(1)}, u32[]{:S(2)}, u32[]{:S(2)}) async-start(bf16[64,8,1152]{2,1,0:T(8,128)(2,1)} %bitcast.8), calls=%async_computation | async-start | bytes 2359296 | tf_op jit(solution)/shard_map/all_to_all | solution.py:316
  42.5 3.0 %collective-permute-start.7 = (f32[8,128]{1,0:T(8,128)S(1)}, f32[8,128]{1,0:T(8,128)S(1)}, u32[]{:S(2)}, u32[]{:S(2)}) collective-permute-start(f32[8,128]{1,0:T(8,128)S(1)} %copy-done.23), channel_id=1, source_target_pairs={{0,1},{1,0},{2,3},{3,2},{4,5},{5,4},{6,7},{7,6},{8,9},{9,8},{10,11... | collective-permute-start | bytes 12296 | tf_op jit(solution)/shard_map/ppermute | solution.py:319
  46.3 1.6 %copy-done.8 = bf16[128,8192]{1,0:T(8,128)(2,1)S(1)} copy-done((bf16[128,8192]{1,0:T(8,128)(2,1)S(1)}, bf16[128,8192]{1,0:T(8,128)(2,1)}, u32[]{:S(2)}) %copy-start.8) | copy-done | bytes 2097176
  49.6 5.1 %inside.1 = (bf16[128,8192]{1,0:T(8,128)(2,1)S(1)}, bf16[128,8192]{1,0:T(8,128)(2,1)S(1)}) custom-call(s32[1]{0:T(128)} %bitcast.place_ref, s32[4]{0:T(128)S(1)} %copy-done.19, f32[8,128]{1,0:T(8,128)S(1)} %copy-done.23, f32[8,128]{1,0:T(8,128)S(1)} %collective-permute-done.7.got_ref, bf16[128,128]{1,0:T(8,128)(2,1)S(1)} %copy-done.15, ...), custom_call_target="tpu_custom_call" | custom-call | flops 1073741824 | bytes 9437184 | tf_op jit(solution)/shard_map/inside/pallas_call | solution.py:285
  54.8 1.3 %copy-done.1 = bf16[128,8192]{1,0:T(8,128)(2,1)} copy-done((bf16[128,8192]{1,0:T(8,128)(2,1)}, bf16[128,8192]{1,0:T(8,128)(2,1)S(1)}, u32[]{:S(2)}) %copy-start.1) | copy-done | bytes 2097176
  56.1 1.3 %copy-done.3 = bf16[128,8192]{1,0:T(8,128)(2,1)} copy-done((bf16[128,8192]{1,0:T(8,128)(2,1)}, bf16[128,8192]{1,0:T(8,128)(2,1)S(1)}, u32[]{:S(2)}) %copy-start.3) | copy-done | bytes 2097176
  57.4 1.2 %all-to-all-done.pay_ref = bf16[64,8,1152]{2,1,0:T(8,128)(2,1)S(1)} async-done(((bf16[64,8,1152]{2,1,0:T(8,128)(2,1)}), bf16[64,8,1152]{2,1,0:T(8,128)(2,1)S(1)}, u32[]{:S(2)}, u32[]{:S(2)}) %all-to-all-start) | async-done | bytes 1179680 | tf_op jit(solution)/shard_map/all_to_all | solution.py:316
  59.4 25.6 %all_to_all.10 = bf16[64,8,1024]{2,1,0:T(8,128)(2,1)S(1)} all-to-all(bf16[64,8,1024]{2,1,0:T(8,128)(2,1)S(1)} %scan.1), channel_id=1, replica_groups=mesh['ctx'=16,'z'=4,'core'=2] {'ctx','z'}, dimensions={0} | all-to-all | bytes 2097152 | tf_op jit(solution)/shard_map/all_to_all | solution.py:341
  85.8 2.7 %collective-permute-start.8 = (bf16[128,4096]{1,0:T(8,128)(2,1)S(1)}, bf16[128,4096]{1,0:T(8,128)(2,1)S(1)}, u32[]{:S(2)}, u32[]{:S(2)}) collective-permute-start(bf16[128,4096]{1,0:T(8,128)(2,1)S(1)} %get-tuple-element.27), channel_id=1, source_target_pairs={{0,1},{1,0},{2,3},{3,2},{4,5},{5,4},{6,7},{7,6},{8,9},{9,8},{10,11... | collective-permute-start | bytes 3145736 | tf_op jit(solution)/shard_map/ppermute | solution.py:353
  88.5 1.2 %own.1 = (f32[128,4096]{1,0:T(8,128)S(1)}, f32[128,128]{1,0:T(8,128)S(1)}) custom-call(s32[1]{0:T(128)} %bitcast.place_ref, s32[4]{0:T(128)S(1)} %copy-done.19, bf16[128,8192]{1,0:T(8,128)(2,1)S(1)} %copy-done.2, bf16[128,8192]{1,0:T(8,128)(2,1)S(1)} %copy-done.4, bf16[128,1024]{1,0:T(8,128)(2,1)S(1)} %copy-done.5, ...), custom_call_target="tpu_custom_call" | custom-call | flops 268435456 | bytes 5242880 | tf_op jit(solution)/shard_map/own/pallas_call | solution.py:285
  89.7 1.1 %collective-permute-done.8.state_ref = bf16[128,4096]{1,0:T(8,128)(2,1)S(1)} collective-permute-done((bf16[128,4096]{1,0:T(8,128)(2,1)S(1)}, bf16[128,4096]{1,0:T(8,128)(2,1)S(1)}, u32[]{:S(2)}, u32[]{:S(2)}) %collective-permute-start.8) | collective-permute-done | bytes 1048608 | tf_op jit(solution)/shard_map/ppermute | solution.py:353
  90.8 2.9 %last.1 = bf16[128,8192]{1,0:T(8,128)(2,1)} custom-call(s32[1]{0:T(128)} %bitcast.place_ref, s32[4]{0:T(128)S(1)} %copy-done.19, bf16[128,8192]{1,0:T(8,128)(2,1)S(1)} %copy-done.2, bf16[128,8192]{1,0:T(8,128)(2,1)S(1)} %copy-done.4, bf16[128,1024]{1,0:T(8,128)(2,1)S(1)} %copy-done.5, bf16[128,4096]{1,0:T(8,128)(2,1)S(1)} %collective-permute-done.8.state_ref, ...), custom_call_target="tpu_custom_call" | custom-call | tf_op jit(solution)/shard_map/last/pallas_call | solution.py:285
  (60 shorter events, 11.4 us)
Async XLA Ops:
  0.0 23.9 %copy-start = (bf16[128,8192]{1,0:T(8,128)(2,1)S(1)}, bf16[128,8192]{1,0:T(8,128)(2,1)}, u32[]{:S(2)}) copy-start(bf16[128,8192]{1,0:T(8,128)(2,1)} %x_ref.3) | copy-start | bytes 6291460
  0.0 23.9 %copy-start.9 = (bf16[128,1024]{1,0:T(8,128)(2,1)S(1)}, bf16[128,1024]{1,0:T(8,128)(2,1)}, u32[]{:S(2)}) copy-start(bf16[128,1024]{1,0:T(8,128)(2,1)} %b_ref.3) | copy-start | bytes 786436
  0.0 6.0 %copy-start.24 = (f32[16]{0:T(128)S(1)}, f32[16]{0:T(128)}, u32[]{:S(2)}) copy-start(f32[16]{0:T(128)} %param.17) | copy-start | bytes 196
  0.0 6.0 %copy-start.25 = (f32[16]{0:T(128)S(1)}, f32[16]{0:T(128)}, u32[]{:S(2)}) copy-start(f32[16]{0:T(128)} %param.16) | copy-start | bytes 196
  0.0 6.0 %copy-start.26 = (f32[16]{0:T(128)S(1)}, f32[16]{0:T(128)}, u32[]{:S(2)}) copy-start(f32[16]{0:T(128)} %param.15) | copy-start | bytes 196
  0.0 23.9 %copy-start.19 = (s32[4]{0:T(128)S(1)}, s32[4]{0:T(128)}, u32[]{:S(2)}) copy-start(s32[4]{0:T(128)} %starts_ref.7) | copy-start | bytes 52
  2.5 20.4 %collective-permute-start.5 = (bf16[128,4096]{1,0:T(8,128)(2,1)}, bf16[128,4096]{1,0:T(8,128)(2,1)S(1)}, u32[]{:S(2)}, u32[]{:S(2)}) collective-permute-start(bf16[128,4096]{1,0:T(8,128)(2,1)} %constant_dynamic-slice_fusion.1), channel_id=1, source_target_pairs={{0,1},{1,0},{2,3},{3,2},{4,5},{5,4},{6,7},{7,6},{8,9},{9,8},{10,11... | collective-permute-start | bytes 3145736 | tf_op jit(solution)/shard_map/ppermute | solution.py:273
  5.5 16.8 %collective-permute-start.6 = (bf16[128,512]{1,0:T(8,128)(2,1)}, bf16[128,512]{1,0:T(8,128)(2,1)S(1)}, u32[]{:S(2)}, u32[]{:S(2)}) collective-permute-start(bf16[128,512]{1,0:T(8,128)(2,1)} %constant_dynamic-slice_fusion), channel_id=1, source_target_pairs={{0,1},{1,0},{2,3},{3,2},{4,5},{5,4},{6,7},{7,6},{8,9},{9,8},{10,11... | collective-permute-start | bytes 393224 | tf_op jit(solution)/shard_map/ppermute | solution.py:276
  5.5 16.8 %collective-permute-start.4 = (bf16[128,128]{1,0:T(8,128)(2,1)}, bf16[128,128]{1,0:T(8,128)(2,1)}, u32[]{:S(2)}, u32[]{:S(2)}) collective-permute-start(bf16[128,128]{1,0:T(8,128)(2,1)} %logit_ref.3), channel_id=1, source_target_pairs={{0,1},{1,0},{2,3},{3,2},{4,5},{5,4},{6,7},{7,6},{8,9},{9,8},{10,11... | collective-permute-start | bytes 98312 | tf_op jit(solution)/shard_map/ppermute | solution.py:279
  6.6 5.9 %collective-permute-start.2 = (f32[8,128]{1,0:T(8,128)}, f32[8,128]{1,0:T(8,128)S(1)}, u32[]{:S(2)}, u32[]{:S(2)}) collective-permute-start(f32[8,128]{1,0:T(8,128)} %select_maximum_fusion), channel_id=1, source_target_pairs={{2,0},{6,1},{3,2},{7,3},{0,4},{4,5},{1,6},{5,7},{10,8},{14,9},{11,... | collective-permute-start | bytes 12296 | tf_op jit(solution)/shard_map/ppermute | solution.py:266
  10.3 6.1 %collective-permute-start.1 = (f32[8,128]{1,0:T(8,128)}, f32[8,128]{1,0:T(8,128)S(1)}, u32[]{:S(2)}, u32[]{:S(2)}) collective-permute-start(f32[8,128]{1,0:T(8,128)} %select_maximum_fusion), channel_id=1, source_target_pairs={{1,0},{5,1},{2,2},{6,3},{3,4},{7,5},{0,6},{4,7},{9,8},{13,9},{10,1... | collective-permute-start | bytes 12296 | tf_op jit(solution)/shard_map/ppermute | solution.py:266
  12.5 7.1 %collective-permute-start = (f32[8,128]{1,0:T(8,128)}, f32[8,128]{1,0:T(8,128)S(1)}, u32[]{:S(2)}, u32[]{:S(2)}) collective-permute-start(f32[8,128]{1,0:T(8,128)} %select_maximum_fusion), channel_id=1, source_target_pairs={{0,0},{4,1},{1,2},{5,3},{2,4},{6,5},{3,6},{7,7},{8,8},{12,9},{9,10... | collective-permute-start | bytes 12296 | tf_op jit(solution)/shard_map/ppermute | solution.py:266
  16.4 5.9 %collective-permute-start.3 = (f32[8,128]{1,0:T(8,128)}, f32[8,128]{1,0:T(8,128)}, u32[]{:S(2)}, u32[]{:S(2)}) collective-permute-start(f32[8,128]{1,0:T(8,128)} %select_maximum_fusion), channel_id=1, source_target_pairs={{3,0},{7,1},{0,2},{4,3},{1,4},{5,5},{2,6},{6,7},{11,8},{15,9},{8,1... | collective-permute-start | bytes 12296 | tf_op jit(solution)/shard_map/ppermute | solution.py:266
  27.5 18.9 %copy-start.5 = (bf16[128,1024]{1,0:T(8,128)(2,1)S(1)}, bf16[128,1024]{1,0:T(8,128)(2,1)}, u32[]{:S(2)}) copy-start(bf16[128,1024]{1,0:T(8,128)(2,1)} %c_ref.5) | copy-start | bytes 786436
  31.7 1.4 %copy-start.6 = (f32[128,4096]{1,0:T(8,128)}, f32[128,4096]{1,0:T(8,128)S(1)}, u32[]{:S(2)}) copy-start(f32[128,4096]{1,0:T(8,128)S(1)} %get-tuple-element.25.middle_ref) | copy-start | bytes 6291460
  34.7 7.8 %copy-start.23 = (f32[8,128]{1,0:T(8,128)S(1)}, f32[8,128]{1,0:T(8,128)}, u32[]{:S(2)}) copy-start(f32[8,128]{1,0:T(8,128)} %copy-done.22) | copy-start | bytes 12292
  34.7 23.9 %all-to-all-start = ((bf16[64,8,1152]{2,1,0:T(8,128)(2,1)}), bf16[64,8,1152]{2,1,0:T(8,128)(2,1)S(1)}, u32[]{:S(2)}, u32[]{:S(2)}) async-start(bf16[64,8,1152]{2,1,0:T(8,128)(2,1)} %bitcast.8), calls=%async_computation | async-start | bytes 2359296 | tf_op jit(solution)/shard_map/all_to_all | solution.py:316
  42.5 3.8 %collective-permute-start.7 = (f32[8,128]{1,0:T(8,128)S(1)}, f32[8,128]{1,0:T(8,128)S(1)}, u32[]{:S(2)}, u32[]{:S(2)}) collective-permute-start(f32[8,128]{1,0:T(8,128)S(1)} %copy-done.23), channel_id=1, source_target_pairs={{0,1},{1,0},{2,3},{3,2},{4,5},{5,4},{6,7},{7,6},{8,9},{9,8},{10,11... | collective-permute-start | bytes 12296 | tf_op jit(solution)/shard_map/ppermute | solution.py:319
  46.3 1.6 %copy-start.8 = (bf16[128,8192]{1,0:T(8,128)(2,1)S(1)}, bf16[128,8192]{1,0:T(8,128)(2,1)}, u32[]{:S(2)}) copy-start(bf16[128,8192]{1,0:T(8,128)(2,1)} %gate_ref.1) | copy-start | bytes 6291460
  58.6 26.4 %copy-start.7 = (f32[128,4096]{1,0:T(8,128)S(1)}, f32[128,4096]{1,0:T(8,128)}, u32[]{:S(2)}) copy-start(f32[128,4096]{1,0:T(8,128)} %copy-done.6) | copy-start | bytes 6291460
  59.3 29.1 %copy-start.4 = (bf16[128,8192]{1,0:T(8,128)(2,1)S(1)}, bf16[128,8192]{1,0:T(8,128)(2,1)}, u32[]{:S(2)}) copy-start(bf16[128,8192]{1,0:T(8,128)(2,1)} %copy-done.3) | copy-start | bytes 6291460
  85.0 3.5 %copy-start.2 = (bf16[128,8192]{1,0:T(8,128)(2,1)S(1)}, bf16[128,8192]{1,0:T(8,128)(2,1)}, u32[]{:S(2)}) copy-start(bf16[128,8192]{1,0:T(8,128)(2,1)} %copy-done.1) | copy-start | bytes 6291460
  85.8 5.0 %collective-permute-start.8 = (bf16[128,4096]{1,0:T(8,128)(2,1)S(1)}, bf16[128,4096]{1,0:T(8,128)(2,1)S(1)}, u32[]{:S(2)}, u32[]{:S(2)}) collective-permute-start(bf16[128,4096]{1,0:T(8,128)(2,1)S(1)} %get-tuple-element.27), channel_id=1, source_target_pairs={{0,1},{1,0},{2,3},{3,2},{4,5},{5,4},{6,7},{7,6},{8,9},{9,8},{10,11... | collective-permute-start | bytes 3145736 | tf_op jit(solution)/shard_map/ppermute | solution.py:353
  88.5 2.3 %copy-start.18 = (f32[8192]{0:T(1024)S(1)}, f32[8192]{0:T(1024)}, u32[]{:S(2)}) copy-start(f32[8192]{0:T(1024)} %param.18) | copy-start | bytes 98308
  (13 other events, 11.8 us)

commit v4 on v3

--- a/solution.py
+++ b/solution.py
@@ -42,7 +42,7 @@
 
 
 def to_front(v, group):
-    return pltpu.roll(v, (LANES - PER_GROUP * group) % LANES, 1)
+    return pltpu.roll(v, (2 * LANES - PER_GROUP * group) % LANES, 1)
 
 
 def spread(v, group, spread_ref):
@@ -52,6 +52,14 @@
     return jnp.dot(
         jnp.concatenate([high, low], axis=1), spread_ref[...], preferred_element_type=f32
     )
+
+
+def from_front(v, group):
+    return pltpu.roll(v, PER_GROUP * group, 1)
+
+
+def columns_of(group, half, width):
+    return pl.ds(pl.multiple_of((CORES * group + half) * width, width), width)
 
 
 def softplus(v):
@@ -74,24 +82,47 @@
     return jnp.where((begun >= 0) & (begun < CHUNK), begun, CHUNK)
 
 
+def fetch(source, target, sem):
+    copy = pltpu.make_async_copy(source, target, sem)
+    copy.start()
+    return copy
+
+
+def pack_kernel(place_ref, bias_ref, decay_ref, skip_ref, logit_ref, x_ref, b_ref, packed_ref, own_ref, sems):
+    core = place_ref[0] % CORES
+    tail = HALF_WIDE + HALF * STATE
+    copies = [fetch(logit_ref, packed_ref.at[:, pl.ds(tail, LANES)], sems.at[2 * HALF])]
+    for group in range(HALF):
+        to_x, to_key = pl.ds(group * WIDE, WIDE), pl.ds(HALF_WIDE + group * STATE, STATE)
+        copies.append(fetch(x_ref.at[:, columns_of(group, 1 - core, WIDE)], packed_ref.at[:, to_x], sems.at[group]))
+        copies.append(
+            fetch(b_ref.at[:, columns_of(group, 1 - core, STATE)], packed_ref.at[:, to_key], sems.at[HALF + group])
+        )
+    own_ref[...] = jnp.zeros_like(own_ref)
+    for i, ref in enumerate((bias_ref, decay_ref, skip_ref)):
+        own_ref[i : i + 1, :PER_GROUP] = ref[...]
+    for copy in copies:
+        copy.wait()
+
+
 def write_kernel(
-    place_ref, starts_ref, own0, own1, own2, own3, logit_ref, logit_got_ref, x_ref, x_got_ref, b_ref, b_got_ref,
-    pay_ref, middle_ref, params_ref, decay_ref, spread_ref,
+    place_ref, starts_ref, own0, own1, own2, own3, logit_ref, got_ref, x_ref, b_ref,
+    pay_out, middle_out, params_ref, decay_ref, pay_ref, middle_ref, spread_ref, sems,
 ):
     place = place_ref[0]
     core = place % CORES
+    tail = HALF_WIDE + HALF * STATE
     spread_ref[...] = spreader(2 * LANES, 1)
     lane = iota((SLAB, LANES), 1)
     params = jnp.zeros((SLAB, LANES), f32)
     for turn, ref in enumerate((own0, own1, own2, own3)):
         some = jnp.where(lane < PER_GROUP, ref[...], 0.0)
-        params = params + pltpu.roll(some, PER_GROUP * ((place // CORES + turn) % HALF), 1)
+        params = params + from_front(some, 2 * ((place // CORES + turn) % HALF) + core)
     params_ref[...] = params
-    half = iota((CHUNK, LANES), 1) < HALF_HEADS
+    half = iota((CHUNK, LANES), 1) // PER_GROUP % CORES == core
     chunks = []
-    for ref, of_core in ((logit_ref, core), (logit_got_ref, 1 - core)):
-        logit = pltpu.roll(ref[...].astype(f32), (LANES - HALF_HEADS * core) % LANES, 1)
-        step = jnp.where(half, softplus(logit + params[0:1]), 0.0)
+    for logit, of_core in ((logit_ref[...], core), (got_ref[:, tail:], 1 - core)):
+        step = jnp.where(half, softplus(logit.astype(f32) + params[0:1]), 0.0)
         p, q = cumulated(step, params[1:2])
         start = chunk_start(place, starts_ref, of_core)
         last = jnp.broadcast_to(p[CHUNK - 1 : CHUNK, :], (SLAB, LANES))
@@ -101,16 +132,16 @@
     high = whole.astype(bf16).astype(f32)
     middle = (whole - high).astype(bf16).astype(f32)
     low = whole - high - middle
-    first_decay = jnp.where(core == 0, chunks[0][2], chunks[1][2])
     second_decay = jnp.where(core == 0, chunks[1][2], chunks[0][2])
-    decay_ref[...] = first_decay
-
-    for group in range(HALF):
-        at = group * WIDE
-        own_at = pl.multiple_of(core * HALF_WIDE + at, WIDE)
-        own_key = pl.multiple_of((core * HALF + group) * STATE, STATE)
-        xs = (x_ref[:, pl.ds(own_at, WIDE)], x_got_ref[:, at : at + WIDE])
-        keys = (b_ref[:, pl.ds(own_key, STATE)], b_got_ref[:, group * STATE : (group + 1) * STATE])
+    decay_ref[...] = jnp.where(core == 0, chunks[0][2], chunks[1][2])
+
+    sent = []
+    for j in range(HALF):
+        group = 2 * j + core
+        columns = slice(j * WIDE, (j + 1) * WIDE)
+        at = HALF_WIDE + j * STATE
+        xs = (x_ref[:, columns_of(j, core, WIDE)], got_ref[:, columns])
+        keys = (b_ref[:, columns_of(j, core, STATE)], got_ref[:, at : at + STATE])
         written = []
         for (q, last, _, kept), x, b in zip(chunks, xs, keys):
             xq = (x.astype(f32) * spread(q, group, spread_ref)).astype(bf16)
@@ -119,8 +150,7 @@
             written.append(w.reshape(SLABS, SLAB, WIDE) * spread(last, group, spread_ref)[None])
         before = jnp.where(core == 0, written[0], written[1])
         after = jnp.where(core == 0, written[1], written[0])
-        middle_ref[:, at : at + WIDE] = before.reshape(STATE, WIDE)
-        pay_ref[:, group, :, :WIDE] = (before * spread(second_decay, group, spread_ref)[None] + after).astype(bf16)
+        pay_ref[j, :, :, :WIDE] = (before * spread(second_decay, group, spread_ref)[None] + after).astype(bf16)
         packed = jnp.where(
             lane < PER_GROUP,
             to_front(high, group),
@@ -130,7 +160,12 @@
                 jnp.where(lane < 3 * PER_GROUP, to_front(low, group - 2), 0.0),
             ),
         ).astype(bf16)
-        pay_ref[:, group, :, WIDE:] = jnp.broadcast_to(packed[None], (SLABS, SLAB, LANES))
+        pay_ref[j, :, :, WIDE:] = jnp.broadcast_to(packed[None], (SLABS, SLAB, LANES))
+        sent.append(fetch(pay_ref.at[j], pay_out.at[:, j], sems.at[0, j]))
+        middle_ref[j] = before.reshape(STATE, WIDE)
+        sent.append(fetch(middle_ref.at[j], middle_out.at[j], sems.at[1, j]))
+    for copy in sent:
+        copy.wait()
 
 
 def scan_kernel(blocks, pay_ref, out_ref, carried_ref):
@@ -146,22 +181,29 @@
 
 
 def inside_kernel(
-    place_ref, starts_ref, params_ref, got_ref, logit_ref, x_ref, b_ref, c_ref, gate_ref,
-    base_ref, factor_ref, spread_ref,
+    place_ref, starts_ref, params_ref, got_ref, x_ref, logit_in, b_in, c_in, gate_in,
+    base_out, factor_out,
+    logit_ref, b_ref, c_ref, gate_ref, base_ref, factor_ref, spread_ref, sems, sent_sems,
 ):
     place = place_ref[0]
-    core = place % CORES
-    start = chunk_start(place, starts_ref, core)
+    start = chunk_start(place, starts_ref, place % CORES)
+    logit_copy = fetch(logit_in, logit_ref, sems.at[0])
+    b_copy = fetch(b_in, b_ref, sems.at[1])
+    c_copy = fetch(c_in, c_ref, sems.at[2])
+    gate_copy = fetch(gate_in, gate_ref, sems.at[3])
     spread_ref[...] = spreader(2 * LANES, 1)
-    params = pltpu.roll(params_ref[...], HALF_HEADS * core, 1) + pltpu.roll(
-        got_ref[...], HALF_HEADS * (1 - core), 1
-    )
+    params = params_ref[...] + got_ref[...]
     skips = jnp.broadcast_to(params[2:3], (SLAB, LANES))
+    logit_copy.wait()
     step = softplus(logit_ref[...].astype(f32) + params[0:1])
     p, q = cumulated(step, params[1:2])
     t = iota((CHUNK, CHUNK), 0)
     s = iota((CHUNK, CHUNK), 1)
     allowed = (s <= t) & ((t >= start) == (s >= start))
+    b_copy.wait()
+    c_copy.wait()
+    gate_copy.wait()
+    sent = []
     for group in range(GROUPS):
         columns = slice(group * WIDE, (group + 1) * WIDE)
         states = slice(group * STATE, (group + 1) * STATE)
@@ -176,8 +218,12 @@
         gate = gate_ref[:, columns].astype(f32)
         silu = gate / (1.0 + jnp.exp(-gate))
         grown = spread(p, group, spread_ref)
-        base_ref[:, columns] = ((inside * grown + skip * x) * silu).astype(bf16)
-        factor_ref[:, columns] = (grown * silu).astype(bf16)
+        base_ref[group] = ((inside * grown + skip * x) * silu).astype(bf16)
+        factor_ref[group] = (grown * silu).astype(bf16)
+        sent.append(fetch(base_ref.at[group], base_out.at[group], sent_sems.at[0, group]))
+        sent.append(fetch(factor_ref.at[group], factor_out.at[group], sent_sems.at[1, group]))
+    for copy in sent:
+        copy.wait()
 
 
 def states_kernel(place_ref, state_ref, middle_ref, decay_ref, own_ref, sent_ref, spread_ref):
@@ -186,9 +232,9 @@
     for group in range(HALF):
         columns = slice(group * WIDE, (group + 1) * WIDE)
         block = state_ref[:, group].astype(f32)
-        decay = spread(decay_ref[...], group, spread_ref)
+        decay = spread(decay_ref[...], 2 * group + core, spread_ref)
         first = block.reshape(STATE, WIDE)
-        second = (block * decay[None]).reshape(STATE, WIDE) + middle_ref[:, columns]
+        second = (block * decay[None]).reshape(STATE, WIDE) + middle_ref[group]
         own_ref[:, columns] = jnp.where(core == 0, first, second).astype(bf16)
         sent_ref[:, columns] = jnp.where(core == 0, second, first).astype(bf16)
 
@@ -197,12 +243,12 @@
     start = chunk_start(place, starts_ref, place % CORES)
     seen = iota((CHUNK, STATE), 0) < start
     for group in range(HALF):
-        columns = pl.ds(pl.multiple_of(half * HALF_WIDE + group * WIDE, WIDE), WIDE)
-        states = pl.ds(pl.multiple_of((half * HALF + group) * STATE, STATE), STATE)
+        of_all = CORES * group + half
+        states = columns_of(group, half, STATE)
         queries = jnp.where(seen, c_ref[:, states].astype(f32), 0.0).astype(bf16)
         here = slice(group * WIDE, (group + 1) * WIDE)
         outside = jnp.dot(queries, state_ref[:, here], preferred_element_type=f32)
-        gated = base_ref[:, columns].astype(f32) + outside * factor_ref[:, columns].astype(f32)
+        gated = base_ref[of_all].astype(f32) + outside * factor_ref[of_all].astype(f32)
         gated_ref[:, here] = gated
         squares = gated * gated
         for i in range(WIDE // LANES):
@@ -234,8 +280,10 @@
     for part in range(PARTS):
         some = slice(part * rows, (part + 1) * rows)
         for half, ref in ((core, gated_own_ref), (1 - core, gated_ref)):
-            columns = pl.ds(pl.multiple_of(half * HALF_WIDE, HALF_WIDE), HALF_WIDE)
-            done_ref[some, columns] = (ref[some, :] * scale[some] * gain_ref[:, columns]).astype(bf16)
+            for group in range(HALF):
+                columns = columns_of(group, half, WIDE)
+                gated = ref[some, group * WIDE : (group + 1) * WIDE]
+                done_ref[some, columns] = (gated * scale[some] * gain_ref[:, columns]).astype(bf16)
         copies.append(pltpu.make_async_copy(done_ref.at[some], out_ref.at[some], sems.at[part]))
         copies[-1].start()
     for copy in copies:
@@ -259,36 +307,20 @@
     core = lax.axis_index("core")
     place = (lax.axis_index("z") * CORES + core).astype(jnp.int32).reshape(1)
     swap = [(0, 1), (1, 0)]
-    devices = depth * CORES
-
-    own = jnp.pad(jnp.stack([step_bias, decay_log, skip_scale]), ((0, SLAB - 3), (0, LANES - PER_GROUP)))
-    turns = [
-        lax.ppermute(
-            own,
-            ("z", "core"),
-            [(HALF * (i % CORES) + (i // CORES + turn) % HALF, i) for i in range(devices)],
-        )
-        for turn in range(HALF)
-    ]
-    x_got = lax.ppermute(
-        lax.dynamic_slice(head_inputs, (0, (1 - core) * HALF_WIDE), (CHUNK, HALF_WIDE)), "core", swap
-    )
-    b_got = lax.ppermute(
-        lax.dynamic_slice(write_keys, (0, (1 - core) * HALF * STATE), (CHUNK, HALF * STATE)), "core", swap
-    )
-    logit_got = lax.ppermute(step_logits, "core", swap)
 
     smem = pl.BlockSpec(memory_space=pltpu.SMEM)
     vmem = pl.BlockSpec(memory_space=pltpu.VMEM)
 
-    def call(kernel, scalars, operands, out_shape, scratch, name, cost=None, out_specs=None):
+    anywhere = pl.BlockSpec(memory_space=pl.ANY)
+
+    def call(kernel, scalars, operands, out_shape, scratch, name, cost=None, out_specs=None, in_specs=None, mib=24):
         return pl.pallas_call(
             kernel,
-            in_specs=[smem] * len(scalars) + [vmem] * len(operands),
+            in_specs=[smem] * len(scalars) + (in_specs or [vmem] * len(operands)),
             out_specs=out_specs or [vmem] * len(out_shape),
             out_shape=out_shape,
             scratch_shapes=scratch,
-            compiler_params=pltpu.CompilerParams(vmem_limit_bytes=24 * 2**20),
+            compiler_params=pltpu.CompilerParams(vmem_limit_bytes=mib * 2**20),
             cost_estimate=cost,
             name=name,
         )(*scalars, *operands)
@@ -299,18 +331,43 @@
     where = (place, document_starts)
     spread_scratch = pltpu.VMEM((2 * LANES, WIDE), bf16)
 
+    dma = pltpu.SemaphoreType.DMA
+    packed_width = HALF_WIDE + HALF * STATE + LANES
+    packed, own = call(
+        pack_kernel,
+        (place,),
+        (
+            *(v.reshape(1, PER_GROUP) for v in (step_bias, decay_log, skip_scale)),
+            *(pltpu.with_memory_space_constraint(v, pltpu.HBM) for v in (step_logits, head_inputs, write_keys)),
+        ),
+        [pltpu.VMEM((CHUNK, packed_width), bf16), pltpu.VMEM((SLAB, LANES), f32)],
+        [dma((2 * HALF + 1,))],
+        "pack",
+        in_specs=[vmem] * 3 + [anywhere] * 3,
+    )
+    turns = [own] + [
+        lax.ppermute(own, "z", [((i + turn) % depth, i) for i in range(depth)]) for turn in range(1, HALF)
+    ]
+    packed_got = lax.ppermute(packed, "core", swap)
+
     pay, middle, params, decay = call(
         write_kernel,
         where,
-        (*turns, step_logits, logit_got, head_inputs, x_got, write_keys, b_got),
+        (*turns, step_logits, packed_got, head_inputs, write_keys),
         [
-            shape((SLABS, HALF, SLAB, WIDE + LANES), bf16),
-            shape((STATE, HALF_WIDE), f32),
-            shape((SLAB, LANES), f32),
-            shape((SLAB, LANES), f32),
+            pltpu.HBM((SLABS, HALF, SLAB, WIDE + LANES), bf16),
+            pltpu.HBM((HALF, STATE, WIDE), f32),
+            pltpu.VMEM((SLAB, LANES), f32),
+            pltpu.VMEM((SLAB, LANES), f32),
         ],
-        [spread_scratch],
+        [
+            pltpu.VMEM((HALF, SLABS, SLAB, WIDE + LANES), bf16),
+            pltpu.VMEM((HALF, STATE, WIDE), f32),
+            spread_scratch,
+            dma((2, HALF)),
+        ],
         "write",
+        out_specs=[anywhere] * 2 + [vmem] * 2,
     )
 
     arrived = lax.all_to_all(
@@ -321,11 +378,31 @@
     base, factor = call(
         inside_kernel,
         where,
-        (params, params_got, step_logits, head_inputs, write_keys, read_queries, gate_inputs),
-        [shape((CHUNK, INNER), bf16), shape((CHUNK, INNER), bf16)],
-        [spread_scratch],
+        (
+            params,
+            params_got,
+            head_inputs,
+            *(
+                pltpu.with_memory_space_constraint(v, pltpu.HBM)
+                for v in (step_logits, write_keys, read_queries, gate_inputs)
+            ),
+        ),
+        [pltpu.HBM((GROUPS, CHUNK, WIDE), bf16), pltpu.HBM((GROUPS, CHUNK, WIDE), bf16)],
+        [
+            pltpu.VMEM((CHUNK, LANES), bf16),
+            pltpu.VMEM((CHUNK, GROUPS * STATE), bf16),
+            pltpu.VMEM((CHUNK, GROUPS * STATE), bf16),
+            pltpu.VMEM((CHUNK, INNER), bf16),
+            pltpu.VMEM((GROUPS, CHUNK, WIDE), bf16),
+            pltpu.VMEM((GROUPS, CHUNK, WIDE), bf16),
+            spread_scratch,
+            dma((4,)),
+            dma((2, GROUPS)),
+        ],
         "inside",
         pl.CostEstimate(flops=2 * 4 * CHUNK * STATE * INNER, bytes_accessed=9 * 2**20, transcendentals=2**20),
+        out_specs=[anywhere] * 2,
+        in_specs=[vmem] * 3 + [anywhere] * 4,
     )
     arrived, base, factor = lax.optimization_barrier((arrived, base, factor))
 

time: 94.3 us -> 77.3 us (0.82)
  local copies, waits for them, and re-layouts: 18.8 us -> 2.14 us
  Pallas kernels: 14.9 us -> 19.4 us
  starting transfers between devices: 26.3 us -> 22.1 us
  waiting for transfers between devices: 7.21 us -> 10.4 us
  blocking collectives: 25.6 us -> 22.8 us
    unnamed x54 -> x24, local copies, waits for them, and re-layouts: 14.8 us -> 2.14 us
    ppermute x7 -> x4, starting transfers between devices: 12.9 us -> 7.26 us  [the longest x3 5.78 us: local(): lax.ppermute(own, 'z', [((i + turn) % depth, i) for i in range(depth)])]
    all_to_all x1, waiting for transfers between devices: 1.23 us -> 6.73 us  [local(): lax.all_to_all(pay.reshape(blocks, SLAB, WIDE + LANES), ('ctx', 'z'), 0,...]
    pallas_call x6 -> x7, Pallas kernels: 14.9 us -> 19.4 us  [call(): pl.pallas_call(kernel, in_specs=[smem] * len(scalars) + (in_specs or [vme...]
    dynamic_slice x2 -> x0, local copies, waits for them, and re-layouts: 4 us -> none  [the longest x1 2.44 us: local(): lax.dynamic_slice(head_inputs, (0, (1 - core) * HALF_WIDE), (CHUNK, HALF_...]
    all_to_all x1, blocking collectives: 25.6 us -> 22.8 us  [local(): returned = lax.all_to_all(frozen, ('ctx', 'z'), 0, 0, tiled=True)]
    ppermute x7 -> x4, waiting for transfers between devices: 4.06 us -> 1.73 us  [the longest x3 1.73 us: local(): lax.ppermute(own, 'z', [((i + turn) % depth, i) for i in range(depth)])]
    all_to_all x1, starting transfers between devices: 7.79 us -> 9.33 us  [local(): lax.all_to_all(pay.reshape(blocks, SLAB, WIDE + LANES), ('ctx', 'z'), 0,...]
  transfers between devices with their start and end apart: 10 -> 7, of which waited for: 5 -> 5; matrix products, arithmetic and copies ran while one was open for 2% -> 0% of each run, Pallas kernels for 7% -> 11%
where the time goes in v4:
time: 77.3 us; the launch traced here: 76.9 us
  blocking collectives  22.8 us (29%)
  starting transfers between devices  22.1 us (29%)
  Pallas kernels  19.4 us (25%)
  waiting for transfers between devices  10.4 us (13%)
  local copies, waits for them, and re-layouts  2.14 us (3%)
    all_to_all x1, blocking collectives, local(): returned = lax.all_to_all(frozen, ('ctx', 'z'), 0, 0, tiled=True)  22.8 us
    pallas_call x7, Pallas kernels, call(): pl.pallas_call(kernel, in_specs=[smem] * len(scalars) + (in_specs or [vme...  19.4 us
    all_to_all x1, starting transfers between devices, local(): lax.all_to_all(pay.reshape(blocks, SLAB, WIDE + LANES), ('ctx', 'z'), 0,...  9.33 us
    all_to_all x1, waiting for transfers between devices, local(): lax.all_to_all(pay.reshape(blocks, SLAB, WIDE + LANES), ('ctx', 'z'), 0,...  6.73 us
    ppermute x3, starting transfers between devices, local(): lax.ppermute(own, 'z', [((i + turn) % depth, i) for i in range(depth)])  5.78 us
    ppermute x1, starting transfers between devices, local(): state_got = lax.ppermute(state_sent, 'core', swap)  3.37 us
    unnamed x24, local copies, waits for them, and re-layouts  2.14 us
    ppermute x1, starting transfers between devices, local(): params_got = lax.ppermute(params, 'core', swap)  2.14 us
  transfers between devices with their start and end apart: 7, of which 5 were waited for; matrix products, arithmetic and copies ran while one was open for 0% of the time, Pallas kernels for 11%

profile of v4, /device:TPU:1, one launch (start us, length us, event | category | flops | bytes accessed | tf_op | source)
XLA Modules:
  0.0 76.9 jit_solution(4571196020281435880)
XLA Ops:
  0.0 0.8 %copy-done.9 = f32[16]{0:T(128)S(1)} copy-done((f32[16]{0:T(128)S(1)}, f32[16]{0:T(128)}, u32[]{:S(2)}) %copy-start.9) | copy-done | bytes 88
  0.8 0.7 copy-done.10
  1.5 0.7 copy-done.11
  2.1 1.3 %pack.1 = (bf16[128,4736]{1,0:T(8,128)(2,1)S(1)}, f32[8,128]{1,0:T(8,128)S(1)}) custom-call(s32[1]{0:T(128)} %bitcast.place_ref, f32[1,16]{1,0:T(1,128)S(1)} %bitcast.9, f32[1,16]{1,0:T(1,128)S(1)} %bitcast.10, f32[1,16]{1,0:T(1,128)S(1)} %bitcast.11, bf16[128,128]{1,0:T(8,128)(2,1)} %logit_in.1, bf16[128,8192]{1,0:T(8,128)(2,1)} %x_ref.5, ...), custom_call_target="tpu_custom_call" | custom-call | tf_op jit(solution)/shard_map/pack/pallas_call | solution.py:317
  3.5 1.5 %collective-permute-start.3 = (bf16[128,4736]{1,0:T(8,128)(2,1)S(1)}, bf16[128,4736]{1,0:T(8,128)(2,1)S(1)}, u32[]{:S(2)}, u32[]{:S(2)}) collective-permute-start(bf16[128,4736]{1,0:T(8,128)(2,1)S(1)} %get-tuple-element.21), channel_id=1, source_target_pairs={{0,1},{1,0},{2,3},{3,2},{4,5},{5,4},{6,7},{7,6},{8,9},{9,8},{10,11... | collective-permute-start | bytes 3637256 | tf_op jit(solution)/shard_map/ppermute | solution.py:351
  5.0 1.8 %collective-permute-start.2 = (f32[8,128]{1,0:T(8,128)S(1)}, f32[8,128]{1,0:T(8,128)S(1)}, u32[]{:S(2)}, u32[]{:S(2)}) collective-permute-start(f32[8,128]{1,0:T(8,128)S(1)} %get-tuple-element.20.own0), channel_id=1, source_target_pairs={{6,0},{0,2},{2,4},{4,6},{7,1},{1,3},{3,5},{5,7},{14,8},{8,10},{10,... | collective-permute-start | bytes 12296 | tf_op jit(solution)/shard_map/ppermute | solution.py:349
  6.7 3.3 %collective-permute-start.1 = (f32[8,128]{1,0:T(8,128)S(1)}, f32[8,128]{1,0:T(8,128)S(1)}, u32[]{:S(2)}, u32[]{:S(2)}) collective-permute-start(f32[8,128]{1,0:T(8,128)S(1)} %get-tuple-element.20.own0), channel_id=1, source_target_pairs={{4,0},{6,2},{0,4},{2,6},{5,1},{7,3},{1,5},{3,7},{12,8},{14,10},{8,... | collective-permute-start | bytes 12296 | tf_op jit(solution)/shard_map/ppermute | solution.py:349
  10.0 0.7 collective-permute-start
  10.8 0.0 collective-permute-done.2.own3
  10.8 0.3 collective-permute-done.1.own2
  11.1 1.4 %collective-permute-done.own1 = f32[8,128]{1,0:T(8,128)S(1)} collective-permute-done((f32[8,128]{1,0:T(8,128)S(1)}, f32[8,128]{1,0:T(8,128)S(1)}, u32[]{:S(2)}, u32[]{:S(2)}) %collective-permute-start) | collective-permute-done | bytes 4128 | tf_op jit(solution)/shard_map/ppermute | solution.py:349
  12.5 5.0 %write.1 = (bf16[16,4,8,1152]{3,2,1,0:T(8,128)(2,1)}, f32[4,128,1024]{2,1,0:T(8,128)}, f32[8,128]{1,0:T(8,128)S(1)}, f32[8,128]{1,0:T(8,128)S(1)}) custom-call(s32[1]{0:T(128)} %bitcast.place_ref, s32[4]{0:T(128)S(1)} %copy-done.8, f32[8,128]{1,0:T(8,128)S(1)} %get-tuple-element.20.own0, f32[8,128]{1,0:T(8,128)S(1)} %collective-permute-done.own1, ...), custom_call_target="tpu_custom_call" | custom-call | tf_op jit(solution)/shard_map/write/pallas_call | solution.py:317
  17.5 9.3 %all-to-all-start = ((bf16[64,8,1152]{2,1,0:T(8,128)(2,1)}), bf16[64,8,1152]{2,1,0:T(8,128)(2,1)S(1)}, u32[]{:S(2)}, u32[]{:S(2)}) async-start(bf16[64,8,1152]{2,1,0:T(8,128)(2,1)} %bitcast.12), calls=%async_computation | async-start | bytes 2359296 | tf_op jit(solution)/shard_map/all_to_all | solution.py:373
  26.9 2.1 %collective-permute-start.4 = (f32[8,128]{1,0:T(8,128)S(1)}, f32[8,128]{1,0:T(8,128)S(1)}, u32[]{:S(2)}, u32[]{:S(2)}) collective-permute-start(f32[8,128]{1,0:T(8,128)S(1)} %get-tuple-element.23.params_ref), channel_id=1, source_target_pairs={{0,1},{1,0},{2,3},{3,2},{4,5},{5,4},{6,7},{7,6},{8,9},{9,8},{10,11... | collective-permute-start | bytes 12296 | tf_op jit(solution)/shard_map/ppermute | solution.py:376
  29.0 0.8 %collective-permute-done.4.got_ref = f32[8,128]{1,0:T(8,128)S(1)} collective-permute-done((f32[8,128]{1,0:T(8,128)S(1)}, f32[8,128]{1,0:T(8,128)S(1)}, u32[]{:S(2)}, u32[]{:S(2)}) %collective-permute-start.4) | collective-permute-done | bytes 4128 | tf_op jit(solution)/shard_map/ppermute | solution.py:376
  29.8 7.5 %inside.1 = (bf16[8,128,1024]{2,1,0:T(8,128)(2,1)}, bf16[8,128,1024]{2,1,0:T(8,128)(2,1)}) custom-call(s32[1]{0:T(128)} %bitcast.place_ref, s32[4]{0:T(128)S(1)} %copy-done.8, f32[8,128]{1,0:T(8,128)S(1)} %get-tuple-element.23.params_ref, f32[8,128]{1,0:T(8,128)S(1)} %collective-permute-done.4.got_ref, bf16[128,8192]{1,0:T(8,128)(2,1)S(1)} %copy-done, ...), custom_call_target="tpu_custom_call" | custom-call | flops 1073741824 | bytes 9437184 | tf_op jit(solution)/shard_map/inside/pallas_call | solution.py:317
  37.3 6.7 %all-to-all-done.pay_ref = bf16[64,8,1152]{2,1,0:T(8,128)(2,1)S(1)} async-done(((bf16[64,8,1152]{2,1,0:T(8,128)(2,1)}), bf16[64,8,1152]{2,1,0:T(8,128)(2,1)S(1)}, u32[]{:S(2)}, u32[]{:S(2)}) %all-to-all-start) | async-done | bytes 1179680 | tf_op jit(solution)/shard_map/all_to_all | solution.py:373
  44.0 0.7 scan.1
  44.7 22.8 %all_to_all.10 = bf16[64,8,1024]{2,1,0:T(8,128)(2,1)S(1)} all-to-all(bf16[64,8,1024]{2,1,0:T(8,128)(2,1)S(1)} %scan.1), channel_id=1, replica_groups=mesh['ctx'=16,'z'=4,'core'=2] {'ctx','z'}, dimensions={0} | all-to-all | bytes 2097152 | tf_op jit(solution)/shard_map/all_to_all | solution.py:418
  67.5 0.8 %states.1 = (bf16[128,4096]{1,0:T(8,128)(2,1)S(1)}, bf16[128,4096]{1,0:T(8,128)(2,1)S(1)}) custom-call(s32[1]{0:T(128)} %bitcast.place_ref, bf16[16,4,8,1024]{3,2,1,0:T(8,128)(2,1)S(1)} %bitcast.7, f32[4,128,1024]{2,1,0:T(8,128)S(1)} %copy-done.5, f32[8,128]{1,0:T(8,128)S(1)} %get-tuple-element.30.decay_ref), custom_call_target="tpu_custom_call" | custom-call | tf_op jit(solution)/shard_map/states/pallas_call | solution.py:317
  68.4 3.4 %collective-permute-start.5 = (bf16[128,4096]{1,0:T(8,128)(2,1)S(1)}, bf16[128,4096]{1,0:T(8,128)(2,1)S(1)}, u32[]{:S(2)}, u32[]{:S(2)}) collective-permute-start(bf16[128,4096]{1,0:T(8,128)(2,1)S(1)} %get-tuple-element.31), channel_id=1, source_target_pairs={{0,1},{1,0},{2,3},{3,2},{4,5},{5,4},{6,7},{7,6},{8,9},{9,8},{10,11... | collective-permute-start | bytes 3145736 | tf_op jit(solution)/shard_map/ppermute | solution.py:430
  71.7 1.2 %own.1 = (f32[128,4096]{1,0:T(8,128)S(1)}, f32[128,128]{1,0:T(8,128)S(1)}) custom-call(s32[1]{0:T(128)} %bitcast.place_ref, s32[4]{0:T(128)S(1)} %copy-done.8, bf16[8,128,1024]{2,1,0:T(8,128)(2,1)S(1)} %copy-done.1, bf16[8,128,1024]{2,1,0:T(8,128)(2,1)S(1)} %copy-done.2, bf16[128,1024]{1,0:T(8,128)(2,1)S(1)} %copy-done.3, ...), custom_call_target="tpu_custom_call" | custom-call | flops 268435456 | bytes 5242880 | tf_op jit(solution)/shard_map/own/pallas_call | solution.py:317
  72.9 1.1 %collective-permute-done.5.state_ref = bf16[128,4096]{1,0:T(8,128)(2,1)S(1)} collective-permute-done((bf16[128,4096]{1,0:T(8,128)(2,1)S(1)}, bf16[128,4096]{1,0:T(8,128)(2,1)S(1)}, u32[]{:S(2)}, u32[]{:S(2)}) %collective-permute-start.5) | collective-permute-done | bytes 1048608 | tf_op jit(solution)/shard_map/ppermute | solution.py:430
  74.0 2.9 %last.1 = bf16[128,8192]{1,0:T(8,128)(2,1)} custom-call(s32[1]{0:T(128)} %bitcast.place_ref, s32[4]{0:T(128)S(1)} %copy-done.8, bf16[8,128,1024]{2,1,0:T(8,128)(2,1)S(1)} %copy-done.1, bf16[8,128,1024]{2,1,0:T(8,128)(2,1)S(1)} %copy-done.2, bf16[128,1024]{1,0:T(8,128)(2,1)S(1)} %copy-done.3, bf16[128,4096]{1,0:T(8,128)(2,1)S(1)} %collective-permute-done.5.state_ref, ...), custom_call_target="tpu_custom_call" | custom-call | tf_op jit(solution)/shard_map/last/pallas_call | solution.py:317
  (22 shorter events, 0.0 us)
Async XLA Ops:
  0.0 12.5 %copy-start.6 = (bf16[128,128]{1,0:T(8,128)(2,1)S(1)}, bf16[128,128]{1,0:T(8,128)(2,1)}, u32[]{:S(2)}) copy-start(bf16[128,128]{1,0:T(8,128)(2,1)} %logit_in.1) | copy-start | bytes 98308
  0.0 12.5 %copy-start.4 = (bf16[128,1024]{1,0:T(8,128)(2,1)S(1)}, bf16[128,1024]{1,0:T(8,128)(2,1)}, u32[]{:S(2)}) copy-start(bf16[128,1024]{1,0:T(8,128)(2,1)} %b_in.1) | copy-start | bytes 786436
  0.0 12.5 %copy-start = (bf16[128,8192]{1,0:T(8,128)(2,1)S(1)}, bf16[128,8192]{1,0:T(8,128)(2,1)}, u32[]{:S(2)}) copy-start(bf16[128,8192]{1,0:T(8,128)(2,1)} %x_ref.5) | copy-start | bytes 6291460
  0.0 12.5 %copy-start.8 = (s32[4]{0:T(128)S(1)}, s32[4]{0:T(128)}, u32[]{:S(2)}) copy-start(s32[4]{0:T(128)} %starts_ref.7) | copy-start | bytes 52
  0.0 0.8 %copy-start.9 = (f32[16]{0:T(128)S(1)}, f32[16]{0:T(128)}, u32[]{:S(2)}) copy-start(f32[16]{0:T(128)} %param.15) | copy-start | bytes 196
  0.8 0.7 copy-start.10
  1.5 0.7 copy-start.11
  3.5 9.0 %collective-permute-start.3 = (bf16[128,4736]{1,0:T(8,128)(2,1)S(1)}, bf16[128,4736]{1,0:T(8,128)(2,1)S(1)}, u32[]{:S(2)}, u32[]{:S(2)}) collective-permute-start(bf16[128,4736]{1,0:T(8,128)(2,1)S(1)} %get-tuple-element.21), channel_id=1, source_target_pairs={{0,1},{1,0},{2,3},{3,2},{4,5},{5,4},{6,7},{7,6},{8,9},{9,8},{10,11... | collective-permute-start | bytes 3637256 | tf_op jit(solution)/shard_map/ppermute | solution.py:351
  5.0 5.8 %collective-permute-start.2 = (f32[8,128]{1,0:T(8,128)S(1)}, f32[8,128]{1,0:T(8,128)S(1)}, u32[]{:S(2)}, u32[]{:S(2)}) collective-permute-start(f32[8,128]{1,0:T(8,128)S(1)} %get-tuple-element.20.own0), channel_id=1, source_target_pairs={{6,0},{0,2},{2,4},{4,6},{7,1},{1,3},{3,5},{5,7},{14,8},{8,10},{10,... | collective-permute-start | bytes 12296 | tf_op jit(solution)/shard_map/ppermute | solution.py:349
  6.7 4.3 %collective-permute-start.1 = (f32[8,128]{1,0:T(8,128)S(1)}, f32[8,128]{1,0:T(8,128)S(1)}, u32[]{:S(2)}, u32[]{:S(2)}) collective-permute-start(f32[8,128]{1,0:T(8,128)S(1)} %get-tuple-element.20.own0), channel_id=1, source_target_pairs={{4,0},{6,2},{0,4},{2,6},{5,1},{7,3},{1,5},{3,7},{12,8},{14,10},{8,... | collective-permute-start | bytes 12296 | tf_op jit(solution)/shard_map/ppermute | solution.py:349
  10.0 2.5 %collective-permute-start = (f32[8,128]{1,0:T(8,128)S(1)}, f32[8,128]{1,0:T(8,128)S(1)}, u32[]{:S(2)}, u32[]{:S(2)}) collective-permute-start(f32[8,128]{1,0:T(8,128)S(1)} %get-tuple-element.20.own0), channel_id=1, source_target_pairs={{2,0},{4,2},{6,4},{0,6},{3,1},{5,3},{7,5},{1,7},{10,8},{12,10},{14... | collective-permute-start | bytes 12296 | tf_op jit(solution)/shard_map/ppermute | solution.py:349
  17.5 26.5 %all-to-all-start = ((bf16[64,8,1152]{2,1,0:T(8,128)(2,1)}), bf16[64,8,1152]{2,1,0:T(8,128)(2,1)S(1)}, u32[]{:S(2)}, u32[]{:S(2)}) async-start(bf16[64,8,1152]{2,1,0:T(8,128)(2,1)} %bitcast.12), calls=%async_computation | async-start | bytes 2359296 | tf_op jit(solution)/shard_map/all_to_all | solution.py:373
  26.9 3.0 %collective-permute-start.4 = (f32[8,128]{1,0:T(8,128)S(1)}, f32[8,128]{1,0:T(8,128)S(1)}, u32[]{:S(2)}, u32[]{:S(2)}) collective-permute-start(f32[8,128]{1,0:T(8,128)S(1)} %get-tuple-element.23.params_ref), channel_id=1, source_target_pairs={{0,1},{1,0},{2,3},{3,2},{4,5},{5,4},{6,7},{7,6},{8,9},{9,8},{10,11... | collective-permute-start | bytes 12296 | tf_op jit(solution)/shard_map/ppermute | solution.py:376
  44.0 23.5 %copy-start.5 = (f32[4,128,1024]{2,1,0:T(8,128)S(1)}, f32[4,128,1024]{2,1,0:T(8,128)}, u32[]{:S(2)}) copy-start(f32[4,128,1024]{2,1,0:T(8,128)} %get-tuple-element.29.middle_ref) | copy-start | bytes 6291460
  44.7 27.0 %copy-start.2 = (bf16[8,128,1024]{2,1,0:T(8,128)(2,1)S(1)}, bf16[8,128,1024]{2,1,0:T(8,128)(2,1)}, u32[]{:S(2)}) copy-start(bf16[8,128,1024]{2,1,0:T(8,128)(2,1)} %get-tuple-element.27.factor_ref) | copy-start | bytes 6291460
  67.5 4.2 %copy-start.1 = (bf16[8,128,1024]{2,1,0:T(8,128)(2,1)S(1)}, bf16[8,128,1024]{2,1,0:T(8,128)(2,1)}, u32[]{:S(2)}) copy-start(bf16[8,128,1024]{2,1,0:T(8,128)(2,1)} %get-tuple-element.26.base_ref) | copy-start | bytes 6291460
  67.5 4.2 %copy-start.3 = (bf16[128,1024]{1,0:T(8,128)(2,1)S(1)}, bf16[128,1024]{1,0:T(8,128)(2,1)}, u32[]{:S(2)}) copy-start(bf16[128,1024]{1,0:T(8,128)(2,1)} %c_ref.3) | copy-start | bytes 786436
  68.4 5.7 %collective-permute-start.5 = (bf16[128,4096]{1,0:T(8,128)(2,1)S(1)}, bf16[128,4096]{1,0:T(8,128)(2,1)S(1)}, u32[]{:S(2)}, u32[]{:S(2)}) collective-permute-start(bf16[128,4096]{1,0:T(8,128)(2,1)S(1)} %get-tuple-element.31), channel_id=1, source_target_pairs={{0,1},{1,0},{2,3},{3,2},{4,5},{5,4},{6,7},{7,6},{8,9},{9,8},{10,11... | collective-permute-start | bytes 3145736 | tf_op jit(solution)/shard_map/ppermute | solution.py:430
  71.7 2.3 %copy-start.7 = (f32[8192]{0:T(1024)S(1)}, f32[8192]{0:T(1024)}, u32[]{:S(2)}) copy-start(f32[8192]{0:T(1024)} %param.18) | copy-start | bytes 98308

commit v5 on v4

--- a/solution.py
+++ b/solution.py
@@ -23,6 +23,7 @@
 SLAB = 8
 SLABS = STATE // SLAB
 LANES = 128
+PIECE = 4
 PARTS = 4
 EPS = 1e-5
 
@@ -68,12 +69,14 @@
 
 def cumulated(step, decay):
     rate = -jnp.exp(decay) * step
-    lower = jnp.where(iota((CHUNK, CHUNK), 0) >= iota((CHUNK, CHUNK), 1), 1.0, 0.0).astype(bf16)
-    cum = jnp.zeros(rate.shape, f32)
+    lower = iota((CHUNK, 3 * CHUNK), 0) >= iota((CHUNK, 3 * CHUNK), 1) % CHUNK
+    parts = []
     for _ in range(3):
-        part = rate.astype(bf16)
-        cum = cum + jnp.dot(lower, part, preferred_element_type=f32)
-        rate = rate - part.astype(f32)
+        parts.append(rate.astype(bf16))
+        rate = rate - parts[-1].astype(f32)
+    cum = jnp.dot(
+        jnp.where(lower, 1.0, 0.0).astype(bf16), jnp.concatenate(parts, axis=0), preferred_element_type=f32
+    )
     return jnp.exp(cum), jnp.exp(-cum) * step
 
 
@@ -88,9 +91,18 @@
     return copy
 
 
-def pack_kernel(place_ref, bias_ref, decay_ref, skip_ref, logit_ref, x_ref, b_ref, packed_ref, own_ref, sems):
+def pack_kernel(
+    place_ref, bias_in, decay_in, skip_in, logit_ref, x_ref, b_ref, packed_ref, own_ref, spread_ref,
+    bias_ref, decay_ref, skip_ref, sems, row_sems,
+):
     core = place_ref[0] % CORES
     tail = HALF_WIDE + HALF * STATE
+    rows = [
+        fetch(source, target, row_sems.at[i])
+        for i, (source, target) in enumerate(
+            ((bias_in, bias_ref), (decay_in, decay_ref), (skip_in, skip_ref))
+        )
+    ]
     copies = [fetch(logit_ref, packed_ref.at[:, pl.ds(tail, LANES)], sems.at[2 * HALF])]
     for group in range(HALF):
         to_x, to_key = pl.ds(group * WIDE, WIDE), pl.ds(HALF_WIDE + group * STATE, STATE)
@@ -98,42 +110,42 @@
         copies.append(
             fetch(b_ref.at[:, columns_of(group, 1 - core, STATE)], packed_ref.at[:, to_key], sems.at[HALF + group])
         )
+    spread_ref[...] = spreader(2 * LANES, 1)
     own_ref[...] = jnp.zeros_like(own_ref)
     for i, ref in enumerate((bias_ref, decay_ref, skip_ref)):
+        rows[i].wait()
         own_ref[i : i + 1, :PER_GROUP] = ref[...]
     for copy in copies:
         copy.wait()
 
 
 def write_kernel(
-    place_ref, starts_ref, own0, own1, own2, own3, logit_ref, got_ref, x_ref, b_ref,
-    pay_out, middle_out, params_ref, decay_ref, pay_ref, middle_ref, spread_ref, sems,
+    place_ref, starts_ref, own0, own1, own2, own3, spread_ref, logit_ref, got_ref, x_ref, b_ref,
+    pay_out, middle_out, params_ref, pay_ref, middle_ref, sems,
 ):
     place = place_ref[0]
     core = place % CORES
     tail = HALF_WIDE + HALF * STATE
-    spread_ref[...] = spreader(2 * LANES, 1)
     lane = iota((SLAB, LANES), 1)
     params = jnp.zeros((SLAB, LANES), f32)
     for turn, ref in enumerate((own0, own1, own2, own3)):
         some = jnp.where(lane < PER_GROUP, ref[...], 0.0)
         params = params + from_front(some, 2 * ((place // CORES + turn) % HALF) + core)
     params_ref[...] = params
-    half = iota((CHUNK, LANES), 1) // PER_GROUP % CORES == core
-    chunks = []
-    for logit, of_core in ((logit_ref[...], core), (got_ref[:, tail:], 1 - core)):
-        step = jnp.where(half, softplus(logit.astype(f32) + params[0:1]), 0.0)
-        p, q = cumulated(step, params[1:2])
-        start = chunk_start(place, starts_ref, of_core)
-        last = jnp.broadcast_to(p[CHUNK - 1 : CHUNK, :], (SLAB, LANES))
-        kept = (iota((CHUNK, STATE), 0) >= start) | (start >= CHUNK)
-        chunks.append((q, last, jnp.where(start >= CHUNK, last, 0.0), kept))
-    whole = chunks[0][2] * chunks[1][2]
+    logit = jnp.concatenate([logit_ref[...].astype(f32), got_ref[:, tail:].astype(f32)], axis=1)
+    half = iota((CHUNK, 2 * LANES), 1) // PER_GROUP % CORES == core
+    both = jnp.concatenate([params, params], axis=1)
+    step = jnp.where(half, softplus(logit + both[0:1]), 0.0)
+    p, q = cumulated(step, both[1:2])
+    last = jnp.broadcast_to(p[CHUNK - 1 : CHUNK], (SLAB, 2 * LANES))
+    rows = jnp.concatenate([q[:, :LANES], q[:, LANES:], last[:, :LANES], last[:, LANES:]], axis=0)
+    starts = (chunk_start(place, starts_ref, core), chunk_start(place, starts_ref, 1 - core))
+    open_ = (starts[0] >= CHUNK, starts[1] >= CHUNK)
+    kept = [(iota((CHUNK, STATE), 0) >= start) | (start >= CHUNK) for start in starts]
+    whole = jnp.where(open_[0] & open_[1], last[:, :LANES] * last[:, LANES:], 0.0)
     high = whole.astype(bf16).astype(f32)
     middle = (whole - high).astype(bf16).astype(f32)
     low = whole - high - middle
-    second_decay = jnp.where(core == 0, chunks[1][2], chunks[0][2])
-    decay_ref[...] = jnp.where(core == 0, chunks[0][2], chunks[1][2])
 
     sent = []
     for j in range(HALF):
@@ -142,15 +154,19 @@
         at = HALF_WIDE + j * STATE
         xs = (x_ref[:, columns_of(j, core, WIDE)], got_ref[:, columns])
         keys = (b_ref[:, columns_of(j, core, STATE)], got_ref[:, at : at + STATE])
+        wide = spread(rows, group, spread_ref)
+        lasts = (wide[2 * CHUNK : 2 * CHUNK + SLAB], wide[2 * CHUNK + SLAB :])
         written = []
-        for (q, last, _, kept), x, b in zip(chunks, xs, keys):
-            xq = (x.astype(f32) * spread(q, group, spread_ref)).astype(bf16)
-            b = jnp.where(kept, b.astype(f32), 0.0).astype(bf16)
+        for i in range(2):
+            xq = (xs[i].astype(f32) * wide[i * CHUNK : (i + 1) * CHUNK]).astype(bf16)
+            b = jnp.where(kept[i], keys[i].astype(f32), 0.0).astype(bf16)
             w = lax.dot_general(b, xq, (((0,), (0,)), ((), ())), preferred_element_type=f32)
-            written.append(w.reshape(SLABS, SLAB, WIDE) * spread(last, group, spread_ref)[None])
+            written.append(w.reshape(SLABS, SLAB, WIDE) * lasts[i][None])
+        decays = [jnp.where(open_[i], lasts[i], 0.0) for i in range(2)]
+        second = jnp.where(core == 0, decays[1], decays[0])
         before = jnp.where(core == 0, written[0], written[1])
         after = jnp.where(core == 0, written[1], written[0])
-        pay_ref[j, :, :, :WIDE] = (before * spread(second_decay, group, spread_ref)[None] + after).astype(bf16)
+        pay_ref[j, :, :, :WIDE] = (before * second[None] + after).astype(bf16)
         packed = jnp.where(
             lane < PER_GROUP,
             to_front(high, group),
@@ -162,7 +178,8 @@
         ).astype(bf16)
         pay_ref[j, :, :, WIDE:] = jnp.broadcast_to(packed[None], (SLABS, SLAB, LANES))
         sent.append(fetch(pay_ref.at[j], pay_out.at[:, j], sems.at[0, j]))
-        middle_ref[j] = before.reshape(STATE, WIDE)
+        middle_ref[j, :STATE] = before.reshape(STATE, WIDE)
+        middle_ref[j, STATE:] = jnp.where(core == 0, decays[0], decays[1])
         sent.append(fetch(middle_ref.at[j], middle_out.at[j], sems.at[1, j]))
     for copy in sent:
         copy.wait()
@@ -193,10 +210,10 @@
     gate_copy = fetch(gate_in, gate_ref, sems.at[3])
     spread_ref[...] = spreader(2 * LANES, 1)
     params = params_ref[...] + got_ref[...]
-    skips = jnp.broadcast_to(params[2:3], (SLAB, LANES))
     logit_copy.wait()
     step = softplus(logit_ref[...].astype(f32) + params[0:1])
     p, q = cumulated(step, params[1:2])
+    rows = jnp.concatenate([q, p, jnp.broadcast_to(params[2:3], (2 * SLAB, LANES))], axis=0)
     t = iota((CHUNK, CHUNK), 0)
     s = iota((CHUNK, CHUNK), 1)
     allowed = (s <= t) & ((t >= start) == (s >= start))
@@ -207,17 +224,18 @@
     for group in range(GROUPS):
         columns = slice(group * WIDE, (group + 1) * WIDE)
         states = slice(group * STATE, (group + 1) * STATE)
+        wide = spread(rows, group, spread_ref)
+        grown = wide[CHUNK : 2 * CHUNK]
         x = x_ref[:, columns].astype(f32)
-        xq = (x * spread(q, group, spread_ref)).astype(bf16)
+        xq = (x * wide[:CHUNK]).astype(bf16)
         score = lax.dot_general(
             c_ref[:, states], b_ref[:, states], (((1,), (1,)), ((), ())), preferred_element_type=f32
         )
         mixing = jnp.where(allowed, score, 0.0).astype(bf16)
         inside = jnp.dot(mixing, xq, preferred_element_type=f32)
-        skip = spread(skips, group, spread_ref)[:1]
+        skip = wide[2 * CHUNK : 2 * CHUNK + 1]
         gate = gate_ref[:, columns].astype(f32)
         silu = gate / (1.0 + jnp.exp(-gate))
-        grown = spread(p, group, spread_ref)
         base_ref[group] = ((inside * grown + skip * x) * silu).astype(bf16)
         factor_ref[group] = (grown * silu).astype(bf16)
         sent.append(fetch(base_ref.at[group], base_out.at[group], sent_sems.at[0, group]))
@@ -226,53 +244,55 @@
         copy.wait()
 
 
-def states_kernel(place_ref, state_ref, middle_ref, decay_ref, own_ref, sent_ref, spread_ref):
+def states_kernel(first_group, place_ref, state_ref, middle_ref, own_ref, sent_ref):
     core = place_ref[0] % CORES
-    spread_ref[...] = spreader(2 * LANES, 1)
-    for group in range(HALF):
-        columns = slice(group * WIDE, (group + 1) * WIDE)
+    for i in range(PIECE):
+        group = first_group + i
         block = state_ref[:, group].astype(f32)
-        decay = spread(decay_ref[...], 2 * group + core, spread_ref)
         first = block.reshape(STATE, WIDE)
-        second = (block * decay[None]).reshape(STATE, WIDE) + middle_ref[group]
-        own_ref[:, columns] = jnp.where(core == 0, first, second).astype(bf16)
-        sent_ref[:, columns] = jnp.where(core == 0, second, first).astype(bf16)
-
-
-def gated_part(place, starts_ref, half, base_ref, factor_ref, c_ref, state_ref, gated_ref, power):
+        second = (block * middle_ref[group, STATE:][None]).reshape(STATE, WIDE) + middle_ref[group, :STATE]
+        own_ref[i] = jnp.where(core == 0, first, second).astype(bf16)
+        sent_ref[i] = jnp.where(core == 0, second, first).astype(bf16)
+
+
+def gated_part(place, starts_ref, half, first_group, base_ref, factor_ref, c_ref, state_ref, gated_ref, power):
     start = chunk_start(place, starts_ref, place % CORES)
     seen = iota((CHUNK, STATE), 0) < start
-    for group in range(HALF):
+    for i in range(PIECE):
+        group = first_group + i
         of_all = CORES * group + half
-        states = columns_of(group, half, STATE)
-        queries = jnp.where(seen, c_ref[:, states].astype(f32), 0.0).astype(bf16)
-        here = slice(group * WIDE, (group + 1) * WIDE)
-        outside = jnp.dot(queries, state_ref[:, here], preferred_element_type=f32)
+        queries = jnp.where(seen, c_ref[:, columns_of(group, half, STATE)].astype(f32), 0.0).astype(bf16)
+        outside = jnp.dot(queries, state_ref[i], preferred_element_type=f32)
         gated = base_ref[of_all].astype(f32) + outside * factor_ref[of_all].astype(f32)
-        gated_ref[:, here] = gated
+        gated_ref[group] = gated
         squares = gated * gated
-        for i in range(WIDE // LANES):
-            power = power + squares[:, i * LANES : (i + 1) * LANES]
+        for k in range(WIDE // LANES):
+            power = power + squares[:, k * LANES : (k + 1) * LANES]
     return power
 
 
-def own_kernel(place_ref, starts_ref, base_ref, factor_ref, c_ref, state_ref, gated_ref, power_ref):
+def own_kernel(place_ref, starts_ref, base_ref, factor_ref, c_ref, *refs):
+    *states, gated_ref, power_ref = refs
     place = place_ref[0]
-    power_ref[...] = gated_part(
-        place, starts_ref, place % CORES, base_ref, factor_ref, c_ref, state_ref, gated_ref,
-        jnp.zeros((CHUNK, LANES), f32),
-    )
+    power = jnp.zeros((CHUNK, LANES), f32)
+    for i, state_ref in enumerate(states):
+        power = gated_part(
+            place, starts_ref, place % CORES, i * PIECE, base_ref, factor_ref, c_ref, state_ref, gated_ref, power
+        )
+    power_ref[...] = power
 
 
 def last_kernel(
-    place_ref, starts_ref, base_ref, factor_ref, c_ref, state_ref, gated_own_ref, power_own_ref, gain_ref,
-    out_ref, gated_ref, done_ref, sems,
+    place_ref, starts_ref, base_ref, factor_ref, c_ref, *refs
 ):
+    *states, gated_own_ref, power_own_ref, gain_ref, out_ref, gated_ref, done_ref, sems = refs
     place = place_ref[0]
     core = place % CORES
-    power = gated_part(
-        place, starts_ref, 1 - core, base_ref, factor_ref, c_ref, state_ref, gated_ref, power_own_ref[...]
-    )
+    power = power_own_ref[...]
+    for i, state_ref in enumerate(states):
+        power = gated_part(
+            place, starts_ref, 1 - core, i * PIECE, base_ref, factor_ref, c_ref, state_ref, gated_ref, power
+        )
     total = jnp.sum(power, axis=1, keepdims=True)
     scale = lax.rsqrt(total * (1.0 / INNER) + EPS)
     rows = CHUNK // PARTS
@@ -282,10 +302,9 @@
         for half, ref in ((core, gated_own_ref), (1 - core, gated_ref)):
             for group in range(HALF):
                 columns = columns_of(group, half, WIDE)
-                gated = ref[some, group * WIDE : (group + 1) * WIDE]
+                gated = ref[group, some]
                 done_ref[some, columns] = (gated * scale[some] * gain_ref[:, columns]).astype(bf16)
-        copies.append(pltpu.make_async_copy(done_ref.at[some], out_ref.at[some], sems.at[part]))
-        copies[-1].start()
+        copies.append(fetch(done_ref.at[some], out_ref.at[some], sems.at[part]))
     for copy in copies:
         copy.wait()
 
@@ -333,41 +352,50 @@
 
     dma = pltpu.SemaphoreType.DMA
     packed_width = HALF_WIDE + HALF * STATE + LANES
-    packed, own = call(
+    packed, own, spread_matrix = call(
         pack_kernel,
         (place,),
         (
-            *(v.reshape(1, PER_GROUP) for v in (step_bias, decay_log, skip_scale)),
-            *(pltpu.with_memory_space_constraint(v, pltpu.HBM) for v in (step_logits, head_inputs, write_keys)),
+            *(
+                pltpu.with_memory_space_constraint(v, pltpu.HBM)
+                for v in (
+                    *(v.reshape(1, PER_GROUP) for v in (step_bias, decay_log, skip_scale)),
+                    step_logits,
+                    head_inputs,
+                    write_keys,
+                )
+            ),
         ),
-        [pltpu.VMEM((CHUNK, packed_width), bf16), pltpu.VMEM((SLAB, LANES), f32)],
-        [dma((2 * HALF + 1,))],
+        [
+            pltpu.VMEM((CHUNK, packed_width), bf16),
+            pltpu.VMEM((SLAB, LANES), f32),
+            pltpu.VMEM((2 * LANES, WIDE), bf16),
+        ],
+        [pltpu.VMEM((1, PER_GROUP), f32)] * 3 + [dma((2 * HALF + 1,)), dma((3,))],
         "pack",
-        in_specs=[vmem] * 3 + [anywhere] * 3,
+        in_specs=[anywhere] * 6,
     )
     turns = [own] + [
         lax.ppermute(own, "z", [((i + turn) % depth, i) for i in range(depth)]) for turn in range(1, HALF)
     ]
     packed_got = lax.ppermute(packed, "core", swap)
 
-    pay, middle, params, decay = call(
+    pay, middle, params = call(
         write_kernel,
         where,
-        (*turns, step_logits, packed_got, head_inputs, write_keys),
+        (*turns, spread_matrix, step_logits, packed_got, head_inputs, write_keys),
         [
             pltpu.HBM((SLABS, HALF, SLAB, WIDE + LANES), bf16),
-            pltpu.HBM((HALF, STATE, WIDE), f32),
-            pltpu.VMEM((SLAB, LANES), f32),
+            pltpu.HBM((HALF, STATE + SLAB, WIDE), f32),
             pltpu.VMEM((SLAB, LANES), f32),
         ],
         [
             pltpu.VMEM((HALF, SLABS, SLAB, WIDE + LANES), bf16),
-            pltpu.VMEM((HALF, STATE, WIDE), f32),
-            spread_scratch,
+            pltpu.VMEM((HALF, STATE + SLAB, WIDE), f32),
             dma((2, HALF)),
         ],
         "write",
-        out_specs=[anywhere] * 2 + [vmem] * 2,
+        out_specs=[anywhere] * 2 + [vmem],
     )
 
     arrived = lax.all_to_all(
@@ -417,23 +445,26 @@
 
     returned = lax.all_to_all(frozen, ("ctx", "z"), 0, 0, tiled=True)
 
-    half_state = shape((STATE, HALF_WIDE), bf16)
-    state_own, state_sent = call(
-        states_kernel,
-        (place,),
-        (returned.reshape(SLABS, HALF, SLAB, WIDE), middle, decay),
-        [half_state, half_state],
-        [spread_scratch],
-        "states",
-    )
-
-    state_got = lax.ppermute(state_sent, "core", swap)
+    piece_state = shape((PIECE, STATE, WIDE), bf16)
+    states_own, states_sent = [], []
+    for first_group in range(0, HALF, PIECE):
+        one, other = call(
+            functools.partial(states_kernel, first_group),
+            (place,),
+            (returned.reshape(SLABS, HALF, SLAB, WIDE), middle),
+            [piece_state, piece_state],
+            [],
+            "states",
+        )
+        states_own.append(one)
+        states_sent.append(other)
+    states_got = [lax.ppermute(v, "core", swap) for v in states_sent]
 
     gated, power = call(
         own_kernel,
         where,
-        (base, factor, read_queries, state_own),
-        [shape((CHUNK, HALF_WIDE), f32), shape((CHUNK, LANES), f32)],
+        (base, factor, read_queries, *states_own),
+        [shape((HALF, CHUNK, WIDE), f32), shape((CHUNK, LANES), f32)],
         [],
         "own",
         pl.CostEstimate(flops=2 * CHUNK * STATE * INNER, bytes_accessed=5 * 2**20, transcendentals=0),
@@ -442,15 +473,15 @@
     [out] = call(
         last_kernel,
         where,
-        (base, factor, read_queries, state_got, gated, power, norm_gain.reshape(1, INNER)),
+        (base, factor, read_queries, *states_got, gated, power, norm_gain.reshape(1, INNER)),
         [shape((CHUNK, INNER), bf16)],
         [
-            pltpu.VMEM((CHUNK, HALF_WIDE), f32),
+            pltpu.VMEM((HALF, CHUNK, WIDE), f32),
             pltpu.VMEM((CHUNK, INNER), bf16),
-            pltpu.SemaphoreType.DMA((PARTS,)),
+            dma((PARTS,)),
         ],
         "last",
-        out_specs=[pl.BlockSpec(memory_space=pl.ANY)],
+        out_specs=[anywhere],
     )
     return out
 

time: 77.3 us -> 73.6 us (0.952)
  local copies, waits for them, and re-layouts: 2.14 us -> 0.03 us
  Pallas kernels: 19.4 us -> 17.4 us
    unnamed x24 -> x18, local copies, waits for them, and re-layouts: 2.14 us -> 0.03 us
    pallas_call x7, Pallas kernels: 19.4 us -> 17.4 us  [call(): pl.pallas_call(kernel, in_specs=[smem] * len(scalars) + (in_specs or [vme...]
where the time goes in v5:
time: 73.6 us; the launch traced here: 73.3 us
  blocking collectives  22.8 us (31%)
  starting transfers between devices  22.1 us (30%)
  Pallas kernels  17.4 us (24%)
  waiting for transfers between devices  10.9 us (15%)
    all_to_all x1, blocking collectives, local(): returned = lax.all_to_all(frozen, ('ctx', 'z'), 0, 0, tiled=True)  22.8 us
    pallas_call x7, Pallas kernels, call(): pl.pallas_call(kernel, in_specs=[smem] * len(scalars) + (in_specs or [vme...  17.4 us
    all_to_all x1, starting transfers between devices, local(): lax.all_to_all(pay.reshape(blocks, SLAB, WIDE + LANES), ('ctx', 'z'), 0,...  9.33 us
    all_to_all x1, waiting for transfers between devices, local(): lax.all_to_all(pay.reshape(blocks, SLAB, WIDE + LANES), ('ctx', 'z'), 0,...  7.28 us
    ppermute x3, starting transfers between devices, local(): lax.ppermute(own, 'z', [((i + turn) % depth, i) for i in range(depth)])  5.78 us
    ppermute x1, starting transfers between devices, local(): states_got = [lax.ppermute(v, 'core', swap) for v in states_sent]  3.37 us
    ppermute x1, starting transfers between devices, local(): params_got = lax.ppermute(params, 'core', swap)  2.14 us
    ppermute x3, waiting for transfers between devices, local(): lax.ppermute(own, 'z', [((i + turn) % depth, i) for i in range(depth)])  1.73 us
  transfers between devices with their start and end apart: 7, of which 5 were waited for; matrix products, arithmetic and copies ran while one was open for 0% of the time, Pallas kernels for 11%

profile of v5, /device:TPU:1, one launch (start us, length us, event | category | flops | bytes accessed | tf_op | source)
XLA Modules:
  0.0 73.3 jit_solution(6034263153411718482)
XLA Ops:
  0.0 0.0 copy-start.8
  0.0 1.5 %pack.1 = (bf16[128,4736]{1,0:T(8,128)(2,1)S(1)}, f32[8,128]{1,0:T(8,128)S(1)}, bf16[256,1024]{1,0:T(8,128)(2,1)S(1)}) custom-call(s32[1]{0:T(128)} %bitcast.place_ref, f32[1,16]{1,0:T(1,128)} %bitcast.10, f32[1,16]{1,0:T(1,128)} %bitcast.11, f32[1,16]{1,0:T(1,128)} %bitcast.12, bf16[128,128]{1,0:T(8,128)(2,1)} %logit_in.1, bf16[128,8192]{1,0:T(8,128)(2,1)} %x_ref.5, ...), custom_call_target="tpu_custom_call" | custom-call | tf_op jit(solution)/shard_map/pack/pallas_call | solution.py:336
  1.6 1.5 %collective-permute-start.3 = (bf16[128,4736]{1,0:T(8,128)(2,1)S(1)}, bf16[128,4736]{1,0:T(8,128)(2,1)S(1)}, u32[]{:S(2)}, u32[]{:S(2)}) collective-permute-start(bf16[128,4736]{1,0:T(8,128)(2,1)S(1)} %get-tuple-element.22), channel_id=1, source_target_pairs={{0,1},{1,0},{2,3},{3,2},{4,5},{5,4},{6,7},{7,6},{8,9},{9,8},{10,11... | collective-permute-start | bytes 3637256 | tf_op jit(solution)/shard_map/ppermute | solution.py:381
  3.1 1.8 %collective-permute-start.2 = (f32[8,128]{1,0:T(8,128)S(1)}, f32[8,128]{1,0:T(8,128)S(1)}, u32[]{:S(2)}, u32[]{:S(2)}) collective-permute-start(f32[8,128]{1,0:T(8,128)S(1)} %get-tuple-element.20.own0), channel_id=1, source_target_pairs={{6,0},{0,2},{2,4},{4,6},{7,1},{1,3},{3,5},{5,7},{14,8},{8,10},{10,... | collective-permute-start | bytes 12296 | tf_op jit(solution)/shard_map/ppermute | solution.py:379
  4.8 3.3 %collective-permute-start.1 = (f32[8,128]{1,0:T(8,128)S(1)}, f32[8,128]{1,0:T(8,128)S(1)}, u32[]{:S(2)}, u32[]{:S(2)}) collective-permute-start(f32[8,128]{1,0:T(8,128)S(1)} %get-tuple-element.20.own0), channel_id=1, source_target_pairs={{4,0},{6,2},{0,4},{2,6},{5,1},{7,3},{1,5},{3,7},{12,8},{14,10},{8,... | collective-permute-start | bytes 12296 | tf_op jit(solution)/shard_map/ppermute | solution.py:379
  8.1 0.7 collective-permute-start
  8.8 0.0 collective-permute-done.2.own3
  8.8 0.3 collective-permute-done.1.own2
  9.2 1.4 %collective-permute-done.own1 = f32[8,128]{1,0:T(8,128)S(1)} collective-permute-done((f32[8,128]{1,0:T(8,128)S(1)}, f32[8,128]{1,0:T(8,128)S(1)}, u32[]{:S(2)}, u32[]{:S(2)}) %collective-permute-start) | collective-permute-done | bytes 4128 | tf_op jit(solution)/shard_map/ppermute | solution.py:379
  10.6 0.0 collective-permute-done.3.got_ref
  10.6 0.0 copy-done
  10.6 3.6 %write.1 = (bf16[16,4,8,1152]{3,2,1,0:T(8,128)(2,1)}, f32[4,136,1024]{2,1,0:T(8,128)}, f32[8,128]{1,0:T(8,128)S(1)}) custom-call(s32[1]{0:T(128)} %bitcast.place_ref, s32[4]{0:T(128)S(1)} %copy-done.8, f32[8,128]{1,0:T(8,128)S(1)} %get-tuple-element.20.own0, f32[8,128]{1,0:T(8,128)S(1)} %collective-permute-done.own1, ...), custom_call_target="tpu_custom_call" | custom-call | tf_op jit(solution)/shard_map/write/pallas_call | solution.py:336
  14.3 9.3 %all-to-all-start = ((bf16[64,8,1152]{2,1,0:T(8,128)(2,1)}), bf16[64,8,1152]{2,1,0:T(8,128)(2,1)S(1)}, u32[]{:S(2)}, u32[]{:S(2)}) async-start(bf16[64,8,1152]{2,1,0:T(8,128)(2,1)} %bitcast.9), calls=%async_computation | async-start | bytes 2359296 | tf_op jit(solution)/shard_map/all_to_all | solution.py:401
  23.6 2.1 %collective-permute-start.4 = (f32[8,128]{1,0:T(8,128)S(1)}, f32[8,128]{1,0:T(8,128)S(1)}, u32[]{:S(2)}, u32[]{:S(2)}) collective-permute-start(f32[8,128]{1,0:T(8,128)S(1)} %get-tuple-element.24.params_ref), channel_id=1, source_target_pairs={{0,1},{1,0},{2,3},{3,2},{4,5},{5,4},{6,7},{7,6},{8,9},{9,8},{10,11... | collective-permute-start | bytes 12296 | tf_op jit(solution)/shard_map/ppermute | solution.py:404
  25.7 0.8 %collective-permute-done.4.got_ref = f32[8,128]{1,0:T(8,128)S(1)} collective-permute-done((f32[8,128]{1,0:T(8,128)S(1)}, f32[8,128]{1,0:T(8,128)S(1)}, u32[]{:S(2)}, u32[]{:S(2)}) %collective-permute-start.4) | collective-permute-done | bytes 4128 | tf_op jit(solution)/shard_map/ppermute | solution.py:404
  26.5 6.9 %inside.1 = (bf16[8,128,1024]{2,1,0:T(8,128)(2,1)}, bf16[8,128,1024]{2,1,0:T(8,128)(2,1)}) custom-call(s32[1]{0:T(128)} %bitcast.place_ref, s32[4]{0:T(128)S(1)} %copy-done.8, f32[8,128]{1,0:T(8,128)S(1)} %get-tuple-element.24.params_ref, f32[8,128]{1,0:T(8,128)S(1)} %collective-permute-done.4.got_ref, bf16[128,8192]{1,0:T(8,128)(2,1)S(1)} %copy-done, ...), custom_call_target="tpu_custom_call" | custom-call | flops 1073741824 | bytes 9437184 | tf_op jit(solution)/shard_map/inside/pallas_call | solution.py:336
  33.5 7.3 %all-to-all-done.pay_ref = bf16[64,8,1152]{2,1,0:T(8,128)(2,1)S(1)} async-done(((bf16[64,8,1152]{2,1,0:T(8,128)(2,1)}), bf16[64,8,1152]{2,1,0:T(8,128)(2,1)S(1)}, u32[]{:S(2)}, u32[]{:S(2)}) %all-to-all-start) | async-done | bytes 1179680 | tf_op jit(solution)/shard_map/all_to_all | solution.py:401
  40.8 0.7 scan.1
  41.5 22.8 %all_to_all.10 = bf16[64,8,1024]{2,1,0:T(8,128)(2,1)S(1)} all-to-all(bf16[64,8,1024]{2,1,0:T(8,128)(2,1)S(1)} %scan.1), channel_id=1, replica_groups=mesh['ctx'=16,'z'=4,'core'=2] {'ctx','z'}, dimensions={0} | all-to-all | bytes 2097152 | tf_op jit(solution)/shard_map/all_to_all | solution.py:446
  64.3 0.5 states.1
  64.8 3.4 %collective-permute-start.5 = (bf16[4,128,1024]{2,1,0:T(8,128)(2,1)S(1)}, bf16[4,128,1024]{2,1,0:T(8,128)(2,1)S(1)}, u32[]{:S(2)}, u32[]{:S(2)}) collective-permute-start(bf16[4,128,1024]{2,1,0:T(8,128)(2,1)S(1)} %get-tuple-element.31), channel_id=1, source_target_pairs={{0,1},{1,0},{2,3},{3,2},{4,5},{5,4},{6,7},{7,6},{8,9},{9,8},{10,11... | collective-permute-start | bytes 3145736 | tf_op jit(solution)/shard_map/ppermute | solution.py:461
  68.1 1.2 %own.1 = (f32[4,128,1024]{2,1,0:T(8,128)S(1)}, f32[128,128]{1,0:T(8,128)S(1)}) custom-call(s32[1]{0:T(128)} %bitcast.place_ref, s32[4]{0:T(128)S(1)} %copy-done.8, bf16[8,128,1024]{2,1,0:T(8,128)(2,1)S(1)} %copy-done.1, bf16[8,128,1024]{2,1,0:T(8,128)(2,1)S(1)} %copy-done.2, bf16[128,1024]{1,0:T(8,128)(2,1)S(1)} %copy-done.3, ...), custom_call_target="tpu_custom_call" | custom-call | flops 268435456 | bytes 5242880 | tf_op jit(solution)/shard_map/own/pallas_call | solution.py:336
  69.3 1.1 %collective-permute-done.5.refs_0_ = bf16[4,128,1024]{2,1,0:T(8,128)(2,1)S(1)} collective-permute-done((bf16[4,128,1024]{2,1,0:T(8,128)(2,1)S(1)}, bf16[4,128,1024]{2,1,0:T(8,128)(2,1)S(1)}, u32[]{:S(2)}, u32[]{:S(2)}) %collective-permute-start.5) | collective-permute-done | bytes 1048608 | tf_op jit(solution)/shard_map/ppermute | solution.py:461
  70.4 2.9 %last.1 = bf16[128,8192]{1,0:T(8,128)(2,1)} custom-call(s32[1]{0:T(128)} %bitcast.place_ref, s32[4]{0:T(128)S(1)} %copy-done.8, bf16[8,128,1024]{2,1,0:T(8,128)(2,1)S(1)} %copy-done.1, bf16[8,128,1024]{2,1,0:T(8,128)(2,1)S(1)} %copy-done.2, bf16[128,1024]{1,0:T(8,128)(2,1)S(1)} %copy-done.3, bf16[4,128,1024]{2,1,0:T(8,128)(2,1)S(1)} %collective-permute-done.5.refs_0_, ...), custom_call_target="tpu_custom_call" | custom-call | tf_op jit(solution)/shard_map/last/pallas_call | solution.py:336
  (16 shorter events, 0.0 us)
Async XLA Ops:
  0.0 10.6 %copy-start.6 = (bf16[128,128]{1,0:T(8,128)(2,1)S(1)}, bf16[128,128]{1,0:T(8,128)(2,1)}, u32[]{:S(2)}) copy-start(bf16[128,128]{1,0:T(8,128)(2,1)} %logit_in.1) | copy-start | bytes 98308
  0.0 10.6 %copy-start.4 = (bf16[128,1024]{1,0:T(8,128)(2,1)S(1)}, bf16[128,1024]{1,0:T(8,128)(2,1)}, u32[]{:S(2)}) copy-start(bf16[128,1024]{1,0:T(8,128)(2,1)} %b_in.1) | copy-start | bytes 786436
  0.0 10.6 %copy-start = (bf16[128,8192]{1,0:T(8,128)(2,1)S(1)}, bf16[128,8192]{1,0:T(8,128)(2,1)}, u32[]{:S(2)}) copy-start(bf16[128,8192]{1,0:T(8,128)(2,1)} %x_ref.5) | copy-start | bytes 6291460
  0.0 10.6 %copy-start.8 = (s32[4]{0:T(128)S(1)}, s32[4]{0:T(128)}, u32[]{:S(2)}) copy-start(s32[4]{0:T(128)} %starts_ref.7) | copy-start | bytes 52
  1.6 9.0 %collective-permute-start.3 = (bf16[128,4736]{1,0:T(8,128)(2,1)S(1)}, bf16[128,4736]{1,0:T(8,128)(2,1)S(1)}, u32[]{:S(2)}, u32[]{:S(2)}) collective-permute-start(bf16[128,4736]{1,0:T(8,128)(2,1)S(1)} %get-tuple-element.22), channel_id=1, source_target_pairs={{0,1},{1,0},{2,3},{3,2},{4,5},{5,4},{6,7},{7,6},{8,9},{9,8},{10,11... | collective-permute-start | bytes 3637256 | tf_op jit(solution)/shard_map/ppermute | solution.py:381
  3.1 5.8 %collective-permute-start.2 = (f32[8,128]{1,0:T(8,128)S(1)}, f32[8,128]{1,0:T(8,128)S(1)}, u32[]{:S(2)}, u32[]{:S(2)}) collective-permute-start(f32[8,128]{1,0:T(8,128)S(1)} %get-tuple-element.20.own0), channel_id=1, source_target_pairs={{6,0},{0,2},{2,4},{4,6},{7,1},{1,3},{3,5},{5,7},{14,8},{8,10},{10,... | collective-permute-start | bytes 12296 | tf_op jit(solution)/shard_map/ppermute | solution.py:379
  4.8 4.3 %collective-permute-start.1 = (f32[8,128]{1,0:T(8,128)S(1)}, f32[8,128]{1,0:T(8,128)S(1)}, u32[]{:S(2)}, u32[]{:S(2)}) collective-permute-start(f32[8,128]{1,0:T(8,128)S(1)} %get-tuple-element.20.own0), channel_id=1, source_target_pairs={{4,0},{6,2},{0,4},{2,6},{5,1},{7,3},{1,5},{3,7},{12,8},{14,10},{8,... | collective-permute-start | bytes 12296 | tf_op jit(solution)/shard_map/ppermute | solution.py:379
  8.1 2.5 %collective-permute-start = (f32[8,128]{1,0:T(8,128)S(1)}, f32[8,128]{1,0:T(8,128)S(1)}, u32[]{:S(2)}, u32[]{:S(2)}) collective-permute-start(f32[8,128]{1,0:T(8,128)S(1)} %get-tuple-element.20.own0), channel_id=1, source_target_pairs={{2,0},{4,2},{6,4},{0,6},{3,1},{5,3},{7,5},{1,7},{10,8},{12,10},{14... | collective-permute-start | bytes 12296 | tf_op jit(solution)/shard_map/ppermute | solution.py:379
  14.3 26.5 %all-to-all-start = ((bf16[64,8,1152]{2,1,0:T(8,128)(2,1)}), bf16[64,8,1152]{2,1,0:T(8,128)(2,1)S(1)}, u32[]{:S(2)}, u32[]{:S(2)}) async-start(bf16[64,8,1152]{2,1,0:T(8,128)(2,1)} %bitcast.9), calls=%async_computation | async-start | bytes 2359296 | tf_op jit(solution)/shard_map/all_to_all | solution.py:401
  23.6 3.0 %collective-permute-start.4 = (f32[8,128]{1,0:T(8,128)S(1)}, f32[8,128]{1,0:T(8,128)S(1)}, u32[]{:S(2)}, u32[]{:S(2)}) collective-permute-start(f32[8,128]{1,0:T(8,128)S(1)} %get-tuple-element.24.params_ref), channel_id=1, source_target_pairs={{0,1},{1,0},{2,3},{3,2},{4,5},{5,4},{6,7},{7,6},{8,9},{9,8},{10,11... | collective-permute-start | bytes 12296 | tf_op jit(solution)/shard_map/ppermute | solution.py:404
  40.8 23.5 %copy-start.5 = (f32[4,136,1024]{2,1,0:T(8,128)S(1)}, f32[4,136,1024]{2,1,0:T(8,128)}, u32[]{:S(2)}) copy-start(f32[4,136,1024]{2,1,0:T(8,128)} %get-tuple-element.30.middle_ref) | copy-start | bytes 6684676
  41.5 26.7 %copy-start.2 = (bf16[8,128,1024]{2,1,0:T(8,128)(2,1)S(1)}, bf16[8,128,1024]{2,1,0:T(8,128)(2,1)}, u32[]{:S(2)}) copy-start(bf16[8,128,1024]{2,1,0:T(8,128)(2,1)} %get-tuple-element.28.factor_ref) | copy-start | bytes 6291460
  64.2 3.9 %copy-start.1 = (bf16[8,128,1024]{2,1,0:T(8,128)(2,1)S(1)}, bf16[8,128,1024]{2,1,0:T(8,128)(2,1)}, u32[]{:S(2)}) copy-start(bf16[8,128,1024]{2,1,0:T(8,128)(2,1)} %get-tuple-element.27.base_ref) | copy-start | bytes 6291460
  64.2 3.9 %copy-start.3 = (bf16[128,1024]{1,0:T(8,128)(2,1)S(1)}, bf16[128,1024]{1,0:T(8,128)(2,1)}, u32[]{:S(2)}) copy-start(bf16[128,1024]{1,0:T(8,128)(2,1)} %c_ref.3) | copy-start | bytes 786436
  64.8 5.7 %collective-permute-start.5 = (bf16[4,128,1024]{2,1,0:T(8,128)(2,1)S(1)}, bf16[4,128,1024]{2,1,0:T(8,128)(2,1)S(1)}, u32[]{:S(2)}, u32[]{:S(2)}) collective-permute-start(bf16[4,128,1024]{2,1,0:T(8,128)(2,1)S(1)} %get-tuple-element.31), channel_id=1, source_target_pairs={{0,1},{1,0},{2,3},{3,2},{4,5},{5,4},{6,7},{7,6},{8,9},{9,8},{10,11... | collective-permute-start | bytes 3145736 | tf_op jit(solution)/shard_map/ppermute | solution.py:461
  68.1 2.3 %copy-start.7 = (f32[8192]{0:T(1024)S(1)}, f32[8192]{0:T(1024)}, u32[]{:S(2)}) copy-start(f32[8192]{0:T(1024)} %param.18) | copy-start | bytes 98308

commit v6 on v5

--- a/solution.py
+++ b/solution.py
@@ -24,6 +24,7 @@
 SLABS = STATE // SLAB
 LANES = 128
 PIECE = 4
+AHEAD = 6
 PARTS = 4
 EPS = 1e-5
 
@@ -89,6 +90,35 @@
     copy = pltpu.make_async_copy(source, target, sem)
     copy.start()
     return copy
+
+
+def placed(turn_rows, place, core):
+    lane = iota((SLAB, LANES), 1)
+    params = jnp.zeros((SLAB, LANES), f32)
+    for turn, rows in enumerate(turn_rows):
+        some = jnp.where(lane < PER_GROUP, rows, 0.0)
+        params = params + from_front(some, 2 * ((place // CORES + turn) % HALF) + core)
+    return params
+
+
+def allowed_pairs(start):
+    t = iota((CHUNK, CHUNK), 0)
+    s = iota((CHUNK, CHUNK), 1)
+    return (s <= t) & ((t >= start) == (s >= start))
+
+
+def group_terms(rows, group, spread_ref, allowed, x, keys, queries, gate):
+    wide = spread(rows, group, spread_ref)
+    grown = wide[CHUNK : 2 * CHUNK]
+    x = x.astype(f32)
+    xq = (x * wide[:CHUNK]).astype(bf16)
+    score = lax.dot_general(queries, keys, (((1,), (1,)), ((), ())), preferred_element_type=f32)
+    mixing = jnp.where(allowed, score, 0.0).astype(bf16)
+    inside = jnp.dot(mixing, xq, preferred_element_type=f32)
+    skip = wide[2 * CHUNK : 2 * CHUNK + 1]
+    gate = gate.astype(f32)
+    silu = gate / (1.0 + jnp.exp(-gate))
+    return ((inside * grown + skip * x) * silu).astype(bf16), (grown * silu).astype(bf16)
 
 
 def pack_kernel(
@@ -121,17 +151,13 @@
 
 def write_kernel(
     place_ref, starts_ref, own0, own1, own2, own3, spread_ref, logit_ref, got_ref, x_ref, b_ref,
-    pay_out, middle_out, params_ref, pay_ref, middle_ref, sems,
+    pay_out, middle_out, pay_ref, middle_ref, sems,
 ):
     place = place_ref[0]
     core = place % CORES
     tail = HALF_WIDE + HALF * STATE
     lane = iota((SLAB, LANES), 1)
-    params = jnp.zeros((SLAB, LANES), f32)
-    for turn, ref in enumerate((own0, own1, own2, own3)):
-        some = jnp.where(lane < PER_GROUP, ref[...], 0.0)
-        params = params + from_front(some, 2 * ((place // CORES + turn) % HALF) + core)
-    params_ref[...] = params
+    params = placed([ref[...] for ref in (own0, own1, own2, own3)], place, core)
     logit = jnp.concatenate([logit_ref[...].astype(f32), got_ref[:, tail:].astype(f32)], axis=1)
     half = iota((CHUNK, 2 * LANES), 1) // PER_GROUP % CORES == core
     both = jnp.concatenate([params, params], axis=1)
@@ -197,51 +223,63 @@
     lax.fori_loop(0, blocks, one, jnp.zeros((SLAB, WIDE), f32), unroll=8)
 
 
-def inside_kernel(
-    place_ref, starts_ref, params_ref, got_ref, x_ref, logit_in, b_in, c_in, gate_in,
-    base_out, factor_out,
-    logit_ref, b_ref, c_ref, gate_ref, base_ref, factor_ref, spread_ref, sems, sent_sems,
+def inside_kernel(ahead, place_ref, starts_ref, *refs):
+    core = place_ref[0] % CORES
+    if ahead:
+
+        @pl.when(core == 0)
+        def _():
+            inside_terms(True, place_ref, starts_ref, *refs)
+
+    else:
+        inside_terms(False, place_ref, starts_ref, *refs)
+
+
+def inside_terms(
+    ahead, place_ref, starts_ref, own_ref, got_ref, x_ref, logit_in, b_in, c_in, gate_in, *refs
 ):
+    base_out, factor_out, logit_ref, b_ref, c_ref, gate_ref, base_ref, factor_ref, spread_ref, sems, sent_sems = refs[-11:]
     place = place_ref[0]
-    start = chunk_start(place, starts_ref, place % CORES)
+    core = place % CORES
+    start = chunk_start(place, starts_ref, core)
     logit_copy = fetch(logit_in, logit_ref, sems.at[0])
     b_copy = fetch(b_in, b_ref, sems.at[1])
     c_copy = fetch(c_in, c_ref, sems.at[2])
     gate_copy = fetch(gate_in, gate_ref, sems.at[3])
     spread_ref[...] = spreader(2 * LANES, 1)
-    params = params_ref[...] + got_ref[...]
+    params = placed([own_ref[i * SLAB : (i + 1) * SLAB] for i in range(HALF)], place, core)
+    params = params + placed([got_ref[i * SLAB : (i + 1) * SLAB] for i in range(HALF)], place, 1 - core)
     logit_copy.wait()
     step = softplus(logit_ref[...].astype(f32) + params[0:1])
     p, q = cumulated(step, params[1:2])
     rows = jnp.concatenate([q, p, jnp.broadcast_to(params[2:3], (2 * SLAB, LANES))], axis=0)
-    t = iota((CHUNK, CHUNK), 0)
-    s = iota((CHUNK, CHUNK), 1)
-    allowed = (s <= t) & ((t >= start) == (s >= start))
+    allowed = allowed_pairs(start)
     b_copy.wait()
     c_copy.wait()
     gate_copy.wait()
-    sent = []
-    for group in range(GROUPS):
-        columns = slice(group * WIDE, (group + 1) * WIDE)
-        states = slice(group * STATE, (group + 1) * STATE)
-        wide = spread(rows, group, spread_ref)
-        grown = wide[CHUNK : 2 * CHUNK]
-        x = x_ref[:, columns].astype(f32)
-        xq = (x * wide[:CHUNK]).astype(bf16)
-        score = lax.dot_general(
-            c_ref[:, states], b_ref[:, states], (((1,), (1,)), ((), ())), preferred_element_type=f32
-        )
-        mixing = jnp.where(allowed, score, 0.0).astype(bf16)
-        inside = jnp.dot(mixing, xq, preferred_element_type=f32)
-        skip = wide[2 * CHUNK : 2 * CHUNK + 1]
-        gate = gate_ref[:, columns].astype(f32)
-        silu = gate / (1.0 + jnp.exp(-gate))
-        base_ref[group] = ((inside * grown + skip * x) * silu).astype(bf16)
-        factor_ref[group] = (grown * silu).astype(bf16)
-        sent.append(fetch(base_ref.at[group], base_out.at[group], sent_sems.at[0, group]))
-        sent.append(fetch(factor_ref.at[group], factor_out.at[group], sent_sems.at[1, group]))
-    for copy in sent:
-        copy.wait()
+
+    def terms(groups):
+        sent = []
+        for i, (j, half) in enumerate(groups):
+            group = CORES * j + half
+            columns, states = columns_of(j, half, WIDE), columns_of(j, half, STATE)
+            base_ref[group], factor_ref[group] = group_terms(
+                rows, group, spread_ref, allowed, x_ref[:, columns], b_ref[:, states], c_ref[:, states], gate_ref[:, columns]
+            )
+            sent.append(fetch(base_ref.at[group], base_out.at[group], sent_sems.at[0, i]))
+            sent.append(fetch(factor_ref.at[group], factor_out.at[group], sent_sems.at[1, i]))
+        for copy in sent:
+            copy.wait()
+
+    order = [(j, half) for half in (core, 1 - core) for j in range(HALF)]
+    if ahead:
+        terms(order[:AHEAD])
+    else:
+        terms(order[AHEAD:])
+
+        @pl.when(core > 0)
+        def _():
+            terms(order[:AHEAD])
 
 
 def states_kernel(first_group, place_ref, state_ref, middle_ref, own_ref, sent_ref):
@@ -332,7 +370,7 @@
 
     anywhere = pl.BlockSpec(memory_space=pl.ANY)
 
-    def call(kernel, scalars, operands, out_shape, scratch, name, cost=None, out_specs=None, in_specs=None, mib=24):
+    def call(kernel, scalars, operands, out_shape, scratch, name, cost=None, out_specs=None, in_specs=None, mib=24, aliases={}):
         return pl.pallas_call(
             kernel,
             in_specs=[smem] * len(scalars) + (in_specs or [vmem] * len(operands)),
@@ -341,6 +379,7 @@
             scratch_shapes=scratch,
             compiler_params=pltpu.CompilerParams(vmem_limit_bytes=mib * 2**20),
             cost_estimate=cost,
+            input_output_aliases=aliases,
             name=name,
         )(*scalars, *operands)
 
@@ -348,7 +387,6 @@
         return jax.ShapeDtypeStruct(dims, kind)
 
     where = (place, document_starts)
-    spread_scratch = pltpu.VMEM((2 * LANES, WIDE), bf16)
 
     dma = pltpu.SemaphoreType.DMA
     packed_width = HALF_WIDE + HALF * STATE + LANES
@@ -380,14 +418,19 @@
     ]
     packed_got = lax.ppermute(packed, "core", swap)
 
-    pay, middle, params = call(
+    own_rows = jnp.concatenate(turns)
+    got_rows = lax.ppermute(own_rows, "core", swap)
+
+    def in_hbm(v):
+        return pltpu.with_memory_space_constraint(v, pltpu.HBM)
+
+    pay, middle = call(
         write_kernel,
         where,
         (*turns, spread_matrix, step_logits, packed_got, head_inputs, write_keys),
         [
             pltpu.HBM((SLABS, HALF, SLAB, WIDE + LANES), bf16),
             pltpu.HBM((HALF, STATE + SLAB, WIDE), f32),
-            pltpu.VMEM((SLAB, LANES), f32),
         ],
         [
             pltpu.VMEM((HALF, SLABS, SLAB, WIDE + LANES), bf16),
@@ -395,43 +438,47 @@
             dma((2, HALF)),
         ],
         "write",
-        out_specs=[anywhere] * 2 + [vmem],
-    )
-
+        out_specs=[anywhere] * 2,
+    )
+
+    def inside(ahead, passed, passed_shapes, name):
+        terms = (pltpu.HBM((GROUPS, CHUNK, WIDE), bf16),) * 2
+        outs = len(passed_shapes)
+        return call(
+            functools.partial(inside_kernel, ahead),
+            where,
+            (
+                own_rows,
+                got_rows,
+                head_inputs,
+                *(in_hbm(v) for v in (step_logits, write_keys, read_queries, gate_inputs, *passed)),
+            ),
+            (*passed_shapes, *terms),
+            [
+                pltpu.VMEM((CHUNK, LANES), bf16),
+                pltpu.VMEM((CHUNK, GROUPS * STATE), bf16),
+                pltpu.VMEM((CHUNK, GROUPS * STATE), bf16),
+                pltpu.VMEM((CHUNK, INNER), bf16),
+                pltpu.VMEM((GROUPS, CHUNK, WIDE), bf16),
+                pltpu.VMEM((GROUPS, CHUNK, WIDE), bf16),
+                pltpu.VMEM((2 * LANES, WIDE), bf16),
+                dma((4,)),
+                dma((2, GROUPS)),
+            ],
+            name,
+            pl.CostEstimate(flops=2 * 4 * CHUNK * STATE * INNER, bytes_accessed=9 * 2**20, transcendentals=2**20),
+            out_specs=[anywhere] * (outs + 2),
+            in_specs=[vmem] * 3 + [anywhere] * (4 + len(passed)),
+            aliases={2 + 7 + i: i for i in range(len(passed))},
+        )
+
+    pay, base, factor = inside(
+        True, (pay,), (pltpu.HBM((SLABS, HALF, SLAB, WIDE + LANES), bf16),), "ahead"
+    )
     arrived = lax.all_to_all(
         pay.reshape(blocks, SLAB, WIDE + LANES), ("ctx", "z"), 0, 0, tiled=True
     )
-    params_got = lax.ppermute(params, "core", swap)
-
-    base, factor = call(
-        inside_kernel,
-        where,
-        (
-            params,
-            params_got,
-            head_inputs,
-            *(
-                pltpu.with_memory_space_constraint(v, pltpu.HBM)
-                for v in (step_logits, write_keys, read_queries, gate_inputs)
-            ),
-        ),
-        [pltpu.HBM((GROUPS, CHUNK, WIDE), bf16), pltpu.HBM((GROUPS, CHUNK, WIDE), bf16)],
-        [
-            pltpu.VMEM((CHUNK, LANES), bf16),
-            pltpu.VMEM((CHUNK, GROUPS * STATE), bf16),
-            pltpu.VMEM((CHUNK, GROUPS * STATE), bf16),
-            pltpu.VMEM((CHUNK, INNER), bf16),
-            pltpu.VMEM((GROUPS, CHUNK, WIDE), bf16),
-            pltpu.VMEM((GROUPS, CHUNK, WIDE), bf16),
-            spread_scratch,
-            dma((4,)),
-            dma((2, GROUPS)),
-        ],
-        "inside",
-        pl.CostEstimate(flops=2 * 4 * CHUNK * STATE * INNER, bytes_accessed=9 * 2**20, transcendentals=2**20),
-        out_specs=[anywhere] * 2,
-        in_specs=[vmem] * 3 + [anywhere] * 4,
-    )
+    base, factor = inside(False, (base, factor), (), "inside")
     arrived, base, factor = lax.optimization_barrier((arrived, base, factor))
 
     [frozen] = call(

time: 73.6 us -> 73.2 us (level)
  blocking collectives: 22.8 us -> 17.8 us
  starting transfers between devices: 22.1 us -> 25.8 us
  Pallas kernels: 17.4 us -> 19.1 us
  waiting for transfers between devices: 10.9 us -> 9.7 us
    all_to_all x1, blocking collectives: 22.8 us -> 17.8 us  [local(): returned = lax.all_to_all(frozen, ('ctx', 'z'), 0, 0, tiled=True)]
    ppermute x1, starting transfers between devices: 3.37 us -> 7.27 us  [local(): states_got = [lax.ppermute(v, 'core', swap) for v in states_sent]]
    pallas_call x7 -> x8, Pallas kernels: 17.4 us -> 19.1 us  [call(): pl.pallas_call(kernel, in_specs=[smem] * len(scalars) + (in_specs or [vme...]
    ppermute x1, waiting for transfers between devices: 0.82 us -> 0.01 us  [local(): got_rows = lax.ppermute(own_rows, 'core', swap)]
  transfers between devices with their start and end apart: 7 -> 7, of which waited for: 5 -> 3; matrix products, arithmetic and copies ran while one was open for 0% -> 0% of each run, Pallas kernels for 11% -> 18%
where the time goes in v6:
time: 73.2 us; the launch traced here: 72.9 us
  starting transfers between devices  25.8 us (35%)
  Pallas kernels  19.1 us (26%)
  blocking collectives  17.8 us (24%)
  waiting for transfers between devices  9.7 us (13%)
    pallas_call x8, Pallas kernels, call(): pl.pallas_call(kernel, in_specs=[smem] * len(scalars) + (in_specs or [vme...  19.1 us
    all_to_all x1, blocking collectives, local(): returned = lax.all_to_all(frozen, ('ctx', 'z'), 0, 0, tiled=True)  17.8 us
    all_to_all x1, starting transfers between devices, local(): lax.all_to_all(pay.reshape(blocks, SLAB, WIDE + LANES), ('ctx', 'z'), 0,...  9.46 us
    ppermute x1, starting transfers between devices, local(): states_got = [lax.ppermute(v, 'core', swap) for v in states_sent]  7.27 us
    all_to_all x1, waiting for transfers between devices, local(): lax.all_to_all(pay.reshape(blocks, SLAB, WIDE + LANES), ('ctx', 'z'), 0,...  6.89 us
    ppermute x3, starting transfers between devices, local(): lax.ppermute(own, 'z', [((i + turn) % depth, i) for i in range(depth)])  5.79 us
    ppermute x1, starting transfers between devices, local(): got_rows = lax.ppermute(own_rows, 'core', swap)  1.86 us
    ppermute x3, waiting for transfers between devices, local(): lax.ppermute(own, 'z', [((i + turn) % depth, i) for i in range(depth)])  1.73 us
  transfers between devices with their start and end apart: 7, of which 3 were waited for; matrix products, arithmetic and copies ran while one was open for 0% of the time, Pallas kernels for 18%

profile of v6, /device:TPU:1, one launch (start us, length us, event | category | flops | bytes accessed | tf_op | source)
XLA Modules:
  0.0 72.9 jit_solution(7908429883477489003)
XLA Ops:
  0.0 0.0 copy-start.10
  0.0 1.5 %pack.1 = (bf16[128,4736]{1,0:T(8,128)(2,1)S(1)}, f32[8,128]{1,0:T(8,128)S(1)}, bf16[256,1024]{1,0:T(8,128)(2,1)S(1)}) custom-call(s32[1]{0:T(128)} %bitcast.place_ref, f32[1,16]{1,0:T(1,128)} %bitcast.10, f32[1,16]{1,0:T(1,128)} %bitcast.11, f32[1,16]{1,0:T(1,128)} %bitcast.12, bf16[128,128]{1,0:T(8,128)(2,1)} %refs_3_.3, bf16[128,8192]{1,0:T(8,128)(2,1)} %refs_2_.3, ...), custom_call_target="tpu_custom_call" | custom-call | tf_op jit(solution)/shard_map/pack/pallas_call | solution.py:374
  1.6 1.5 %collective-permute-start.4 = (bf16[128,4736]{1,0:T(8,128)(2,1)S(1)}, bf16[128,4736]{1,0:T(8,128)(2,1)S(1)}, u32[]{:S(2)}, u32[]{:S(2)}) collective-permute-start(bf16[128,4736]{1,0:T(8,128)(2,1)S(1)} %get-tuple-element.24), channel_id=1, source_target_pairs={{0,1},{1,0},{2,3},{3,2},{4,5},{5,4},{6,7},{7,6},{8,9},{9,8},{10,11... | collective-permute-start | bytes 3637256 | tf_op jit(solution)/shard_map/ppermute | solution.py:419
  3.1 1.8 %collective-permute-start.2 = (f32[8,128]{1,0:T(8,128)S(1)}, f32[8,128]{1,0:T(8,128)S(1)}, u32[]{:S(2)}, u32[]{:S(2)}) collective-permute-start(f32[8,128]{1,0:T(8,128)S(1)} %get-tuple-element.22.own0), channel_id=1, source_target_pairs={{6,0},{0,2},{2,4},{4,6},{7,1},{1,3},{3,5},{5,7},{14,8},{8,10},{10,... | collective-permute-start | bytes 12296 | tf_op jit(solution)/shard_map/ppermute | solution.py:417
  4.8 3.3 %collective-permute-start.1 = (f32[8,128]{1,0:T(8,128)S(1)}, f32[8,128]{1,0:T(8,128)S(1)}, u32[]{:S(2)}, u32[]{:S(2)}) collective-permute-start(f32[8,128]{1,0:T(8,128)S(1)} %get-tuple-element.22.own0), channel_id=1, source_target_pairs={{4,0},{6,2},{0,4},{2,6},{5,1},{7,3},{1,5},{3,7},{12,8},{14,10},{8,... | collective-permute-start | bytes 12296 | tf_op jit(solution)/shard_map/ppermute | solution.py:417
  8.1 0.7 collective-permute-start
  8.8 1.7 %collective-permute-done.own1 = f32[8,128]{1,0:T(8,128)S(1)} collective-permute-done((f32[8,128]{1,0:T(8,128)S(1)}, f32[8,128]{1,0:T(8,128)S(1)}, u32[]{:S(2)}, u32[]{:S(2)}) %collective-permute-start) | collective-permute-done | bytes 4128 | tf_op jit(solution)/shard_map/ppermute | solution.py:417
  10.6 0.0 collective-permute-done.1.own2
  10.6 0.0 collective-permute-done.2.own3
  10.6 1.9 %collective-permute-start.3 = (f32[32,128]{1,0:T(8,128)S(1)}, f32[32,128]{1,0:T(8,128)S(1)}, u32[]{:S(2)}, u32[]{:S(2)}) collective-permute-start(f32[32,128]{1,0:T(8,128)S(1)} %constant_dynamic-update-slice_fusion.refs_0_), channel_id=1, source_target_pairs={{0,1},{1,0},{2,3},{3,2},{4,5},{5,4},{6,7},{7,6},{8,9},{9,8},{10,11... | collective-permute-start | bytes 49160 | tf_op jit(solution)/shard_map/ppermute | solution.py:422
  12.5 3.7 %write.1 = (bf16[16,4,8,1152]{3,2,1,0:T(8,128)(2,1)}, f32[4,136,1024]{2,1,0:T(8,128)}) custom-call(s32[1]{0:T(128)} %bitcast.place_ref, s32[4]{0:T(128)S(1)} %copy-done.10, f32[8,128]{1,0:T(8,128)S(1)} %get-tuple-element.22.own0, f32[8,128]{1,0:T(8,128)S(1)} %collective-permute-done.own1, f32[8,128]{1,0:T(8,128)S(1)} %collective-permute-done.1.own2, ...), custom_call_target="tpu_custom_call" | custom-call | tf_op jit(solution)/shard_map/write/pallas_call | solution.py:374
  16.2 0.0 collective-permute-done.3.refs_1_
  16.2 0.7 %ahead.1 = (bf16[16,4,8,1152]{3,2,1,0:T(8,128)(2,1)}, bf16[8,128,1024]{2,1,0:T(8,128)(2,1)}, bf16[8,128,1024]{2,1,0:T(8,128)(2,1)}) custom-call(s32[1]{0:T(128)} %bitcast.place_ref, s32[4]{0:T(128)S(1)} %copy-done.10, f32[32,128]{1,0:T(8,128)S(1)} %constant_dynamic-update-slice_fusion.refs_0_, ...), custom_call_target="tpu_custom_call", output_to_operand_aliasing={{0}: (9, {})} | custom-call | flops 1073741824 | bytes 9437184 | tf_op jit(solution)/shard_map/ahead/pallas_call | solution.py:374
  16.9 0.0 copy-start.11
  17.0 9.5 %all-to-all-start = ((bf16[64,8,1152]{2,1,0:T(8,128)(2,1)}), bf16[64,8,1152]{2,1,0:T(8,128)(2,1)S(1)}, u32[]{:S(2)}, u32[]{:S(2)}) async-start(bf16[64,8,1152]{2,1,0:T(8,128)(2,1)} %bitcast.9), calls=%async_computation | async-start | bytes 2359296 | tf_op jit(solution)/shard_map/all_to_all | solution.py:478
  26.4 7.9 %inside.1 = (bf16[8,128,1024]{2,1,0:T(8,128)(2,1)}, bf16[8,128,1024]{2,1,0:T(8,128)(2,1)}) custom-call(s32[1]{0:T(128)} %bitcast.place_ref, s32[4]{0:T(128)S(1)} %copy-done.11, f32[32,128]{1,0:T(8,128)S(1)} %constant_dynamic-update-slice_fusion.refs_0_, f32[32,128]{1,0:T(8,128)S(1)} %copy-done.8, ...), custom_call_target="tpu_custom_call", output_to_operand_aliasing={{0}: (9, {}), {1}: (10, {})} | custom-call | flops 1073741824 | bytes 9437184 | tf_op jit(solution)/shard_map/inside/pallas_call | solution.py:374
  34.4 6.9 %all-to-all-done.pay_ref = bf16[64,8,1152]{2,1,0:T(8,128)(2,1)S(1)} async-done(((bf16[64,8,1152]{2,1,0:T(8,128)(2,1)}), bf16[64,8,1152]{2,1,0:T(8,128)(2,1)S(1)}, u32[]{:S(2)}, u32[]{:S(2)}) %all-to-all-start) | async-done | bytes 1179680 | tf_op jit(solution)/shard_map/all_to_all | solution.py:478
  41.3 0.7 scan.1
  42.0 17.8 %all_to_all.10 = bf16[64,8,1024]{2,1,0:T(8,128)(2,1)S(1)} all-to-all(bf16[64,8,1024]{2,1,0:T(8,128)(2,1)S(1)} %scan.1), channel_id=1, replica_groups=mesh['ctx'=16,'z'=4,'core'=2] {'ctx','z'}, dimensions={0} | all-to-all | bytes 2097152 | tf_op jit(solution)/shard_map/all_to_all | solution.py:493
  59.8 0.5 states.1
  60.3 7.3 %collective-permute-start.5 = (bf16[4,128,1024]{2,1,0:T(8,128)(2,1)S(1)}, bf16[4,128,1024]{2,1,0:T(8,128)(2,1)S(1)}, u32[]{:S(2)}, u32[]{:S(2)}) collective-permute-start(bf16[4,128,1024]{2,1,0:T(8,128)(2,1)S(1)} %get-tuple-element.35), channel_id=1, source_target_pairs={{0,1},{1,0},{2,3},{3,2},{4,5},{5,4},{6,7},{7,6},{8,9},{9,8},{10,11... | collective-permute-start | bytes 3145736 | tf_op jit(solution)/shard_map/ppermute | solution.py:508
  67.5 1.2 %own.1 = (f32[4,128,1024]{2,1,0:T(8,128)S(1)}, f32[128,128]{1,0:T(8,128)S(1)}) custom-call(s32[1]{0:T(128)} %bitcast.place_ref, s32[4]{0:T(128)S(1)} %copy-done.11, bf16[8,128,1024]{2,1,0:T(8,128)(2,1)S(1)} %copy-done.1, bf16[8,128,1024]{2,1,0:T(8,128)(2,1)S(1)} %copy-done.2, bf16[128,1024]{1,0:T(8,128)(2,1)S(1)} %copy-done.3, ...), custom_call_target="tpu_custom_call" | custom-call | flops 268435456 | bytes 5242880 | tf_op jit(solution)/shard_map/own/pallas_call | solution.py:374
  68.7 1.1 %collective-permute-done.5.refs_0_ = bf16[4,128,1024]{2,1,0:T(8,128)(2,1)S(1)} collective-permute-done((bf16[4,128,1024]{2,1,0:T(8,128)(2,1)S(1)}, bf16[4,128,1024]{2,1,0:T(8,128)(2,1)S(1)}, u32[]{:S(2)}, u32[]{:S(2)}) %collective-permute-start.5) | collective-permute-done | bytes 1048608 | tf_op jit(solution)/shard_map/ppermute | solution.py:508
  69.8 2.9 %last.1 = bf16[128,8192]{1,0:T(8,128)(2,1)} custom-call(s32[1]{0:T(128)} %bitcast.place_ref, s32[4]{0:T(128)S(1)} %copy-done.11, bf16[8,128,1024]{2,1,0:T(8,128)(2,1)S(1)} %copy-done.1, bf16[8,128,1024]{2,1,0:T(8,128)(2,1)S(1)} %copy-done.2, bf16[128,1024]{1,0:T(8,128)(2,1)S(1)} %copy-done.3, bf16[4,128,1024]{2,1,0:T(8,128)(2,1)S(1)} %collective-permute-done.5.refs_0_, ...), custom_call_target="tpu_custom_call" | custom-call | tf_op jit(solution)/shard_map/last/pallas_call | solution.py:374
  (27 shorter events, 0.1 us)
Async XLA Ops:
  0.0 12.5 %copy-start.6 = (bf16[128,128]{1,0:T(8,128)(2,1)S(1)}, bf16[128,128]{1,0:T(8,128)(2,1)}, u32[]{:S(2)}) copy-start(bf16[128,128]{1,0:T(8,128)(2,1)} %refs_3_.3) | copy-start | bytes 98308
  0.0 12.5 %copy-start.4 = (bf16[128,1024]{1,0:T(8,128)(2,1)S(1)}, bf16[128,1024]{1,0:T(8,128)(2,1)}, u32[]{:S(2)}) copy-start(bf16[128,1024]{1,0:T(8,128)(2,1)} %refs_4_.3) | copy-start | bytes 786436
  0.0 12.5 %copy-start = (bf16[128,8192]{1,0:T(8,128)(2,1)S(1)}, bf16[128,8192]{1,0:T(8,128)(2,1)}, u32[]{:S(2)}) copy-start(bf16[128,8192]{1,0:T(8,128)(2,1)} %refs_2_.3) | copy-start | bytes 6291460
  0.0 12.5 %copy-start.10 = (s32[4]{0:T(128)S(1)}, s32[4]{0:T(128)}, u32[]{:S(2)}) copy-start(s32[4]{0:T(128)} %starts_ref.9) | copy-start | bytes 52
  1.6 10.9 %collective-permute-start.4 = (bf16[128,4736]{1,0:T(8,128)(2,1)S(1)}, bf16[128,4736]{1,0:T(8,128)(2,1)S(1)}, u32[]{:S(2)}, u32[]{:S(2)}) collective-permute-start(bf16[128,4736]{1,0:T(8,128)(2,1)S(1)} %get-tuple-element.24), channel_id=1, source_target_pairs={{0,1},{1,0},{2,3},{3,2},{4,5},{5,4},{6,7},{7,6},{8,9},{9,8},{10,11... | collective-permute-start | bytes 3637256 | tf_op jit(solution)/shard_map/ppermute | solution.py:419
  3.1 7.5 %collective-permute-start.2 = (f32[8,128]{1,0:T(8,128)S(1)}, f32[8,128]{1,0:T(8,128)S(1)}, u32[]{:S(2)}, u32[]{:S(2)}) collective-permute-start(f32[8,128]{1,0:T(8,128)S(1)} %get-tuple-element.22.own0), channel_id=1, source_target_pairs={{6,0},{0,2},{2,4},{4,6},{7,1},{1,3},{3,5},{5,7},{14,8},{8,10},{10,... | collective-permute-start | bytes 12296 | tf_op jit(solution)/shard_map/ppermute | solution.py:417
  4.8 5.8 %collective-permute-start.1 = (f32[8,128]{1,0:T(8,128)S(1)}, f32[8,128]{1,0:T(8,128)S(1)}, u32[]{:S(2)}, u32[]{:S(2)}) collective-permute-start(f32[8,128]{1,0:T(8,128)S(1)} %get-tuple-element.22.own0), channel_id=1, source_target_pairs={{4,0},{6,2},{0,4},{2,6},{5,1},{7,3},{1,5},{3,7},{12,8},{14,10},{8,... | collective-permute-start | bytes 12296 | tf_op jit(solution)/shard_map/ppermute | solution.py:417
  8.1 2.5 %collective-permute-start = (f32[8,128]{1,0:T(8,128)S(1)}, f32[8,128]{1,0:T(8,128)S(1)}, u32[]{:S(2)}, u32[]{:S(2)}) collective-permute-start(f32[8,128]{1,0:T(8,128)S(1)} %get-tuple-element.22.own0), channel_id=1, source_target_pairs={{2,0},{4,2},{6,4},{0,6},{3,1},{5,3},{7,5},{1,7},{10,8},{12,10},{14... | collective-permute-start | bytes 12296 | tf_op jit(solution)/shard_map/ppermute | solution.py:417
  10.6 5.6 %collective-permute-start.3 = (f32[32,128]{1,0:T(8,128)S(1)}, f32[32,128]{1,0:T(8,128)S(1)}, u32[]{:S(2)}, u32[]{:S(2)}) collective-permute-start(f32[32,128]{1,0:T(8,128)S(1)} %constant_dynamic-update-slice_fusion.refs_0_), channel_id=1, source_target_pairs={{0,1},{1,0},{2,3},{3,2},{4,5},{5,4},{6,7},{7,6},{8,9},{9,8},{10,11... | collective-permute-start | bytes 49160 | tf_op jit(solution)/shard_map/ppermute | solution.py:422
  16.2 0.8 %copy-start.7 = (f32[32,128]{1,0:T(8,128)}, f32[32,128]{1,0:T(8,128)S(1)}, u32[]{:S(2)}) copy-start(f32[32,128]{1,0:T(8,128)S(1)} %collective-permute-done.3.refs_1_) | copy-start | bytes 49156
  16.9 9.5 %copy-start.11 = (s32[4]{0:T(128)S(1)}, s32[4]{0:T(128)}, u32[]{:S(2)}) copy-start(s32[4]{0:T(128)} %starts_ref.9) | copy-start | bytes 52
  16.9 9.5 %copy-start.8 = (f32[32,128]{1,0:T(8,128)S(1)}, f32[32,128]{1,0:T(8,128)}, u32[]{:S(2)}) copy-start(f32[32,128]{1,0:T(8,128)} %copy-done.7) | copy-start | bytes 49156
  17.0 24.3 %all-to-all-start = ((bf16[64,8,1152]{2,1,0:T(8,128)(2,1)}), bf16[64,8,1152]{2,1,0:T(8,128)(2,1)S(1)}, u32[]{:S(2)}, u32[]{:S(2)}) async-start(bf16[64,8,1152]{2,1,0:T(8,128)(2,1)} %bitcast.9), calls=%async_computation | async-start | bytes 2359296 | tf_op jit(solution)/shard_map/all_to_all | solution.py:478
  41.3 18.5 %copy-start.5 = (f32[4,136,1024]{2,1,0:T(8,128)S(1)}, f32[4,136,1024]{2,1,0:T(8,128)}, u32[]{:S(2)}) copy-start(f32[4,136,1024]{2,1,0:T(8,128)} %get-tuple-element.34.middle_ref) | copy-start | bytes 6684676
  42.0 25.6 %copy-start.2 = (bf16[8,128,1024]{2,1,0:T(8,128)(2,1)S(1)}, bf16[8,128,1024]{2,1,0:T(8,128)(2,1)}, u32[]{:S(2)}) copy-start(bf16[8,128,1024]{2,1,0:T(8,128)(2,1)} %get-tuple-element.32.factor_ref) | copy-start | bytes 6291460
  59.8 7.8 %copy-start.1 = (bf16[8,128,1024]{2,1,0:T(8,128)(2,1)S(1)}, bf16[8,128,1024]{2,1,0:T(8,128)(2,1)}, u32[]{:S(2)}) copy-start(bf16[8,128,1024]{2,1,0:T(8,128)(2,1)} %get-tuple-element.31.base_ref) | copy-start | bytes 6291460
  59.8 7.8 %copy-start.3 = (bf16[128,1024]{1,0:T(8,128)(2,1)S(1)}, bf16[128,1024]{1,0:T(8,128)(2,1)}, u32[]{:S(2)}) copy-start(bf16[128,1024]{1,0:T(8,128)(2,1)} %c_ref.3) | copy-start | bytes 786436
  60.3 9.6 %collective-permute-start.5 = (bf16[4,128,1024]{2,1,0:T(8,128)(2,1)S(1)}, bf16[4,128,1024]{2,1,0:T(8,128)(2,1)S(1)}, u32[]{:S(2)}, u32[]{:S(2)}) collective-permute-start(bf16[4,128,1024]{2,1,0:T(8,128)(2,1)S(1)} %get-tuple-element.35), channel_id=1, source_target_pairs={{0,1},{1,0},{2,3},{3,2},{4,5},{5,4},{6,7},{7,6},{8,9},{9,8},{10,11... | collective-permute-start | bytes 3145736 | tf_op jit(solution)/shard_map/ppermute | solution.py:508
  67.5 2.3 %copy-start.9 = (f32[8192]{0:T(1024)S(1)}, f32[8192]{0:T(1024)}, u32[]{:S(2)}) copy-start(f32[8192]{0:T(1024)} %param.18) | copy-start | bytes 98308

commit v7 on v6

--- a/solution.py
+++ b/solution.py
@@ -24,8 +24,8 @@
 SLABS = STATE // SLAB
 LANES = 128
 PIECE = 4
-AHEAD = 6
-PARTS = 4
+AHEAD = 5
+PARTS = 8
 EPS = 1e-5
 
 bf16 = jnp.bfloat16
@@ -293,7 +293,7 @@
         sent_ref[i] = jnp.where(core == 0, second, first).astype(bf16)
 
 
-def gated_part(place, starts_ref, half, first_group, base_ref, factor_ref, c_ref, state_ref, gated_ref, power):
+def gated_part(place, starts_ref, half, first_group, base_ref, factor_ref, c_ref, state_ref, gain_ref, gated_ref, power):
     start = chunk_start(place, starts_ref, place % CORES)
     seen = iota((CHUNK, STATE), 0) < start
     for i in range(PIECE):
@@ -302,20 +302,20 @@
         queries = jnp.where(seen, c_ref[:, columns_of(group, half, STATE)].astype(f32), 0.0).astype(bf16)
         outside = jnp.dot(queries, state_ref[i], preferred_element_type=f32)
         gated = base_ref[of_all].astype(f32) + outside * factor_ref[of_all].astype(f32)
-        gated_ref[group] = gated
+        gated_ref[group] = gated * gain_ref[:, columns_of(group, half, WIDE)]
         squares = gated * gated
         for k in range(WIDE // LANES):
             power = power + squares[:, k * LANES : (k + 1) * LANES]
     return power
 
 
-def own_kernel(place_ref, starts_ref, base_ref, factor_ref, c_ref, *refs):
+def own_kernel(place_ref, starts_ref, base_ref, factor_ref, c_ref, gain_ref, *refs):
     *states, gated_ref, power_ref = refs
     place = place_ref[0]
     power = jnp.zeros((CHUNK, LANES), f32)
     for i, state_ref in enumerate(states):
         power = gated_part(
-            place, starts_ref, place % CORES, i * PIECE, base_ref, factor_ref, c_ref, state_ref, gated_ref, power
+            place, starts_ref, place % CORES, i * PIECE, base_ref, factor_ref, c_ref, state_ref, gain_ref, gated_ref, power
         )
     power_ref[...] = power
 
@@ -329,7 +329,7 @@
     power = power_own_ref[...]
     for i, state_ref in enumerate(states):
         power = gated_part(
-            place, starts_ref, 1 - core, i * PIECE, base_ref, factor_ref, c_ref, state_ref, gated_ref, power
+            place, starts_ref, 1 - core, i * PIECE, base_ref, factor_ref, c_ref, state_ref, gain_ref, gated_ref, power
         )
     total = jnp.sum(power, axis=1, keepdims=True)
     scale = lax.rsqrt(total * (1.0 / INNER) + EPS)
@@ -337,11 +337,12 @@
     copies = []
     for part in range(PARTS):
         some = slice(part * rows, (part + 1) * rows)
+        wide_scale = jnp.broadcast_to(scale[some], (rows, WIDE))
         for half, ref in ((core, gated_own_ref), (1 - core, gated_ref)):
             for group in range(HALF):
                 columns = columns_of(group, half, WIDE)
                 gated = ref[group, some]
-                done_ref[some, columns] = (gated * scale[some] * gain_ref[:, columns]).astype(bf16)
+                done_ref[some, columns] = (gated * wide_scale).astype(bf16)
         copies.append(fetch(done_ref.at[some], out_ref.at[some], sems.at[part]))
     for copy in copies:
         copy.wait()
@@ -510,7 +511,7 @@
     gated, power = call(
         own_kernel,
         where,
-        (base, factor, read_queries, *states_own),
+        (base, factor, read_queries, norm_gain.reshape(1, INNER), *states_own),
         [shape((HALF, CHUNK, WIDE), f32), shape((CHUNK, LANES), f32)],
         [],
         "own",

time: 73.2 us -> 73.1 us (level)
  blocking collectives: 17.8 us -> 19.4 us
  starting transfers between devices: 25.8 us -> 24.4 us
    all_to_all x1, blocking collectives: 17.8 us -> 19.4 us  [local(): returned = lax.all_to_all(frozen, ('ctx', 'z'), 0, 0, tiled=True)]
    ppermute x1, starting transfers between devices: 7.27 us -> 5.79 us  [local(): states_got = [lax.ppermute(v, 'core', swap) for v in states_sent]]
where the time goes in v7:
time: 73.1 us; the launch traced here: 72.7 us
  starting transfers between devices  24.4 us (33%)
  blocking collectives  19.4 us (27%)
  Pallas kernels  19.1 us (26%)
  waiting for transfers between devices  9.49 us (13%)
    all_to_all x1, blocking collectives, local(): returned = lax.all_to_all(frozen, ('ctx', 'z'), 0, 0, tiled=True)  19.4 us
    pallas_call x8, Pallas kernels, call(): pl.pallas_call(kernel, in_specs=[smem] * len(scalars) + (in_specs or [vme...  19.1 us
    all_to_all x1, starting transfers between devices, local(): lax.all_to_all(pay.reshape(blocks, SLAB, WIDE + LANES), ('ctx', 'z'), 0,...  9.46 us
    all_to_all x1, waiting for transfers between devices, local(): lax.all_to_all(pay.reshape(blocks, SLAB, WIDE + LANES), ('ctx', 'z'), 0,...  6.75 us
    ppermute x1, starting transfers between devices, local(): states_got = [lax.ppermute(v, 'core', swap) for v in states_sent]  5.79 us
    ppermute x3, starting transfers between devices, local(): lax.ppermute(own, 'z', [((i + turn) % depth, i) for i in range(depth)])  5.79 us
    ppermute x1, starting transfers between devices, local(): got_rows = lax.ppermute(own_rows, 'core', swap)  1.86 us
    ppermute x3, waiting for transfers between devices, local(): lax.ppermute(own, 'z', [((i + turn) % depth, i) for i in range(depth)])  1.73 us
  transfers between devices with their start and end apart: 7, of which 3 were waited for; matrix products, arithmetic and copies ran while one was open for 0% of the time, Pallas kernels for 18%

profile of v7, /device:TPU:1, one launch (start us, length us, event | category | flops | bytes accessed | tf_op | source)
XLA Modules:
  0.0 72.7 jit_solution(2741221897343060176)
XLA Ops:
  0.0 0.0 copy-start.10
  0.0 1.5 %pack.1 = (bf16[128,4736]{1,0:T(8,128)(2,1)S(1)}, f32[8,128]{1,0:T(8,128)S(1)}, bf16[256,1024]{1,0:T(8,128)(2,1)S(1)}) custom-call(s32[1]{0:T(128)} %bitcast.place_ref, f32[1,16]{1,0:T(1,128)} %bitcast.11, f32[1,16]{1,0:T(1,128)} %bitcast.12, f32[1,16]{1,0:T(1,128)} %bitcast.13, bf16[128,128]{1,0:T(8,128)(2,1)} %refs_3_.3, bf16[128,8192]{1,0:T(8,128)(2,1)} %refs_2_.3, ...), custom_call_target="tpu_custom_call" | custom-call | tf_op jit(solution)/shard_map/pack/pallas_call | solution.py:375
  1.6 1.5 %collective-permute-start.4 = (bf16[128,4736]{1,0:T(8,128)(2,1)S(1)}, bf16[128,4736]{1,0:T(8,128)(2,1)S(1)}, u32[]{:S(2)}, u32[]{:S(2)}) collective-permute-start(bf16[128,4736]{1,0:T(8,128)(2,1)S(1)} %get-tuple-element.24), channel_id=1, source_target_pairs={{0,1},{1,0},{2,3},{3,2},{4,5},{5,4},{6,7},{7,6},{8,9},{9,8},{10,11... | collective-permute-start | bytes 3637256 | tf_op jit(solution)/shard_map/ppermute | solution.py:420
  3.1 1.8 %collective-permute-start.2 = (f32[8,128]{1,0:T(8,128)S(1)}, f32[8,128]{1,0:T(8,128)S(1)}, u32[]{:S(2)}, u32[]{:S(2)}) collective-permute-start(f32[8,128]{1,0:T(8,128)S(1)} %get-tuple-element.22.own0), channel_id=1, source_target_pairs={{6,0},{0,2},{2,4},{4,6},{7,1},{1,3},{3,5},{5,7},{14,8},{8,10},{10,... | collective-permute-start | bytes 12296 | tf_op jit(solution)/shard_map/ppermute | solution.py:418
  4.8 3.3 %collective-permute-start.1 = (f32[8,128]{1,0:T(8,128)S(1)}, f32[8,128]{1,0:T(8,128)S(1)}, u32[]{:S(2)}, u32[]{:S(2)}) collective-permute-start(f32[8,128]{1,0:T(8,128)S(1)} %get-tuple-element.22.own0), channel_id=1, source_target_pairs={{4,0},{6,2},{0,4},{2,6},{5,1},{7,3},{1,5},{3,7},{12,8},{14,10},{8,... | collective-permute-start | bytes 12296 | tf_op jit(solution)/shard_map/ppermute | solution.py:418
  8.1 0.7 %collective-permute-start = (f32[8,128]{1,0:T(8,128)S(1)}, f32[8,128]{1,0:T(8,128)S(1)}, u32[]{:S(2)}, u32[]{:S(2)}) collective-permute-start(f32[8,128]{1,0:T(8,128)S(1)} %get-tuple-element.22.own0), channel_id=1, source_target_pairs={{2,0},{4,2},{6,4},{0,6},{3,1},{5,3},{7,5},{1,7},{10,8},{12,10},{14... | collective-permute-start | bytes 12296 | tf_op jit(solution)/shard_map/ppermute | solution.py:418
  8.8 1.7 %collective-permute-done.own1 = f32[8,128]{1,0:T(8,128)S(1)} collective-permute-done((f32[8,128]{1,0:T(8,128)S(1)}, f32[8,128]{1,0:T(8,128)S(1)}, u32[]{:S(2)}, u32[]{:S(2)}) %collective-permute-start) | collective-permute-done | bytes 4128 | tf_op jit(solution)/shard_map/ppermute | solution.py:418
  10.6 0.0 collective-permute-done.1.own2
  10.6 0.0 collective-permute-done.2.own3
  10.6 1.9 %collective-permute-start.3 = (f32[32,128]{1,0:T(8,128)S(1)}, f32[32,128]{1,0:T(8,128)S(1)}, u32[]{:S(2)}, u32[]{:S(2)}) collective-permute-start(f32[32,128]{1,0:T(8,128)S(1)} %constant_dynamic-update-slice_fusion.refs_0_), channel_id=1, source_target_pairs={{0,1},{1,0},{2,3},{3,2},{4,5},{5,4},{6,7},{7,6},{8,9},{9,8},{10,11... | collective-permute-start | bytes 49160 | tf_op jit(solution)/shard_map/ppermute | solution.py:423
  12.5 0.0 collective-permute-done.4.got_ref
  12.5 3.7 %write.1 = (bf16[16,4,8,1152]{3,2,1,0:T(8,128)(2,1)}, f32[4,136,1024]{2,1,0:T(8,128)}) custom-call(s32[1]{0:T(128)} %bitcast.place_ref, s32[4]{0:T(128)S(1)} %copy-done.10, f32[8,128]{1,0:T(8,128)S(1)} %get-tuple-element.22.own0, f32[8,128]{1,0:T(8,128)S(1)} %collective-permute-done.own1, f32[8,128]{1,0:T(8,128)S(1)} %collective-permute-done.1.own2, ...), custom_call_target="tpu_custom_call" | custom-call | tf_op jit(solution)/shard_map/write/pallas_call | solution.py:375
  16.2 0.7 %ahead.1 = (bf16[16,4,8,1152]{3,2,1,0:T(8,128)(2,1)}, bf16[8,128,1024]{2,1,0:T(8,128)(2,1)}, bf16[8,128,1024]{2,1,0:T(8,128)(2,1)}) custom-call(s32[1]{0:T(128)} %bitcast.place_ref, s32[4]{0:T(128)S(1)} %copy-done.10, f32[32,128]{1,0:T(8,128)S(1)} %constant_dynamic-update-slice_fusion.refs_0_, ...), custom_call_target="tpu_custom_call", output_to_operand_aliasing={{0}: (9, {})} | custom-call | flops 1073741824 | bytes 9437184 | tf_op jit(solution)/shard_map/ahead/pallas_call | solution.py:375
  16.9 0.0 copy-start.11
  17.0 9.5 %all-to-all-start = ((bf16[64,8,1152]{2,1,0:T(8,128)(2,1)}), bf16[64,8,1152]{2,1,0:T(8,128)(2,1)S(1)}, u32[]{:S(2)}, u32[]{:S(2)}) async-start(bf16[64,8,1152]{2,1,0:T(8,128)(2,1)} %bitcast.10), calls=%async_computation | async-start | bytes 2359296 | tf_op jit(solution)/shard_map/all_to_all | solution.py:479
  26.4 8.0 %inside.1 = (bf16[8,128,1024]{2,1,0:T(8,128)(2,1)}, bf16[8,128,1024]{2,1,0:T(8,128)(2,1)}) custom-call(s32[1]{0:T(128)} %bitcast.place_ref, s32[4]{0:T(128)S(1)} %copy-done.11, f32[32,128]{1,0:T(8,128)S(1)} %constant_dynamic-update-slice_fusion.refs_0_, f32[32,128]{1,0:T(8,128)S(1)} %copy-done.9, ...), custom_call_target="tpu_custom_call", output_to_operand_aliasing={{0}: (9, {}), {1}: (10, {})} | custom-call | flops 1073741824 | bytes 9437184 | tf_op jit(solution)/shard_map/inside/pallas_call | solution.py:375
  34.4 6.8 %all-to-all-done.pay_ref = bf16[64,8,1152]{2,1,0:T(8,128)(2,1)S(1)} async-done(((bf16[64,8,1152]{2,1,0:T(8,128)(2,1)}), bf16[64,8,1152]{2,1,0:T(8,128)(2,1)S(1)}, u32[]{:S(2)}, u32[]{:S(2)}) %all-to-all-start) | async-done | bytes 1179680 | tf_op jit(solution)/shard_map/all_to_all | solution.py:479
  41.2 0.7 scan.1
  41.9 19.4 %all_to_all.10 = bf16[64,8,1024]{2,1,0:T(8,128)(2,1)S(1)} all-to-all(bf16[64,8,1024]{2,1,0:T(8,128)(2,1)S(1)} %scan.1), channel_id=1, replica_groups=mesh['ctx'=16,'z'=4,'core'=2] {'ctx','z'}, dimensions={0} | all-to-all | bytes 2097152 | tf_op jit(solution)/shard_map/all_to_all | solution.py:494
  61.2 0.5 states.1
  61.7 5.8 %collective-permute-start.5 = (bf16[4,128,1024]{2,1,0:T(8,128)(2,1)S(1)}, bf16[4,128,1024]{2,1,0:T(8,128)(2,1)S(1)}, u32[]{:S(2)}, u32[]{:S(2)}) collective-permute-start(bf16[4,128,1024]{2,1,0:T(8,128)(2,1)S(1)} %get-tuple-element.35), channel_id=1, source_target_pairs={{0,1},{1,0},{2,3},{3,2},{4,5},{5,4},{6,7},{7,6},{8,9},{9,8},{10,11... | collective-permute-start | bytes 3145736 | tf_op jit(solution)/shard_map/ppermute | solution.py:509
  67.6 1.3 %own.1 = (f32[4,128,1024]{2,1,0:T(8,128)S(1)}, f32[128,128]{1,0:T(8,128)S(1)}) custom-call(s32[1]{0:T(128)} %bitcast.place_ref, s32[4]{0:T(128)S(1)} %copy-done.11, bf16[8,128,1024]{2,1,0:T(8,128)(2,1)S(1)} %copy-done.1, bf16[8,128,1024]{2,1,0:T(8,128)(2,1)S(1)} %copy-done.2, bf16[128,1024]{1,0:T(8,128)(2,1)S(1)} %copy-done.3, f32[1,8192]{1,0:T(1,128)S(1)} %bitcast.8, ...), custom_call_target="tpu_custom_call" | custom-call | flops 268435456 | bytes 5242880 | tf_op jit(solution)/shard_map/own/pallas_call | solution.py:375
  68.8 1.0 %collective-permute-done.5.refs_0_ = bf16[4,128,1024]{2,1,0:T(8,128)(2,1)S(1)} collective-permute-done((bf16[4,128,1024]{2,1,0:T(8,128)(2,1)S(1)}, bf16[4,128,1024]{2,1,0:T(8,128)(2,1)S(1)}, u32[]{:S(2)}, u32[]{:S(2)}) %collective-permute-start.5) | collective-permute-done | bytes 1048608 | tf_op jit(solution)/shard_map/ppermute | solution.py:509
  69.8 2.8 %last.1 = bf16[128,8192]{1,0:T(8,128)(2,1)} custom-call(s32[1]{0:T(128)} %bitcast.place_ref, s32[4]{0:T(128)S(1)} %copy-done.11, bf16[8,128,1024]{2,1,0:T(8,128)(2,1)S(1)} %copy-done.1, bf16[8,128,1024]{2,1,0:T(8,128)(2,1)S(1)} %copy-done.2, bf16[128,1024]{1,0:T(8,128)(2,1)S(1)} %copy-done.3, bf16[4,128,1024]{2,1,0:T(8,128)(2,1)S(1)} %collective-permute-done.5.refs_0_, ...), custom_call_target="tpu_custom_call" | custom-call | tf_op jit(solution)/shard_map/last/pallas_call | solution.py:375
  (27 shorter events, 0.1 us)
Async XLA Ops:
  0.0 12.5 %copy-start.6 = (bf16[128,128]{1,0:T(8,128)(2,1)S(1)}, bf16[128,128]{1,0:T(8,128)(2,1)}, u32[]{:S(2)}) copy-start(bf16[128,128]{1,0:T(8,128)(2,1)} %refs_3_.3) | copy-start | bytes 98308
  0.0 12.5 %copy-start.4 = (bf16[128,1024]{1,0:T(8,128)(2,1)S(1)}, bf16[128,1024]{1,0:T(8,128)(2,1)}, u32[]{:S(2)}) copy-start(bf16[128,1024]{1,0:T(8,128)(2,1)} %refs_4_.3) | copy-start | bytes 786436
  0.0 12.5 %copy-start = (bf16[128,8192]{1,0:T(8,128)(2,1)S(1)}, bf16[128,8192]{1,0:T(8,128)(2,1)}, u32[]{:S(2)}) copy-start(bf16[128,8192]{1,0:T(8,128)(2,1)} %refs_2_.3) | copy-start | bytes 6291460
  0.0 12.5 %copy-start.10 = (s32[4]{0:T(128)S(1)}, s32[4]{0:T(128)}, u32[]{:S(2)}) copy-start(s32[4]{0:T(128)} %starts_ref.9) | copy-start | bytes 52
  1.6 10.9 %collective-permute-start.4 = (bf16[128,4736]{1,0:T(8,128)(2,1)S(1)}, bf16[128,4736]{1,0:T(8,128)(2,1)S(1)}, u32[]{:S(2)}, u32[]{:S(2)}) collective-permute-start(bf16[128,4736]{1,0:T(8,128)(2,1)S(1)} %get-tuple-element.24), channel_id=1, source_target_pairs={{0,1},{1,0},{2,3},{3,2},{4,5},{5,4},{6,7},{7,6},{8,9},{9,8},{10,11... | collective-permute-start | bytes 3637256 | tf_op jit(solution)/shard_map/ppermute | solution.py:420
  3.1 7.5 %collective-permute-start.2 = (f32[8,128]{1,0:T(8,128)S(1)}, f32[8,128]{1,0:T(8,128)S(1)}, u32[]{:S(2)}, u32[]{:S(2)}) collective-permute-start(f32[8,128]{1,0:T(8,128)S(1)} %get-tuple-element.22.own0), channel_id=1, source_target_pairs={{6,0},{0,2},{2,4},{4,6},{7,1},{1,3},{3,5},{5,7},{14,8},{8,10},{10,... | collective-permute-start | bytes 12296 | tf_op jit(solution)/shard_map/ppermute | solution.py:418
  4.8 5.8 %collective-permute-start.1 = (f32[8,128]{1,0:T(8,128)S(1)}, f32[8,128]{1,0:T(8,128)S(1)}, u32[]{:S(2)}, u32[]{:S(2)}) collective-permute-start(f32[8,128]{1,0:T(8,128)S(1)} %get-tuple-element.22.own0), channel_id=1, source_target_pairs={{4,0},{6,2},{0,4},{2,6},{5,1},{7,3},{1,5},{3,7},{12,8},{14,10},{8,... | collective-permute-start | bytes 12296 | tf_op jit(solution)/shard_map/ppermute | solution.py:418
  8.1 2.5 %collective-permute-start = (f32[8,128]{1,0:T(8,128)S(1)}, f32[8,128]{1,0:T(8,128)S(1)}, u32[]{:S(2)}, u32[]{:S(2)}) collective-permute-start(f32[8,128]{1,0:T(8,128)S(1)} %get-tuple-element.22.own0), channel_id=1, source_target_pairs={{2,0},{4,2},{6,4},{0,6},{3,1},{5,3},{7,5},{1,7},{10,8},{12,10},{14... | collective-permute-start | bytes 12296 | tf_op jit(solution)/shard_map/ppermute | solution.py:418
  10.6 5.6 %collective-permute-start.3 = (f32[32,128]{1,0:T(8,128)S(1)}, f32[32,128]{1,0:T(8,128)S(1)}, u32[]{:S(2)}, u32[]{:S(2)}) collective-permute-start(f32[32,128]{1,0:T(8,128)S(1)} %constant_dynamic-update-slice_fusion.refs_0_), channel_id=1, source_target_pairs={{0,1},{1,0},{2,3},{3,2},{4,5},{5,4},{6,7},{7,6},{8,9},{9,8},{10,11... | collective-permute-start | bytes 49160 | tf_op jit(solution)/shard_map/ppermute | solution.py:423
  16.2 0.8 %copy-start.8 = (f32[32,128]{1,0:T(8,128)}, f32[32,128]{1,0:T(8,128)S(1)}, u32[]{:S(2)}) copy-start(f32[32,128]{1,0:T(8,128)S(1)} %collective-permute-done.3.refs_1_) | copy-start | bytes 49156
  16.9 9.5 %copy-start.11 = (s32[4]{0:T(128)S(1)}, s32[4]{0:T(128)}, u32[]{:S(2)}) copy-start(s32[4]{0:T(128)} %starts_ref.9) | copy-start | bytes 52
  16.9 9.5 %copy-start.9 = (f32[32,128]{1,0:T(8,128)S(1)}, f32[32,128]{1,0:T(8,128)}, u32[]{:S(2)}) copy-start(f32[32,128]{1,0:T(8,128)} %copy-done.8) | copy-start | bytes 49156
  17.0 24.2 %all-to-all-start = ((bf16[64,8,1152]{2,1,0:T(8,128)(2,1)}), bf16[64,8,1152]{2,1,0:T(8,128)(2,1)S(1)}, u32[]{:S(2)}, u32[]{:S(2)}) async-start(bf16[64,8,1152]{2,1,0:T(8,128)(2,1)} %bitcast.10), calls=%async_computation | async-start | bytes 2359296 | tf_op jit(solution)/shard_map/all_to_all | solution.py:479
  41.2 20.1 %copy-start.5 = (f32[4,136,1024]{2,1,0:T(8,128)S(1)}, f32[4,136,1024]{2,1,0:T(8,128)}, u32[]{:S(2)}) copy-start(f32[4,136,1024]{2,1,0:T(8,128)} %get-tuple-element.34.middle_ref) | copy-start | bytes 6684676
  41.8 25.7 %copy-start.2 = (bf16[8,128,1024]{2,1,0:T(8,128)(2,1)S(1)}, bf16[8,128,1024]{2,1,0:T(8,128)(2,1)}, u32[]{:S(2)}) copy-start(bf16[8,128,1024]{2,1,0:T(8,128)(2,1)} %get-tuple-element.32.factor_ref) | copy-start | bytes 6291460
  61.2 6.3 %copy-start.1 = (bf16[8,128,1024]{2,1,0:T(8,128)(2,1)S(1)}, bf16[8,128,1024]{2,1,0:T(8,128)(2,1)}, u32[]{:S(2)}) copy-start(bf16[8,128,1024]{2,1,0:T(8,128)(2,1)} %get-tuple-element.31.base_ref) | copy-start | bytes 6291460
  61.2 6.3 %copy-start.3 = (bf16[128,1024]{1,0:T(8,128)(2,1)S(1)}, bf16[128,1024]{1,0:T(8,128)(2,1)}, u32[]{:S(2)}) copy-start(bf16[128,1024]{1,0:T(8,128)(2,1)} %c_ref.3) | copy-start | bytes 786436
  61.2 6.3 %copy-start.7 = (f32[8192]{0:T(1024)S(1)}, f32[8192]{0:T(1024)}, u32[]{:S(2)}) copy-start(f32[8192]{0:T(1024)} %param.18) | copy-start | bytes 98308
  61.7 8.1 %collective-permute-start.5 = (bf16[4,128,1024]{2,1,0:T(8,128)(2,1)S(1)}, bf16[4,128,1024]{2,1,0:T(8,128)(2,1)S(1)}, u32[]{:S(2)}, u32[]{:S(2)}) collective-permute-start(bf16[4,128,1024]{2,1,0:T(8,128)(2,1)S(1)} %get-tuple-element.35), channel_id=1, source_target_pairs={{0,1},{1,0},{2,3},{3,2},{4,5},{5,4},{6,7},{7,6},{8,9},{9,8},{10,11... | collective-permute-start | bytes 3145736 | tf_op jit(solution)/shard_map/ppermute | solution.py:509

commit v8 on v7

--- a/solution.py
+++ b/solution.py
@@ -24,7 +24,7 @@
 SLABS = STATE // SLAB
 LANES = 128
 PIECE = 4
-AHEAD = 5
+AHEAD = 6
 PARTS = 8
 EPS = 1e-5
 

time: 73.1 us -> 73.1 us (level)
  blocking collectives: 19.4 us -> 17.8 us
  starting transfers between devices: 24.4 us -> 25.8 us
    all_to_all x1, blocking collectives: 19.4 us -> 17.8 us  [local(): returned = lax.all_to_all(frozen, ('ctx', 'z'), 0, 0, tiled=True)]
    ppermute x1, starting transfers between devices: 5.79 us -> 7.27 us  [local(): states_got = [lax.ppermute(v, 'core', swap) for v in states_sent]]
where the time goes in v8:
time: 73.1 us; the launch traced here: 72.7 us
  starting transfers between devices  25.8 us (35%)
  Pallas kernels  19.1 us (26%)
  blocking collectives  17.8 us (24%)
  waiting for transfers between devices  9.62 us (13%)
    pallas_call x8, Pallas kernels, call(): pl.pallas_call(kernel, in_specs=[smem] * len(scalars) + (in_specs or [vme...  19.1 us
    all_to_all x1, blocking collectives, local(): returned = lax.all_to_all(frozen, ('ctx', 'z'), 0, 0, tiled=True)  17.8 us
    all_to_all x1, starting transfers between devices, local(): lax.all_to_all(pay.reshape(blocks, SLAB, WIDE + LANES), ('ctx', 'z'), 0,...  9.46 us
    ppermute x1, starting transfers between devices, local(): states_got = [lax.ppermute(v, 'core', swap) for v in states_sent]  7.27 us
    all_to_all x1, waiting for transfers between devices, local(): lax.all_to_all(pay.reshape(blocks, SLAB, WIDE + LANES), ('ctx', 'z'), 0,...  6.89 us
    ppermute x3, starting transfers between devices, local(): lax.ppermute(own, 'z', [((i + turn) % depth, i) for i in range(depth)])  5.79 us
    ppermute x1, starting transfers between devices, local(): got_rows = lax.ppermute(own_rows, 'core', swap)  1.86 us
    ppermute x3, waiting for transfers between devices, local(): lax.ppermute(own, 'z', [((i + turn) % depth, i) for i in range(depth)])  1.73 us
  transfers between devices with their start and end apart: 7, of which 3 were waited for; matrix products, arithmetic and copies ran while one was open for 0% of the time, Pallas kernels for 18%

profile of v8, /device:TPU:1, one launch (start us, length us, event | category | flops | bytes accessed | tf_op | source)
XLA Modules:
  0.0 72.7 jit_solution(14860629880776093521)
XLA Ops:
  0.0 0.0 copy-start.10
  0.0 1.5 %pack.1 = (bf16[128,4736]{1,0:T(8,128)(2,1)S(1)}, f32[8,128]{1,0:T(8,128)S(1)}, bf16[256,1024]{1,0:T(8,128)(2,1)S(1)}) custom-call(s32[1]{0:T(128)} %bitcast.place_ref, f32[1,16]{1,0:T(1,128)} %bitcast.11, f32[1,16]{1,0:T(1,128)} %bitcast.12, f32[1,16]{1,0:T(1,128)} %bitcast.13, bf16[128,128]{1,0:T(8,128)(2,1)} %refs_3_.3, bf16[128,8192]{1,0:T(8,128)(2,1)} %refs_2_.3, ...), custom_call_target="tpu_custom_call" | custom-call | tf_op jit(solution)/shard_map/pack/pallas_call | solution.py:375
  1.6 1.5 %collective-permute-start.4 = (bf16[128,4736]{1,0:T(8,128)(2,1)S(1)}, bf16[128,4736]{1,0:T(8,128)(2,1)S(1)}, u32[]{:S(2)}, u32[]{:S(2)}) collective-permute-start(bf16[128,4736]{1,0:T(8,128)(2,1)S(1)} %get-tuple-element.24), channel_id=1, source_target_pairs={{0,1},{1,0},{2,3},{3,2},{4,5},{5,4},{6,7},{7,6},{8,9},{9,8},{10,11... | collective-permute-start | bytes 3637256 | tf_op jit(solution)/shard_map/ppermute | solution.py:420
  3.1 1.8 %collective-permute-start.2 = (f32[8,128]{1,0:T(8,128)S(1)}, f32[8,128]{1,0:T(8,128)S(1)}, u32[]{:S(2)}, u32[]{:S(2)}) collective-permute-start(f32[8,128]{1,0:T(8,128)S(1)} %get-tuple-element.22.own0), channel_id=1, source_target_pairs={{6,0},{0,2},{2,4},{4,6},{7,1},{1,3},{3,5},{5,7},{14,8},{8,10},{10,... | collective-permute-start | bytes 12296 | tf_op jit(solution)/shard_map/ppermute | solution.py:418
  4.8 3.3 %collective-permute-start.1 = (f32[8,128]{1,0:T(8,128)S(1)}, f32[8,128]{1,0:T(8,128)S(1)}, u32[]{:S(2)}, u32[]{:S(2)}) collective-permute-start(f32[8,128]{1,0:T(8,128)S(1)} %get-tuple-element.22.own0), channel_id=1, source_target_pairs={{4,0},{6,2},{0,4},{2,6},{5,1},{7,3},{1,5},{3,7},{12,8},{14,10},{8,... | collective-permute-start | bytes 12296 | tf_op jit(solution)/shard_map/ppermute | solution.py:418
  8.1 0.7 %collective-permute-start = (f32[8,128]{1,0:T(8,128)S(1)}, f32[8,128]{1,0:T(8,128)S(1)}, u32[]{:S(2)}, u32[]{:S(2)}) collective-permute-start(f32[8,128]{1,0:T(8,128)S(1)} %get-tuple-element.22.own0), channel_id=1, source_target_pairs={{2,0},{4,2},{6,4},{0,6},{3,1},{5,3},{7,5},{1,7},{10,8},{12,10},{14... | collective-permute-start | bytes 12296 | tf_op jit(solution)/shard_map/ppermute | solution.py:418
  8.8 1.7 %collective-permute-done.own1 = f32[8,128]{1,0:T(8,128)S(1)} collective-permute-done((f32[8,128]{1,0:T(8,128)S(1)}, f32[8,128]{1,0:T(8,128)S(1)}, u32[]{:S(2)}, u32[]{:S(2)}) %collective-permute-start) | collective-permute-done | bytes 4128 | tf_op jit(solution)/shard_map/ppermute | solution.py:418
  10.6 0.0 collective-permute-done.1.own2
  10.6 0.0 collective-permute-done.2.own3
  10.6 1.9 %collective-permute-start.3 = (f32[32,128]{1,0:T(8,128)S(1)}, f32[32,128]{1,0:T(8,128)S(1)}, u32[]{:S(2)}, u32[]{:S(2)}) collective-permute-start(f32[32,128]{1,0:T(8,128)S(1)} %constant_dynamic-update-slice_fusion.refs_0_), channel_id=1, source_target_pairs={{0,1},{1,0},{2,3},{3,2},{4,5},{5,4},{6,7},{7,6},{8,9},{9,8},{10,11... | collective-permute-start | bytes 49160 | tf_op jit(solution)/shard_map/ppermute | solution.py:423
  12.5 0.0 collective-permute-done.4.got_ref
  12.5 3.7 %write.1 = (bf16[16,4,8,1152]{3,2,1,0:T(8,128)(2,1)}, f32[4,136,1024]{2,1,0:T(8,128)}) custom-call(s32[1]{0:T(128)} %bitcast.place_ref, s32[4]{0:T(128)S(1)} %copy-done.10, f32[8,128]{1,0:T(8,128)S(1)} %get-tuple-element.22.own0, f32[8,128]{1,0:T(8,128)S(1)} %collective-permute-done.own1, f32[8,128]{1,0:T(8,128)S(1)} %collective-permute-done.1.own2, ...), custom_call_target="tpu_custom_call" | custom-call | tf_op jit(solution)/shard_map/write/pallas_call | solution.py:375
  16.2 0.7 %ahead.1 = (bf16[16,4,8,1152]{3,2,1,0:T(8,128)(2,1)}, bf16[8,128,1024]{2,1,0:T(8,128)(2,1)}, bf16[8,128,1024]{2,1,0:T(8,128)(2,1)}) custom-call(s32[1]{0:T(128)} %bitcast.place_ref, s32[4]{0:T(128)S(1)} %copy-done.10, f32[32,128]{1,0:T(8,128)S(1)} %constant_dynamic-update-slice_fusion.refs_0_, ...), custom_call_target="tpu_custom_call", output_to_operand_aliasing={{0}: (9, {})} | custom-call | flops 1073741824 | bytes 9437184 | tf_op jit(solution)/shard_map/ahead/pallas_call | solution.py:375
  16.9 0.0 copy-start.11
  17.0 9.5 %all-to-all-start = ((bf16[64,8,1152]{2,1,0:T(8,128)(2,1)}), bf16[64,8,1152]{2,1,0:T(8,128)(2,1)S(1)}, u32[]{:S(2)}, u32[]{:S(2)}) async-start(bf16[64,8,1152]{2,1,0:T(8,128)(2,1)} %bitcast.10), calls=%async_computation | async-start | bytes 2359296 | tf_op jit(solution)/shard_map/all_to_all | solution.py:479
  26.4 7.9 %inside.1 = (bf16[8,128,1024]{2,1,0:T(8,128)(2,1)}, bf16[8,128,1024]{2,1,0:T(8,128)(2,1)}) custom-call(s32[1]{0:T(128)} %bitcast.place_ref, s32[4]{0:T(128)S(1)} %copy-done.11, f32[32,128]{1,0:T(8,128)S(1)} %constant_dynamic-update-slice_fusion.refs_0_, f32[32,128]{1,0:T(8,128)S(1)} %copy-done.9, ...), custom_call_target="tpu_custom_call", output_to_operand_aliasing={{0}: (9, {}), {1}: (10, {})} | custom-call | flops 1073741824 | bytes 9437184 | tf_op jit(solution)/shard_map/inside/pallas_call | solution.py:375
  34.4 6.9 %all-to-all-done.pay_ref = bf16[64,8,1152]{2,1,0:T(8,128)(2,1)S(1)} async-done(((bf16[64,8,1152]{2,1,0:T(8,128)(2,1)}), bf16[64,8,1152]{2,1,0:T(8,128)(2,1)S(1)}, u32[]{:S(2)}, u32[]{:S(2)}) %all-to-all-start) | async-done | bytes 1179680 | tf_op jit(solution)/shard_map/all_to_all | solution.py:479
  41.3 0.7 scan.1
  42.0 17.8 %all_to_all.10 = bf16[64,8,1024]{2,1,0:T(8,128)(2,1)S(1)} all-to-all(bf16[64,8,1024]{2,1,0:T(8,128)(2,1)S(1)} %scan.1), channel_id=1, replica_groups=mesh['ctx'=16,'z'=4,'core'=2] {'ctx','z'}, dimensions={0} | all-to-all | bytes 2097152 | tf_op jit(solution)/shard_map/all_to_all | solution.py:494
  59.8 0.5 states.1
  60.3 7.3 %collective-permute-start.5 = (bf16[4,128,1024]{2,1,0:T(8,128)(2,1)S(1)}, bf16[4,128,1024]{2,1,0:T(8,128)(2,1)S(1)}, u32[]{:S(2)}, u32[]{:S(2)}) collective-permute-start(bf16[4,128,1024]{2,1,0:T(8,128)(2,1)S(1)} %get-tuple-element.35), channel_id=1, source_target_pairs={{0,1},{1,0},{2,3},{3,2},{4,5},{5,4},{6,7},{7,6},{8,9},{9,8},{10,11... | collective-permute-start | bytes 3145736 | tf_op jit(solution)/shard_map/ppermute | solution.py:509
  67.6 1.3 %own.1 = (f32[4,128,1024]{2,1,0:T(8,128)S(1)}, f32[128,128]{1,0:T(8,128)S(1)}) custom-call(s32[1]{0:T(128)} %bitcast.place_ref, s32[4]{0:T(128)S(1)} %copy-done.11, bf16[8,128,1024]{2,1,0:T(8,128)(2,1)S(1)} %copy-done.1, bf16[8,128,1024]{2,1,0:T(8,128)(2,1)S(1)} %copy-done.2, bf16[128,1024]{1,0:T(8,128)(2,1)S(1)} %copy-done.3, f32[1,8192]{1,0:T(1,128)S(1)} %bitcast.8, ...), custom_call_target="tpu_custom_call" | custom-call | flops 268435456 | bytes 5242880 | tf_op jit(solution)/shard_map/own/pallas_call | solution.py:375
  68.8 1.0 %collective-permute-done.5.refs_0_ = bf16[4,128,1024]{2,1,0:T(8,128)(2,1)S(1)} collective-permute-done((bf16[4,128,1024]{2,1,0:T(8,128)(2,1)S(1)}, bf16[4,128,1024]{2,1,0:T(8,128)(2,1)S(1)}, u32[]{:S(2)}, u32[]{:S(2)}) %collective-permute-start.5) | collective-permute-done | bytes 1048608 | tf_op jit(solution)/shard_map/ppermute | solution.py:509
  69.8 2.8 %last.1 = bf16[128,8192]{1,0:T(8,128)(2,1)} custom-call(s32[1]{0:T(128)} %bitcast.place_ref, s32[4]{0:T(128)S(1)} %copy-done.11, bf16[8,128,1024]{2,1,0:T(8,128)(2,1)S(1)} %copy-done.1, bf16[8,128,1024]{2,1,0:T(8,128)(2,1)S(1)} %copy-done.2, bf16[128,1024]{1,0:T(8,128)(2,1)S(1)} %copy-done.3, bf16[4,128,1024]{2,1,0:T(8,128)(2,1)S(1)} %collective-permute-done.5.refs_0_, ...), custom_call_target="tpu_custom_call" | custom-call | tf_op jit(solution)/shard_map/last/pallas_call | solution.py:375
  (27 shorter events, 0.1 us)
Async XLA Ops:
  0.0 12.5 %copy-start.6 = (bf16[128,128]{1,0:T(8,128)(2,1)S(1)}, bf16[128,128]{1,0:T(8,128)(2,1)}, u32[]{:S(2)}) copy-start(bf16[128,128]{1,0:T(8,128)(2,1)} %refs_3_.3) | copy-start | bytes 98308
  0.0 12.5 %copy-start.4 = (bf16[128,1024]{1,0:T(8,128)(2,1)S(1)}, bf16[128,1024]{1,0:T(8,128)(2,1)}, u32[]{:S(2)}) copy-start(bf16[128,1024]{1,0:T(8,128)(2,1)} %refs_4_.3) | copy-start | bytes 786436
  0.0 12.5 %copy-start = (bf16[128,8192]{1,0:T(8,128)(2,1)S(1)}, bf16[128,8192]{1,0:T(8,128)(2,1)}, u32[]{:S(2)}) copy-start(bf16[128,8192]{1,0:T(8,128)(2,1)} %refs_2_.3) | copy-start | bytes 6291460
  0.0 12.5 %copy-start.10 = (s32[4]{0:T(128)S(1)}, s32[4]{0:T(128)}, u32[]{:S(2)}) copy-start(s32[4]{0:T(128)} %starts_ref.9) | copy-start | bytes 52
  1.6 10.9 %collective-permute-start.4 = (bf16[128,4736]{1,0:T(8,128)(2,1)S(1)}, bf16[128,4736]{1,0:T(8,128)(2,1)S(1)}, u32[]{:S(2)}, u32[]{:S(2)}) collective-permute-start(bf16[128,4736]{1,0:T(8,128)(2,1)S(1)} %get-tuple-element.24), channel_id=1, source_target_pairs={{0,1},{1,0},{2,3},{3,2},{4,5},{5,4},{6,7},{7,6},{8,9},{9,8},{10,11... | collective-permute-start | bytes 3637256 | tf_op jit(solution)/shard_map/ppermute | solution.py:420
  3.1 7.5 %collective-permute-start.2 = (f32[8,128]{1,0:T(8,128)S(1)}, f32[8,128]{1,0:T(8,128)S(1)}, u32[]{:S(2)}, u32[]{:S(2)}) collective-permute-start(f32[8,128]{1,0:T(8,128)S(1)} %get-tuple-element.22.own0), channel_id=1, source_target_pairs={{6,0},{0,2},{2,4},{4,6},{7,1},{1,3},{3,5},{5,7},{14,8},{8,10},{10,... | collective-permute-start | bytes 12296 | tf_op jit(solution)/shard_map/ppermute | solution.py:418
  4.8 5.8 %collective-permute-start.1 = (f32[8,128]{1,0:T(8,128)S(1)}, f32[8,128]{1,0:T(8,128)S(1)}, u32[]{:S(2)}, u32[]{:S(2)}) collective-permute-start(f32[8,128]{1,0:T(8,128)S(1)} %get-tuple-element.22.own0), channel_id=1, source_target_pairs={{4,0},{6,2},{0,4},{2,6},{5,1},{7,3},{1,5},{3,7},{12,8},{14,10},{8,... | collective-permute-start | bytes 12296 | tf_op jit(solution)/shard_map/ppermute | solution.py:418
  8.1 2.5 %collective-permute-start = (f32[8,128]{1,0:T(8,128)S(1)}, f32[8,128]{1,0:T(8,128)S(1)}, u32[]{:S(2)}, u32[]{:S(2)}) collective-permute-start(f32[8,128]{1,0:T(8,128)S(1)} %get-tuple-element.22.own0), channel_id=1, source_target_pairs={{2,0},{4,2},{6,4},{0,6},{3,1},{5,3},{7,5},{1,7},{10,8},{12,10},{14... | collective-permute-start | bytes 12296 | tf_op jit(solution)/shard_map/ppermute | solution.py:418
  10.6 5.6 %collective-permute-start.3 = (f32[32,128]{1,0:T(8,128)S(1)}, f32[32,128]{1,0:T(8,128)S(1)}, u32[]{:S(2)}, u32[]{:S(2)}) collective-permute-start(f32[32,128]{1,0:T(8,128)S(1)} %constant_dynamic-update-slice_fusion.refs_0_), channel_id=1, source_target_pairs={{0,1},{1,0},{2,3},{3,2},{4,5},{5,4},{6,7},{7,6},{8,9},{9,8},{10,11... | collective-permute-start | bytes 49160 | tf_op jit(solution)/shard_map/ppermute | solution.py:423
  16.2 0.8 %copy-start.8 = (f32[32,128]{1,0:T(8,128)}, f32[32,128]{1,0:T(8,128)S(1)}, u32[]{:S(2)}) copy-start(f32[32,128]{1,0:T(8,128)S(1)} %collective-permute-done.3.refs_1_) | copy-start | bytes 49156
  16.9 9.5 %copy-start.11 = (s32[4]{0:T(128)S(1)}, s32[4]{0:T(128)}, u32[]{:S(2)}) copy-start(s32[4]{0:T(128)} %starts_ref.9) | copy-start | bytes 52
  16.9 9.5 %copy-start.9 = (f32[32,128]{1,0:T(8,128)S(1)}, f32[32,128]{1,0:T(8,128)}, u32[]{:S(2)}) copy-start(f32[32,128]{1,0:T(8,128)} %copy-done.8) | copy-start | bytes 49156
  17.0 24.3 %all-to-all-start = ((bf16[64,8,1152]{2,1,0:T(8,128)(2,1)}), bf16[64,8,1152]{2,1,0:T(8,128)(2,1)S(1)}, u32[]{:S(2)}, u32[]{:S(2)}) async-start(bf16[64,8,1152]{2,1,0:T(8,128)(2,1)} %bitcast.10), calls=%async_computation | async-start | bytes 2359296 | tf_op jit(solution)/shard_map/all_to_all | solution.py:479
  41.3 18.5 %copy-start.5 = (f32[4,136,1024]{2,1,0:T(8,128)S(1)}, f32[4,136,1024]{2,1,0:T(8,128)}, u32[]{:S(2)}) copy-start(f32[4,136,1024]{2,1,0:T(8,128)} %get-tuple-element.34.middle_ref) | copy-start | bytes 6684676
  42.0 25.6 %copy-start.2 = (bf16[8,128,1024]{2,1,0:T(8,128)(2,1)S(1)}, bf16[8,128,1024]{2,1,0:T(8,128)(2,1)}, u32[]{:S(2)}) copy-start(bf16[8,128,1024]{2,1,0:T(8,128)(2,1)} %get-tuple-element.32.factor_ref) | copy-start | bytes 6291460
  59.8 7.8 %copy-start.1 = (bf16[8,128,1024]{2,1,0:T(8,128)(2,1)S(1)}, bf16[8,128,1024]{2,1,0:T(8,128)(2,1)}, u32[]{:S(2)}) copy-start(bf16[8,128,1024]{2,1,0:T(8,128)(2,1)} %get-tuple-element.31.base_ref) | copy-start | bytes 6291460
  59.8 7.8 %copy-start.3 = (bf16[128,1024]{1,0:T(8,128)(2,1)S(1)}, bf16[128,1024]{1,0:T(8,128)(2,1)}, u32[]{:S(2)}) copy-start(bf16[128,1024]{1,0:T(8,128)(2,1)} %c_ref.3) | copy-start | bytes 786436
  59.8 7.8 %copy-start.7 = (f32[8192]{0:T(1024)S(1)}, f32[8192]{0:T(1024)}, u32[]{:S(2)}) copy-start(f32[8192]{0:T(1024)} %param.18) | copy-start | bytes 98308
  60.3 9.6 %collective-permute-start.5 = (bf16[4,128,1024]{2,1,0:T(8,128)(2,1)S(1)}, bf16[4,128,1024]{2,1,0:T(8,128)(2,1)S(1)}, u32[]{:S(2)}, u32[]{:S(2)}) collective-permute-start(bf16[4,128,1024]{2,1,0:T(8,128)(2,1)S(1)} %get-tuple-element.35), channel_id=1, source_target_pairs={{0,1},{1,0},{2,3},{3,2},{4,5},{5,4},{6,7},{7,6},{8,9},{9,8},{10,11... | collective-permute-start | bytes 3145736 | tf_op jit(solution)/shard_map/ppermute | solution.py:509
